TPU v7x, 32 devices: a whole 2x2x4 slice. The times are simulated.
32 devices in a mesh: segment: 4 (over x, core), grp: 4 (over z), sp: 2 (over y).
Axes of the slice: x: 2, y: 2, z: 4, core: 2. Of those that a mesh axis runs over, the one named last changes fastest.
Arguments:
- queries: bfloat16 [4, 4, 4, 8, 16, 2048], P('segment', 'grp', None, 'sp'), may hold values from -140 to 140
- key_states: bfloat16 [4, 4, 4, 8, 16, 2048], P('segment', 'grp', None, 'sp'), may hold values from -6 to 6
- value_states: bfloat16 [4, 4, 4, 8, 16, 2048], P('segment', 'grp', None, 'sp'), may hold values from -6 to 6
- kept_tiles: int32 [16, 2, 2], replicated, may hold values from 0 to 1, as said below
- kept_counts: int32 [16, 2], replicated, may hold values from 1 to 2
- patch_weight: bfloat16 [2048, 64], replicated, may hold values from -1.5 to 1.5
- decode_slot: int32 [4], replicated, may hold values from 0 to 3, each once
- first_kernel: bfloat16 [27, 16, 256], replicated, may hold values from -0.3125 to 0.3125
- second_kernel: bfloat16 [27, 256, 256], P(None, 'grp'), may hold values from -0.078125 to 0.078125
Outputs:
- decoded: bfloat16 [4, 4, 4, 16, 32, 256], P('segment', 'grp', None, 'sp')
Inputs may be any that keep to these rules, and one draw needn't show every extreme that they name: `kept_tiles`: for each head and query tile the 2 entries name distinct tiles, the query tile itself among them in some slot.
All inputs are finite; a program needn't handle non-finite values.
Results may differ from a plain program's by a relative error of at most 0.018.
Values may be sent and summed in bfloat16 or wider, within the bound.
No kernel may reach another device: no remote copies, remote signals or barrier semaphores. Data moves between devices by JAX's collectives and lax.ppermute only.
A program may use at most 128 MiB of HBM per device.

v0:
```python
import jax
import jax.numpy as jnp
from jax import lax
from jax.sharding import PartitionSpec as P

HEADS = 16
HD = 128
LAT = 16
CH = 256
TT = 4
TH = 8
TW = 8


VAE_SCALE = 1.0 / 0.476986


def padded_2(cells, sides, width):
    for axis, dim in sides:
        count = lax.axis_size(axis)
        ends = count - 1
        head = lax.slice_in_dim(cells, 0, width, axis=dim)
        tail = lax.slice_in_dim(cells, cells.shape[dim] - width, cells.shape[dim], axis=dim)
        cells = jnp.concatenate(
            [
                lax.ppermute(tail, axis, [(i, (i + 1) % count) for i in range(ends)]),
                cells,
                lax.ppermute(head, axis, [((i + 1) % count, i) for i in range(ends)]),
            ],
            axis=dim,
        )
    return cells


def to_tiles(grid, tile_size):
    frame_count, row_count, col_count, feature_width = grid.shape
    tiled = grid.reshape(
        frame_count // TT, TT, row_count // TH, TH, col_count // TW, TW, feature_width
    ).transpose(0, 2, 4, 1, 3, 5, 6)
    return tiled.reshape(-1, tile_size, feature_width)


def from_tiles(tiles, frame_count, row_count, col_count):
    feature_width = tiles.shape[-1]
    grid = tiles.reshape(
        frame_count // TT, row_count // TH, col_count // TW, TT, TH, TW, feature_width
    ).transpose(0, 3, 1, 4, 2, 5, 6)
    return grid.reshape(frame_count, row_count, col_count, feature_width)


def attend_tiles(query_tiles, key_tiles, value_tiles, tile_index, live_count):
    head_count = query_tiles.shape[0]
    tile_size = query_tiles.shape[2]
    head_size = query_tiles.shape[3]
    keep_count = tile_index.shape[2]

    def one_tile(packed):
        query_block, index_block, count_block = packed
        key_sel = jax.vmap(lambda source, picks: source[picks])(key_tiles, index_block).reshape(
            head_count, keep_count * tile_size, head_size
        )
        value_sel = jax.vmap(lambda source, picks: source[picks])(value_tiles, index_block).reshape(
            head_count, keep_count * tile_size, head_size
        )
        scores = jnp.einsum(
            "hqd,hkd->hqk", query_block, key_sel, preferred_element_type=jnp.float32
        ) * head_size ** (-0.5)
        live = jnp.arange(keep_count, dtype=jnp.int32)[None, :] < count_block[:, None]
        live = jnp.repeat(live, tile_size, axis=1)[:, None, :]
        scores = jnp.where(live, scores, -1e30)
        row_top = jnp.max(scores, axis=-1, keepdims=True)
        exponent = jnp.where(live, jnp.exp(scores - row_top), 0.0)
        weights = (exponent / jnp.sum(exponent, axis=-1, keepdims=True)).astype(jnp.bfloat16)
        result = jnp.einsum("hqk,hkd->hqd", weights, value_sel, preferred_element_type=jnp.float32)
        return result.astype(jnp.bfloat16)

    return lax.map(
        one_tile,
        (
            query_tiles.transpose(1, 0, 2, 3),
            tile_index.transpose(1, 0, 2),
            live_count.transpose(1, 0),
        ),
    )


def edge_fill(padded, axis_dim, depth, at_first, at_last):
    extent = padded.shape[axis_dim]
    inner_first = lax.slice_in_dim(padded, depth, depth + 1, axis=axis_dim)
    inner_last = lax.slice_in_dim(padded, extent - depth - 1, extent - depth, axis=axis_dim)
    position = lax.broadcasted_iota(jnp.int32, padded.shape, axis_dim)
    padded = jnp.where(jnp.logical_and(at_first, position < depth), inner_first, padded)
    padded = jnp.where(jnp.logical_and(at_last, position >= extent - depth), inner_last, padded)
    return padded


def pad_columns(block, depth):
    return jnp.pad(block, ((0, 0), (0, 0), (0, 0), (depth, depth), (0, 0)))


def causal_pad(block):
    first_frame = block[:, :1]
    return jnp.concatenate([first_frame, first_frame, block], axis=1)


def window_columns(padded, row_count, col_count):
    frame_count = padded.shape[1] - 2
    pieces = []
    for offset_time in range(3):
        for offset_row in range(3):
            for offset_col in range(3):
                pieces.append(
                    padded[
                        :,
                        offset_time : offset_time + frame_count,
                        offset_row : offset_row + row_count,
                        offset_col : offset_col + col_count,
                    ]
                )
    stacked = jnp.stack(pieces, axis=-2)
    return stacked.reshape(-1, 27, padded.shape[-1])


def first_conv(rimmed, kernel, row_count, col_count):
    columns = window_columns(causal_pad(rimmed), row_count, col_count).reshape(
        -1, kernel.shape[0] * kernel.shape[1]
    )
    flat_kernel = kernel.reshape(-1, kernel.shape[2])
    result = jnp.dot(columns, flat_kernel, preferred_element_type=jnp.float32) * VAE_SCALE
    return result.astype(jnp.bfloat16).reshape(
        rimmed.shape[0], rimmed.shape[1] - 0, row_count, col_count, kernel.shape[2]
    )


def local(
    queries,
    key_states,
    value_states,
    kept_tiles,
    kept_counts,
    patch_weight,
    decode_slot,
    first_kernel,
    second_kernel,
):
    frame_count = queries.shape[2]
    local_rows = queries.shape[3]
    token_cols = queries.shape[4]
    feature_count = queries.shape[5]
    tokens = frame_count * local_rows * token_cols
    sp_count = lax.axis_size("sp")
    sp_rank = lax.axis_index("sp")
    local_heads = HEADS // sp_count
    clip_rows = local_rows * sp_count
    tile_size = TT * TH * TW
    flat_query = queries.reshape(tokens, feature_count)
    flat_key = key_states.reshape(tokens, feature_count)
    flat_value = value_states.reshape(tokens, feature_count)
    mixed_query, mixed_key, mixed_value = (
        lax.all_to_all(flat_query, "sp", split_axis=1, concat_axis=0, tiled=True),
        lax.all_to_all(flat_key, "sp", split_axis=1, concat_axis=0, tiled=True),
        lax.all_to_all(flat_value, "sp", split_axis=1, concat_axis=0, tiled=True),
    )
    own_width = mixed_query.shape[1]

    def head_tiles(mixed):
        grid = mixed.reshape(sp_count, frame_count, local_rows, token_cols, own_width).transpose(
            1, 0, 2, 3, 4
        )
        tiles = to_tiles(grid.reshape(frame_count, clip_rows, token_cols, own_width), tile_size)
        return tiles.reshape(tiles.shape[0], tile_size, local_heads, HD).transpose(2, 0, 1, 3)

    own_tiles = lax.dynamic_slice_in_dim(kept_tiles, sp_rank * local_heads, local_heads, 0)
    own_counts = lax.dynamic_slice_in_dim(kept_counts, sp_rank * local_heads, local_heads, 0)
    outputs = attend_tiles(
        head_tiles(mixed_query),
        head_tiles(mixed_key),
        head_tiles(mixed_value),
        own_tiles,
        own_counts,
    )
    tile_count = outputs.shape[0]
    attended = from_tiles(
        outputs.transpose(0, 2, 1, 3).reshape(tile_count, tile_size, own_width),
        frame_count,
        clip_rows,
        token_cols,
    )
    attended = attended.reshape(frame_count, sp_count, local_rows, token_cols, own_width).transpose(
        1, 0, 2, 3, 4
    )
    attended = attended.reshape(sp_count * tokens, own_width)
    restored = lax.all_to_all(attended, "sp", split_axis=0, concat_axis=1, tiled=True)
    latent = jnp.dot(restored, patch_weight, preferred_element_type=jnp.float32)
    latent = latent.astype(jnp.bfloat16)
    segment_count = lax.axis_size("segment")
    segment_rank = lax.axis_index("segment")
    every_segment = lax.all_gather(latent[None], "segment", axis=0, tiled=True)
    picks = (decode_slot == segment_rank).astype(jnp.int32)
    source = jnp.sum(jnp.arange(segment_count, dtype=jnp.int32) * picks)
    chosen = lax.dynamic_index_in_dim(every_segment, source, 0, keepdims=False)
    cells = chosen.reshape(frame_count, local_rows, token_cols, 2, 2, LAT).transpose(
        0, 1, 3, 2, 4, 5
    )
    cells = cells.reshape(1, frame_count, 2 * local_rows, 2 * token_cols, LAT)
    row_count = 2 * local_rows
    col_count = 2 * token_cols
    sp_first = sp_rank == 0
    sp_last = sp_rank == sp_count - 1

    def boundary(block, depth):
        block = edge_fill(block, 2, depth, sp_first, sp_last)
        return edge_fill(block, 3, depth, True, True)

    rimmed = padded_2(cells, (("sp", 2),), 1)
    first = first_conv(boundary(pad_columns(rimmed, 1), 1), first_kernel, row_count, col_count)
    act = jax.nn.silu(first.astype(jnp.float32)).astype(jnp.bfloat16)
    act_rim = padded_2(act, (("sp", 2),), 1)
    act_rim = boundary(pad_columns(act_rim, 1), 1)
    columns = window_columns(causal_pad(act_rim), row_count, col_count)
    cell_count = columns.shape[0]
    second = lax.dot_general(
        columns,
        lax.all_gather(second_kernel, "grp", axis=1, tiled=True),
        (((1, 2), (0, 1)), ((), ())),
        preferred_element_type=jnp.float32,
    )
    summed = first.astype(jnp.float32).reshape(cell_count, CH) + second
    return summed.astype(jnp.bfloat16).reshape(1, 1, frame_count, row_count, col_count, CH)


def solution(mesh):
    return jax.shard_map(
        local,
        mesh=mesh,
        in_specs=(
            P("segment", "grp", None, "sp", None, None),
            P("segment", "grp", None, "sp", None, None),
            P("segment", "grp", None, "sp", None, None),
            P(),
            P(),
            P(),
            P(),
            P(),
            P(None, "grp", None),
        ),
        out_specs=P("segment", "grp", None, "sp", None, None),
        check_vma=False,
    )
```

profile of v0, /device:TPU:0, one launch (start us, length us, event | category | flops | bytes accessed | tf_op | source)
XLA Modules:
  0.0 243.3 jit_solution(12205546361475716972)
XLA Ops:
  6.5 1.9 all_to_all.50
  8.4 1.2 copy.291
  9.7 4.2 %all-to-all-start = ((bf16[256,2,1024]{2,0,1:T(8,128)(2,1)}), bf16[256,2,1024]{2,0,1:T(8,128)(2,1)S(1)}, u32[]{:S(2)}, u32[]{:S(2)}) async-start(bf16[256,2,1024]{2,0,1:T(8,128)(2,1)} %copy.291), calls=%async_computation | async-start | bytes 2097152 | tf_op jit(solution)/shard_map/all_to_all | solution.py:160
  13.9 1.8 all_to_all.53
  15.7 1.3 copy.294
  17.0 11.3 %all-to-all-done = bf16[256,2,1024]{2,0,1:T(8,128)(2,1)S(1)} async-done(((bf16[256,2,1024]{2,0,1:T(8,128)(2,1)}), bf16[256,2,1024]{2,0,1:T(8,128)(2,1)S(1)}, u32[]{:S(2)}, u32[]{:S(2)}) %all-to-all-start) | async-done | bytes 1048608 | tf_op jit(solution)/shard_map/all_to_all | solution.py:160
  28.3 3.6 %all-to-all-start.1 = ((bf16[256,2,1024]{2,0,1:T(8,128)(2,1)}), bf16[256,2,1024]{2,0,1:T(8,128)(2,1)S(1)}, u32[]{:S(2)}, u32[]{:S(2)}) async-start(bf16[256,2,1024]{2,0,1:T(8,128)(2,1)} %copy.294), calls=%async_computation.1 | async-start | bytes 2097152 | tf_op jit(solution)/shard_map/all_to_all | solution.py:161
  31.9 1.8 all_to_all.56
  33.8 1.3 copy.297
  35.7 9.5 %all-to-all-done.1 = bf16[256,2,1024]{2,0,1:T(8,128)(2,1)S(1)} async-done(((bf16[256,2,1024]{2,0,1:T(8,128)(2,1)}), bf16[256,2,1024]{2,0,1:T(8,128)(2,1)S(1)}, u32[]{:S(2)}, u32[]{:S(2)}) %all-to-all-start.1) | async-done | bytes 1048608 | tf_op jit(solution)/shard_map/all_to_all | solution.py:161
  45.2 3.6 %all-to-all-start.2 = ((bf16[256,2,1024]{2,0,1:T(8,128)(2,1)}), bf16[256,2,1024]{2,0,1:T(8,128)(2,1)S(1)}, u32[]{:S(2)}, u32[]{:S(2)}) async-start(bf16[256,2,1024]{2,0,1:T(8,128)(2,1)} %copy.297), calls=%async_computation.2 | async-start | bytes 2097152 | tf_op jit(solution)/shard_map/all_to_all | solution.py:162
  49.6 1.1 bitcast_bitcast_fusion.2
  50.7 10.5 %all-to-all-done.2 = bf16[256,2,1024]{2,0,1:T(8,128)(2,1)S(1)} async-done(((bf16[256,2,1024]{2,0,1:T(8,128)(2,1)}), bf16[256,2,1024]{2,0,1:T(8,128)(2,1)S(1)}, u32[]{:S(2)}, u32[]{:S(2)}) %all-to-all-start.2) | async-done | bytes 1048608 | tf_op jit(solution)/shard_map/all_to_all | solution.py:162
  62.0 17.4 %while.10 = (s32[]{:T(128)}, bf16[2,8,256,128]{3,2,1,0:T(8,128)(2,1)}, s32[2,8]{1,0:T(2,128)S(1)}, bf16[2,8,256,128]{3,1,2,0:T(8,128)(2,1)}, s32[2,8,2]{1,2,0:T(...) while((s32[]{:T(128)}, ...), condition=%wide.region_3.4_spmd, body=%wide.region_0.3_spmd.sunk | while | flops 546570880 | bytes 37774272 | solution.py:77
  62.2 1.7 gather_fusion
  64.6 1.1 constant_dynamic-slice_fusion.4
  66.5 2.2 fusion.112
  68.7 1.0 fusion.113
  69.7 0.9 copy-done.3
  70.9 1.7 gather_fusion
  73.3 1.1 constant_dynamic-slice_fusion.4
  75.2 2.2 fusion.112
  77.4 1.0 fusion.113
  78.5 0.9 copy-done.3
  79.4 1.9 copy.303
  81.9 1.1 copy.305
  83.0 3.6 %all-to-all-start.3 = ((bf16[2,256,1024]{2,1,0:T(8,128)(2,1)}), bf16[2,256,1024]{2,1,0:T(8,128)(2,1)S(1)}, u32[]{:S(2)}, u32[]{:S(2)}) async-start(bf16[2,256,1024]{2,1,0:T(8,128)(2,1)} %bitcast.31), calls=%async_computation.3 | async-start | bytes 2097152 | tf_op jit(solution)/shard_map/all_to_all | solution.py:193
  89.3 8.8 %all-to-all-done.3 = bf16[2,256,1024]{2,1,0:T(8,128)(2,1)S(1)} async-done(((bf16[2,256,1024]{2,1,0:T(8,128)(2,1)}), bf16[2,256,1024]{2,1,0:T(8,128)(2,1)S(1)}, u32[]{:S(2)}, u32[]{:S(2)}) %all-to-all-start.3) | async-done | bytes 1048608 | tf_op jit(solution)/shard_map/all_to_all | solution.py:193
  98.9 5.4 %all-gather = bf16[1024,64]{0,1:T(8,128)(2,1)S(1)} all-gather(bf16[256,64]{0,1:T(8,128)(2,1)S(1)} %convolution_convert_fusion), channel_id=2, replica_groups=mesh['segment'=4,'grp'=4,'sp'=2] {'segment'}, dimensions={0}, use_global_device_ids=true | all-gather | bytes 163840 | tf_op jit(solution)/shard_map/all_gather | solution.py:198
  105.0 1.3 collective-permute-start.1
  106.3 4.7 %collective-permute-start = (bf16[1,4,1,32,16]{4,3,2,1,0:T(8,128)(2,1)S(1)}, bf16[1,4,1,32,16]{4,3,2,1,0:T(8,128)(2,1)S(1)}, u32[]{:S(2)}, u32[]{:S(2)}) collective-permute-start(bf16[1,4,1,32,16]{4,3,2,1,0:T(8,128)(2,1)S(1)} %get-tuple-element.138), channel_id=1, source_target_pairs={{0,1},{2,3},{4,5},{6,7},{8,9},{10,11},{12,13},{14,15},{16,17},{18,... | collective-permute-start | bytes 12296 | tf_op jit(solution)/shard_map/ppermute | solution.py:26
  111.1 1.4 collective-permute-done
  134.6 9.3 %copy.313 = bf16[1,4,8,32,27,16]{3,2,1,5,4,0:T(8,128)(2,1)} copy(bf16[1,4,8,32,27,16]{5,3,2,1,4,0:T(8,128)(2,1)} %fusion.64) | data formatting | bytes 1769472 | tf_op jit(solution)/shard_map/stack | solution.py:120
  143.9 5.3 %reshape_reshape.35 = bf16[1024,432]{0,1:T(8,128)(2,1)S(1)} reshape(bf16[1,4,8,32,27,16]{3,2,1,5,4,0:T(8,128)(2,1)} %copy.313) | data formatting | bytes 1769472 | tf_op jit(solution)/shard_map/reshape;reshape | solution.py:125
  150.1 1.3 collective-permute-start.3
  151.4 4.8 %collective-permute-start.2 = (bf16[1,4,1,32,256]{4,3,2,1,0:T(8,128)(2,1)S(1)}, bf16[1,4,1,32,256]{4,3,2,1,0:T(8,128)(2,1)S(1)}, u32[]{:S(2)}, u32[]{:S(2)}) collective-permute-start(bf16[1,4,1,32,256]{4,3,2,1,0:T(8,128)(2,1)S(1)} %get-tuple-element.132), channel_id=1, source_target_pairs={{0,1},{2,3},{4,5},{6,7},{8,9},{10,11},{12,13},{14,15},{16,17},{18,... | collective-permute-start | bytes 196616 | tf_op jit(solution)/shard_map/ppermute | solution.py:26
  156.2 1.6 collective-permute-done.2
  159.1 0.9 select_select_fusion
  160.7 0.9 constant_dynamic-update-slice_fusion.26
  161.6 0.8 constant_dynamic-update-slice_fusion.25
  168.2 1.3 pad_maximum_fusion.2
  174.6 0.9 constant_dynamic-update-slice_fusion.11
  175.5 0.9 constant_dynamic-update-slice_fusion.10
  178.6 0.9 constant_dynamic-update-slice_fusion.7
  182.0 0.9 constant_dynamic-update-slice_fusion.3
  182.8 0.9 constant_dynamic-update-slice_fusion.2
  185.4 40.5 %all-gather.3.cloned.1.call-done = bf16[27,256,256]{2,1,0:T(8,128)(2,1)} async-done(((bf16[27,64,256]{2,1,0:T(8,128)(2,1)}), bf16[27,256,256]{2,1,0:T(8,128)(2,1)}) %all-gather.3.cloned.1.call-update) | async-done | bytes 3538960 | tf_op jit(solution)/shard_map/all_gather | solution.py:224
  225.9 10.6 %fusion.20 = bf16[1024,256]{1,0:T(8,128)(2,1)} fusion(f32[1024,256]{1,0:T(8,128)S(1)} %fusion.19, bf16[1024,27,256]{2,0,1:T(8,128)(2,1)} %constant_dynamic-update-slice_fusion, bf16[27,256,256]{2,1,0:T(8,128)(2,1)} %all-gather.3.cloned.1.call-done), kind=kOutput, calls=%fused_computation.50 | convolution fusion | flops 3624402944 | bytes 19267584 | tf_op jit(solution)/shard_map/dot_general | solution.py:222
  (142 shorter events, 50.4 us)
Async XLA Ops:
  6.5 92.0 %copy-start = (bf16[2048,64]{0,1:T(8,128)(2,1)S(1)}, bf16[2048,64]{0,1:T(8,128)(2,1)}, u32[]{:S(2)}) copy-start(bf16[2048,64]{0,1:T(8,128)(2,1)} %param.16) | copy-start | bytes 786436
  8.4 26.6 %copy-start.5 = (s32[16,2]{0,1:T(2,128)S(1)}, s32[16,2]{0,1:T(2,128)}, u32[]{:S(2)}) copy-start(s32[16,2]{0,1:T(2,128)} %param.15) | copy-start | bytes 388
  8.4 26.7 %copy-start.4 = (s32[16,2,2]{0,2,1:T(2,128)S(1)}, s32[16,2,2]{0,2,1:T(2,128)}, u32[]{:S(2)}) copy-start(s32[16,2,2]{0,2,1:T(2,128)} %param.14) | copy-start | bytes 772
  9.7 18.7 %all-to-all-start = ((bf16[256,2,1024]{2,0,1:T(8,128)(2,1)}), bf16[256,2,1024]{2,0,1:T(8,128)(2,1)S(1)}, u32[]{:S(2)}, u32[]{:S(2)}) async-start(bf16[256,2,1024]{2,0,1:T(8,128)(2,1)} %copy.291), calls=%async_computation | async-start | bytes 2097152 | tf_op jit(solution)/shard_map/all_to_all | solution.py:160
  28.3 16.9 %all-to-all-start.1 = ((bf16[256,2,1024]{2,0,1:T(8,128)(2,1)}), bf16[256,2,1024]{2,0,1:T(8,128)(2,1)S(1)}, u32[]{:S(2)}, u32[]{:S(2)}) async-start(bf16[256,2,1024]{2,0,1:T(8,128)(2,1)} %copy.294), calls=%async_computation.1 | async-start | bytes 2097152 | tf_op jit(solution)/shard_map/all_to_all | solution.py:161
  45.2 16.0 %all-to-all-start.2 = ((bf16[256,2,1024]{2,0,1:T(8,128)(2,1)}), bf16[256,2,1024]{2,0,1:T(8,128)(2,1)S(1)}, u32[]{:S(2)}, u32[]{:S(2)}) async-start(bf16[256,2,1024]{2,0,1:T(8,128)(2,1)} %copy.297), calls=%async_computation.2 | async-start | bytes 2097152 | tf_op jit(solution)/shard_map/all_to_all | solution.py:162
  66.4 2.3 copy-start.1
  66.4 2.3 copy-start.2
  69.7 1.0 copy-start.3
  75.1 2.3 copy-start.1
  75.1 2.3 copy-start.2
  78.5 1.0 copy-start.3
  79.4 7.3 %copy-start.7 = (s32[4]{0:T(128)S(1)}, s32[4]{0:T(128)}, u32[]{:S(2)}) copy-start(s32[4]{0:T(128)} %param.17) | copy-start | bytes 52
  83.0 15.0 %all-to-all-start.3 = ((bf16[2,256,1024]{2,1,0:T(8,128)(2,1)}), bf16[2,256,1024]{2,1,0:T(8,128)(2,1)S(1)}, u32[]{:S(2)}, u32[]{:S(2)}) async-start(bf16[2,256,1024]{2,1,0:T(8,128)(2,1)} %bitcast.31), calls=%async_computation.3 | async-start | bytes 2097152 | tf_op jit(solution)/shard_map/all_to_all | solution.py:193
  86.6 139.3 %all-gather.3.cloned.1.call-start = ((), (), s32[]{:S(2)}) async-start(), calls=%async_computation.4 | async-start | bytes 4423680 | tf_op jit(solution)/shard_map/all_gather | solution.py:224
  105.0 6.0 %collective-permute-start.1 = (bf16[1,4,1,32,16]{4,3,2,1,0:T(8,128)(2,1)S(1)}, bf16[1,4,1,32,16]{4,3,2,1,0:T(8,128)(2,1)S(1)}, u32[]{:S(2)}, u32[]{:S(2)}) collective-permute-start(bf16[1,4,1,32,16]{4,3,2,1,0:T(8,128)(2,1)S(1)} %get-tuple-element.139), channel_id=1, source_target_pairs={{1,0},{3,2},{5,4},{7,6},{9,8},{11,10},{13,12},{15,14},{17,16},{19,... | collective-permute-start | bytes 12296 | tf_op jit(solution)/shard_map/ppermute | solution.py:28
  106.3 6.1 %collective-permute-start = (bf16[1,4,1,32,16]{4,3,2,1,0:T(8,128)(2,1)S(1)}, bf16[1,4,1,32,16]{4,3,2,1,0:T(8,128)(2,1)S(1)}, u32[]{:S(2)}, u32[]{:S(2)}) collective-permute-start(bf16[1,4,1,32,16]{4,3,2,1,0:T(8,128)(2,1)S(1)} %get-tuple-element.138), channel_id=1, source_target_pairs={{0,1},{2,3},{4,5},{6,7},{8,9},{10,11},{12,13},{14,15},{16,17},{18,... | collective-permute-start | bytes 12296 | tf_op jit(solution)/shard_map/ppermute | solution.py:26
  134.6 14.7 %copy-start.6 = (bf16[27,16,256]{2,1,0:T(8,128)(2,1)S(1)}, bf16[27,16,256]{2,1,0:T(8,128)(2,1)}, u32[]{:S(2)}) copy-start(bf16[27,16,256]{2,1,0:T(8,128)(2,1)} %param.18) | copy-start | bytes 663556
  150.1 6.2 %collective-permute-start.3 = (bf16[1,4,1,32,256]{4,3,2,1,0:T(8,128)(2,1)S(1)}, bf16[1,4,1,32,256]{4,3,2,1,0:T(8,128)(2,1)S(1)}, u32[]{:S(2)}, u32[]{:S(2)}) collective-permute-start(bf16[1,4,1,32,256]{4,3,2,1,0:T(8,128)(2,1)S(1)} %get-tuple-element.133), channel_id=1, source_target_pairs={{1,0},{3,2},{5,4},{7,6},{9,8},{11,10},{13,12},{15,14},{17,16},{19,... | collective-permute-start | bytes 196616 | tf_op jit(solution)/shard_map/ppermute | solution.py:28
  151.4 6.4 %collective-permute-start.2 = (bf16[1,4,1,32,256]{4,3,2,1,0:T(8,128)(2,1)S(1)}, bf16[1,4,1,32,256]{4,3,2,1,0:T(8,128)(2,1)S(1)}, u32[]{:S(2)}, u32[]{:S(2)}) collective-permute-start(bf16[1,4,1,32,256]{4,3,2,1,0:T(8,128)(2,1)S(1)} %get-tuple-element.132), channel_id=1, source_target_pairs={{0,1},{2,3},{4,5},{6,7},{8,9},{10,11},{12,13},{14,15},{16,17},{18,... | collective-permute-start | bytes 196616 | tf_op jit(solution)/shard_map/ppermute | solution.py:26
Sparse Core Ops, SparseCore 0:
  156.3 69.5 all-gather.2
where the time goes:
time: 244 us; the launch traced here: 243 us
  waiting for transfers between devices  83.7 us (34%)
  local copies, waits for them, and re-layouts  79.3 us (32%)
  starting transfers between devices  27.1 us (11%)
  other arithmetic  16.9 us (7%)
  between operations  15.9 us (7%)
  matrix products  14.8 us (6%)
  blocking collectives  5.43 us (2%)
    all_gather x1, waiting for transfers between devices, local(): lax.all_gather(second_kernel, 'grp', axis=1, tiled=True)  40.5 us
    unnamed x57, local copies, waits for them, and re-layouts  35.7 us
    all_to_all x1, waiting for transfers between devices, local(): lax.all_to_all(flat_query, 'sp', split_axis=1, concat_axis=0, tiled=True)  11.3 us
    another operation x3, local copies, waits for them, and re-layouts, window_columns(): stacked = jnp.stack(pieces, axis=-2)  11 us
    dot_general x1, matrix products, local(): lax.dot_general(columns, lax.all_gather(second_kernel, 'grp', axis=1, til...  10.6 us
    all_to_all x1, waiting for transfers between devices, local(): lax.all_to_all(flat_value, 'sp', split_axis=1, concat_axis=0, tiled=True)  10.5 us
    all_to_all x1, waiting for transfers between devices, local(): lax.all_to_all(flat_key, 'sp', split_axis=1, concat_axis=0, tiled=True)  9.53 us
    ppermute x2, starting transfers between devices, padded_2(): lax.ppermute(tail, axis, [(i, (i + 1) % count) for i in range(ends)])  9.49 us
  transfers between devices with their start and end apart: 9, of which 8 were waited for; matrix products, arithmetic and copies ran while one was open for 14% of the time, Pallas kernels for 0%

commit v1 on v0

v1 whole, which is shorter than its diff:
```python
import functools

import jax
import jax.numpy as jnp
from jax import lax
from jax.experimental import pallas as pl
from jax.experimental.pallas import tpu as pltpu
from jax.sharding import PartitionSpec as P

HEADS = 16
HD = 128
LAT = 16
CH = 256
TT = 4
TH = 8
TW = 8

VAE_SCALE = 1.0 / 0.476986
SCORE_UNIT = HD**-0.5 * 1.4426950408889634
HEAD_BLOCK = 4
NARROW = 4 * LAT
MIB = 1 << 20


def partial_head(head, q, k, v, tiles_ref, counts_ref):
    keys, queries = k.shape[0], q.shape[0]
    tile_count = tiles_ref.shape[1]
    keep = tiles_ref.shape[2]
    scores = lax.dot_general(k, q, (((1,), (1,)), ((), ())), preferred_element_type=jnp.float32)
    lane = lax.broadcasted_iota(jnp.int32, (1, queries), 1)
    lane_tile = lax.rem(lax.div(lane, TW), tile_count)
    rows = []
    for key_tile in range(tile_count):
        row = jnp.zeros((1, queries), jnp.float32)
        for query_tile in range(tile_count):
            live = jnp.bool_(False)
            for slot in range(keep):
                here = jnp.logical_and(
                    tiles_ref[head, query_tile, slot] == key_tile, slot < counts_ref[head, query_tile]
                )
                live = jnp.logical_or(live, here)
            row = jnp.where(lane_tile == query_tile, jnp.where(live, 0.0, -1e30), row)
        rows.append(row[None])
    bias = jnp.concatenate(rows, axis=0)
    scores = scores.reshape(keys // (tile_count * TW), tile_count, TW, queries) + bias[None]
    scores = scores.reshape(keys, queries)
    top = jnp.max(scores, axis=0, keepdims=True)
    power = jnp.exp2((scores - top) * SCORE_UNIT)
    total = jnp.sum(power, axis=0, keepdims=True)
    out = lax.dot_general(
        v, power.astype(jnp.bfloat16), (((0,), (0,)), ((), ())), preferred_element_type=jnp.float32
    )
    return top * SCORE_UNIT, total, out


def own_kernel(tiles_ref, counts_ref, q_ref, k_ref, v_ref, w_ref, level_ref, mapped_ref):
    block = pl.program_id(0)
    for i in range(HEAD_BLOCK):
        cols = slice(i * HD, (i + 1) * HD)
        head = block * HEAD_BLOCK + i
        top, total, out = partial_head(
            head, q_ref[:, cols], k_ref[:, cols], v_ref[:, cols], tiles_ref, counts_ref
        )
        out = (out / total).astype(jnp.bfloat16)
        level_ref[pl.ds(head, 1), :] = top + jnp.log2(total)
        mapped_ref[i] = lax.dot_general(
            w_ref[cols, :], out, (((0,), (0,)), ((), ())), preferred_element_type=jnp.float32
        )


def other_kernel(tiles_ref, counts_ref, q_ref, k_ref, v_ref, w_ref, level_ref, sent_ref):
    block = pl.program_id(0)
    mapped = jnp.zeros((NARROW, q_ref.shape[0]), jnp.float32)
    for i in range(HEAD_BLOCK):
        cols = slice(i * HD, (i + 1) * HD)
        head = block * HEAD_BLOCK + i
        top, total, out = partial_head(
            head, q_ref[:, cols], k_ref[:, cols], v_ref[:, cols], tiles_ref, counts_ref
        )
        theirs = level_ref[pl.ds(head, 1), :]
        mine = top + jnp.log2(total)
        high = jnp.maximum(mine, theirs)
        level = high + jnp.log2(jnp.exp2(mine - high) + jnp.exp2(theirs - high))
        out = (out * jnp.exp2(top - level)).astype(jnp.bfloat16)
        sent_ref[pl.ds(NARROW + head, 1), :] = jnp.exp2(theirs - level)
        mapped = mapped + lax.dot_general(
            w_ref[cols, :], out, (((0,), (0,)), ((), ())), preferred_element_type=jnp.float32
        )

    @pl.when(block == 0)
    def _():
        sent_ref[0:NARROW, :] = mapped

    @pl.when(block > 0)
    def _():
        sent_ref[0:NARROW, :] = sent_ref[0:NARROW, :] + mapped


def merge_kernel(got_ref, mapped_ref, out_ref):
    total = got_ref[0:NARROW, :]
    for head in range(HEADS):
        total = total + mapped_ref[head] * got_ref[NARROW + head : NARROW + head + 1, :]
    twice = jnp.concatenate([total, total], axis=0)
    out_ref[...] = twice.T.astype(jnp.bfloat16)


def split_attention(flat_query, flat_key, flat_value, kept_tiles, kept_counts, patch_weight):
    tokens = flat_query.shape[0]
    other_query = lax.ppermute(flat_query, "sp", [(0, 1), (1, 0)])
    smem = pl.BlockSpec(memory_space=pltpu.SMEM)
    heads = pl.BlockSpec((tokens, HEAD_BLOCK * HD), lambda i: (0, i))
    weight = pl.BlockSpec((HEAD_BLOCK * HD, NARROW), lambda i: (i, 0))

    def whole(*shape):
        return pl.BlockSpec(shape, lambda i: (0,) * len(shape))

    params = pltpu.CompilerParams(
        dimension_semantics=("arbitrary",), vmem_limit_bytes=32 * MIB
    )
    cost = pl.CostEstimate(
        flops=4 * HEADS * tokens * tokens * HD,
        bytes_accessed=3 * tokens * HEADS * HD * 2,
        transcendentals=HEADS * tokens * tokens,
    )
    level, mapped = pl.pallas_call(
        own_kernel,
        grid=(HEADS // HEAD_BLOCK,),
        in_specs=[smem, smem, heads, heads, heads, weight],
        out_specs=[
            whole(HEADS, tokens),
            pl.BlockSpec((HEAD_BLOCK, NARROW, tokens), lambda i: (i, 0, 0)),
        ],
        out_shape=[
            jax.ShapeDtypeStruct((HEADS, tokens), jnp.float32),
            jax.ShapeDtypeStruct((HEADS, NARROW, tokens), jnp.float32),
        ],
        compiler_params=params,
        cost_estimate=cost,
        name="own_keys",
    )(kept_tiles, kept_counts, flat_query, flat_key, flat_value, patch_weight)
    other_level = lax.ppermute(level, "sp", [(0, 1), (1, 0)])
    sent = pl.pallas_call(
        other_kernel,
        grid=(HEADS // HEAD_BLOCK,),
        in_specs=[smem, smem, heads, heads, heads, weight, whole(HEADS, tokens)],
        out_specs=whole(NARROW + HEADS, tokens),
        out_shape=jax.ShapeDtypeStruct((NARROW + HEADS, tokens), jnp.float32),
        compiler_params=params,
        cost_estimate=cost,
        name="other_queries",
    )(kept_tiles, kept_counts, other_query, flat_key, flat_value, patch_weight, other_level)
    got = lax.ppermute(sent, "sp", [(0, 1), (1, 0)])
    return pl.pallas_call(
        merge_kernel,
        out_shape=jax.ShapeDtypeStruct((tokens, 2 * NARROW), jnp.bfloat16),
        name="merge",
    )(got, mapped)


def to_tiles(grid, tile_size):
    frame_count, row_count, col_count, feature_width = grid.shape
    tiled = grid.reshape(
        frame_count // TT, TT, row_count // TH, TH, col_count // TW, TW, feature_width
    ).transpose(0, 2, 4, 1, 3, 5, 6)
    return tiled.reshape(-1, tile_size, feature_width)


def from_tiles(tiles, frame_count, row_count, col_count):
    feature_width = tiles.shape[-1]
    grid = tiles.reshape(
        frame_count // TT, row_count // TH, col_count // TW, TT, TH, TW, feature_width
    ).transpose(0, 3, 1, 4, 2, 5, 6)
    return grid.reshape(frame_count, row_count, col_count, feature_width)


def attend_tiles(query_tiles, key_tiles, value_tiles, tile_index, live_count):
    head_count = query_tiles.shape[0]
    tile_size = query_tiles.shape[2]
    head_size = query_tiles.shape[3]
    keep_count = tile_index.shape[2]

    def one_tile(packed):
        query_block, index_block, count_block = packed
        key_sel = jax.vmap(lambda source, picks: source[picks])(key_tiles, index_block).reshape(
            head_count, keep_count * tile_size, head_size
        )
        value_sel = jax.vmap(lambda source, picks: source[picks])(value_tiles, index_block).reshape(
            head_count, keep_count * tile_size, head_size
        )
        scores = jnp.einsum(
            "hqd,hkd->hqk", query_block, key_sel, preferred_element_type=jnp.float32
        ) * head_size ** (-0.5)
        live = jnp.arange(keep_count, dtype=jnp.int32)[None, :] < count_block[:, None]
        live = jnp.repeat(live, tile_size, axis=1)[:, None, :]
        scores = jnp.where(live, scores, -1e30)
        row_top = jnp.max(scores, axis=-1, keepdims=True)
        exponent = jnp.where(live, jnp.exp(scores - row_top), 0.0)
        weights = (exponent / jnp.sum(exponent, axis=-1, keepdims=True)).astype(jnp.bfloat16)
        result = jnp.einsum("hqk,hkd->hqd", weights, value_sel, preferred_element_type=jnp.float32)
        return result.astype(jnp.bfloat16)

    return lax.map(
        one_tile,
        (
            query_tiles.transpose(1, 0, 2, 3),
            tile_index.transpose(1, 0, 2),
            live_count.transpose(1, 0),
        ),
    )


def exchanged_attention(queries, key_states, value_states, kept_tiles, kept_counts, patch_weight):
    frame_count, local_rows, token_cols, feature_count = queries.shape[2:]
    tokens = frame_count * local_rows * token_cols
    sp_count = lax.axis_size("sp")
    sp_rank = lax.axis_index("sp")
    local_heads = HEADS // sp_count
    clip_rows = local_rows * sp_count
    tile_size = TT * TH * TW
    mixed_query, mixed_key, mixed_value = (
        lax.all_to_all(part.reshape(tokens, feature_count), "sp", split_axis=1, concat_axis=0, tiled=True)
        for part in (queries, key_states, value_states)
    )
    own_width = mixed_query.shape[1]

    def head_tiles(mixed):
        grid = mixed.reshape(sp_count, frame_count, local_rows, token_cols, own_width).transpose(
            1, 0, 2, 3, 4
        )
        tiles = to_tiles(grid.reshape(frame_count, clip_rows, token_cols, own_width), tile_size)
        return tiles.reshape(tiles.shape[0], tile_size, local_heads, HD).transpose(2, 0, 1, 3)

    outputs = attend_tiles(
        head_tiles(mixed_query),
        head_tiles(mixed_key),
        head_tiles(mixed_value),
        lax.dynamic_slice_in_dim(kept_tiles, sp_rank * local_heads, local_heads, 0),
        lax.dynamic_slice_in_dim(kept_counts, sp_rank * local_heads, local_heads, 0),
    )
    tile_count = outputs.shape[0]
    attended = from_tiles(
        outputs.transpose(0, 2, 1, 3).reshape(tile_count, tile_size, own_width),
        frame_count,
        clip_rows,
        token_cols,
    )
    attended = attended.reshape(frame_count, sp_count, local_rows, token_cols, own_width).transpose(
        1, 0, 2, 3, 4
    )
    attended = attended.reshape(sp_count * tokens, own_width)
    restored = lax.all_to_all(attended, "sp", split_axis=0, concat_axis=1, tiled=True)
    latent = jnp.dot(restored, patch_weight, preferred_element_type=jnp.float32)
    latent = latent.astype(jnp.bfloat16)
    return jnp.concatenate([latent, latent], axis=1)


def first_weights(first_kernel):
    plain = first_kernel.reshape(3, 3, 3, LAT, CH)
    both_rows = jnp.stack(
        [jnp.pad(plain, ((0, 0), (r, 1 - r), (0, 0), (0, 0), (0, 0))) for r in range(2)], axis=4
    )
    matrices = []
    for c in range(2):
        wide = jnp.pad(both_rows, ((0, 0), (0, 0), (c, 1 - c), (0, 0), (0, 0), (0, 0)))
        wide = wide.reshape(3, 2, 2, 2, 2, LAT, 2, CH).transpose(0, 1, 3, 2, 4, 5, 6, 7)
        matrices.append(wide.reshape(3 * 2 * 2 * NARROW, 2 * CH))
    return matrices


def decode_kernel(
    frames,
    rows,
    cols,
    place_ref,
    latent_ref,
    left_ref,
    right_ref,
    mine_ref,
    theirs_ref,
    out_ref,
    token_ref,
    pair_ref,
    first_ref,
    act_ref,
    wide_ref,
    kernel_ref,
    sems,
):
    rank = place_ref[1]
    ranks = place_ref[2]
    half = place_ref[3]
    copies = [
        pltpu.make_async_copy(mine_ref, kernel_ref.at[half], sems.at[0]),
        pltpu.make_async_copy(theirs_ref, kernel_ref.at[1 - half], sems.at[1]),
    ]
    for copy in copies:
        copy.start()
    at_first = rank == 0
    at_last = rank == ranks - 1

    for f in range(frames):
        for r in range(rows):
            token_ref[f, 1 + r, 8 : 8 + cols, :] = latent_ref[0, rank, f, r].astype(jnp.float32)
        above = latent_ref[0, jnp.maximum(rank - 1, 0), f, rows - 1].astype(jnp.float32)
        edge = pltpu.roll(token_ref[f, 1, 8 : 8 + cols, :], 2 * LAT, 1)
        token_ref[f, 0, 8 : 8 + cols, :] = jnp.where(at_first, edge, above)
        below = latent_ref[0, jnp.minimum(rank + 1, ranks - 1), f, 0].astype(jnp.float32)
        edge = pltpu.roll(token_ref[f, rows, 8 : 8 + cols, :], 2 * NARROW - 2 * LAT, 1)
        token_ref[f, rows + 1, 8 : 8 + cols, :] = jnp.where(at_last, edge, below)
    for f in range(frames):
        for r in range(rows + 2):
            start = token_ref[f, r, 8:16, :]
            token_ref[f, r, 7:8, :] = pltpu.roll(start, LAT, 1)[0:1]
            end = token_ref[f, r, cols : 8 + cols, :]
            token_ref[f, r, 8 + cols : 9 + cols, :] = pltpu.roll(end, 2 * NARROW - LAT, 1)[7:8]

    lane = lax.broadcasted_iota(jnp.int32, (1, 1, cols, 2 * NARROW), 3)
    for side in range(2):
        pair = jnp.where(
            lane < NARROW,
            token_ref[:, :, 7 + side : 7 + side + cols, :],
            token_ref[:, :, 8 + side : 8 + side + cols, :],
        ).astype(jnp.bfloat16)
        pair_ref[side, 2:] = pair
        pair_ref[side, 0] = pair[0]
        pair_ref[side, 1] = pair[0]

    gaps = rows + 1
    for side, weight_ref in ((0, left_ref), (1, right_ref)):
        columns = jnp.concatenate(
            [
                pair_ref[side, dt : dt + frames, rr : rr + gaps].reshape(frames * gaps * cols, 2 * NARROW)
                for dt in range(3)
                for rr in range(2)
            ],
            axis=1,
        )
        first = jnp.dot(columns, weight_ref[...], preferred_element_type=jnp.float32) * VAE_SCALE
        first = first.astype(jnp.bfloat16).astype(jnp.float32)
        act = first / (1.0 + jnp.exp(-first))
        first = first.reshape(frames, gaps, cols, 2 * CH)
        act = act.reshape(frames, gaps, cols, 2 * CH)
        for f in range(frames):
            for g in range(gaps):
                for ro in range(2):
                    for part in range(CH // 128):
                        lanes = slice(ro * CH + part * 128, ro * CH + part * 128 + 128)
                        row = 2 * g + ro
                        into = pl.ds(8 + side, cols, stride=2)
                        first_ref[part, f, row, into, :] = first[f, g, :, lanes]
                        act_ref[part, f, row, into, :] = act[f, g, :, lanes]

    width = 2 * cols
    height = 2 * rows
    for part in range(CH // 128):
        for f in range(frames):
            act_ref[part, f, 0] = jnp.where(at_first, act_ref[part, f, 1], act_ref[part, f, 0])
            act_ref[part, f, height + 1] = jnp.where(
                at_last, act_ref[part, f, height], act_ref[part, f, height + 1]
            )
        act_ref[part, :, :, 7:8, :] = act_ref[part, :, :, 8:9, :]
        act_ref[part, :, :, 8 + width : 9 + width, :] = act_ref[part, :, :, 7 + width : 8 + width, :]
        for dz in range(3):
            lanes = slice(dz * CH + part * 128, dz * CH + part * 128 + 128)
            shifted = act_ref[part, :, :, 7 + dz : 7 + dz + width, :].astype(jnp.bfloat16)
            wide_ref[2:, :, :, lanes] = shifted
            wide_ref[0, :, :, lanes] = shifted[0]
            wide_ref[1, :, :, lanes] = shifted[0]

    for copy in copies:
        copy.wait()
    cells = frames * height * width
    total = None
    for dt in range(3):
        for dy in range(3):
            window = wide_ref[dt : dt + frames, dy : dy + height].reshape(cells, 3 * CH)
            weight = jnp.concatenate(
                [
                    jnp.concatenate(
                        [kernel_ref[side, :, (dt * 3 + dy) * 3 + dz].reshape(CH, CH // 2) for side in range(2)],
                        axis=1,
                    )
                    for dz in range(3)
                ],
                axis=0,
            )
            product = jnp.dot(window, weight, preferred_element_type=jnp.float32)
            total = product if total is None else total + product
    total = total.reshape(frames, height, width, CH)
    for part in range(CH // 128):
        lanes = slice(part * 128, part * 128 + 128)
        residual = first_ref[part, :, 1 : 1 + height, 8 : 8 + width, :]
        out_ref[:, :, :, lanes] = (total[:, :, :, lanes] + residual).astype(jnp.bfloat16)


def decode(place, gathered, left, right, mine, theirs):
    _, ranks, frames, rows, cols, _ = gathered.shape
    height, width = 2 * rows, 2 * cols

    def whole(shape):
        return pl.BlockSpec(shape, lambda i, place: (0,) * len(shape))

    grid_spec = pltpu.PrefetchScalarGridSpec(
        num_scalar_prefetch=1,
        grid=(1,),
        in_specs=[
            pl.BlockSpec((1,) + gathered.shape[1:], lambda i, place: (place[0], 0, 0, 0, 0, 0)),
            whole(left.shape),
            whole(right.shape),
            pl.BlockSpec(memory_space=pl.ANY),
            pl.BlockSpec(memory_space=pl.ANY),
        ],
        out_specs=whole((frames, height, width, CH)),
        scratch_shapes=[
            pltpu.VMEM((frames, rows + 2, cols + 16, 2 * NARROW), jnp.float32),
            pltpu.VMEM((2, frames + 2, rows + 2, cols, 2 * NARROW), jnp.bfloat16),
            pltpu.VMEM((CH // 128, frames, height + 2, width + 16, 128), jnp.float32),
            pltpu.VMEM((CH // 128, frames, height + 2, width + 16, 128), jnp.float32),
            pltpu.VMEM((frames + 2, height + 2, width, 3 * CH), jnp.bfloat16),
            pltpu.VMEM((2,) + mine.shape, jnp.bfloat16),
            pltpu.SemaphoreType.DMA((2,)),
        ],
    )
    return pl.pallas_call(
        functools.partial(decode_kernel, frames, rows, cols),
        grid_spec=grid_spec,
        out_shape=jax.ShapeDtypeStruct((frames, height, width, CH), jnp.bfloat16),
        compiler_params=pltpu.CompilerParams(vmem_limit_bytes=48 * MIB),
        cost_estimate=pl.CostEstimate(
            flops=2 * frames * height * width * 27 * CH * CH,
            bytes_accessed=27 * CH * CH * 2 + frames * height * width * CH * 2,
            transcendentals=frames * height * width * CH,
        ),
        name="decode_block",
    )(place, gathered, left, right, mine, theirs)


def local(
    queries,
    key_states,
    value_states,
    kept_tiles,
    kept_counts,
    patch_weight,
    decode_slot,
    first_kernel,
    second_kernel,
):
    frames, rows, cols, feature_count = queries.shape[2:]
    tokens = frames * rows * cols
    sp_count = lax.axis_size("sp")
    sp_rank = lax.axis_index("sp")
    segment_count = lax.axis_size("segment")
    segment_rank = lax.axis_index("segment")

    half = lax.rem(segment_rank, 2)
    share = lax.dynamic_slice_in_dim(second_kernel, half * (CH // 2), CH // 2, 2)
    mine = lax.all_gather(share, "grp", axis=0, tiled=False)
    theirs = lax.ppermute(mine, "segment", [(i, i ^ 1) for i in range(segment_count)])
    left, right = first_weights(first_kernel)[::-1]

    if sp_count == 2 and rows * sp_count == TH and frames == TT:
        latent = split_attention(
            queries.reshape(tokens, feature_count),
            key_states.reshape(tokens, feature_count),
            value_states.reshape(tokens, feature_count),
            kept_tiles,
            kept_counts,
            patch_weight,
        )
    else:
        latent = exchanged_attention(
            queries, key_states, value_states, kept_tiles, kept_counts, patch_weight
        )

    gathered = lax.all_gather(latent, ("segment", "sp"), axis=0, tiled=False)
    gathered = gathered.reshape(segment_count, sp_count, frames, rows, cols, 2 * NARROW)
    picks = (decode_slot == segment_rank).astype(jnp.int32)
    source = jnp.sum(jnp.arange(segment_count, dtype=jnp.int32) * picks)
    place = jnp.stack([source, sp_rank, jnp.int32(sp_count), half]).astype(jnp.int32)
    return decode(place, gathered, left, right, mine, theirs)[None, None]


def solution(mesh):
    return jax.shard_map(
        local,
        mesh=mesh,
        in_specs=(
            P("segment", "grp", None, "sp", None, None),
            P("segment", "grp", None, "sp", None, None),
            P("segment", "grp", None, "sp", None, None),
            P(),
            P(),
            P(),
            P(),
            P(),
            P(None, "grp", None),
        ),
        out_specs=P("segment", "grp", None, "sp", None, None),
        check_vma=False,
    )
```

time: 244 us -> 128 us (0.52)
  local copies, waits for them, and re-layouts: 79.3 us -> 16.7 us
  waiting for transfers between devices: 83.7 us -> 52.5 us
  starting transfers between devices: 27.1 us -> 3.57 us
  Pallas kernels: 0 us -> 22.2 us
  other arithmetic: 16.9 us -> 1.52 us
  matrix products: 14.8 us -> 0 us
  blocking collectives: 5.43 us -> 16.6 us
    all_to_all x4 -> x0, waiting for transfers between devices: 40.2 us -> none  [the longest x1 11.3 us: local(): lax.all_to_all(flat_query, 'sp', split_axis=1, concat_axis=0, tiled=True)]
    unnamed x57 -> x29, local copies, waits for them, and re-layouts: 35.7 us -> 11.6 us
    pallas_call x0 -> x4, Pallas kernels: none -> 22.2 us  [the longest x1 7.8 us: decode(): pl.pallas_call(functools.partial(decode_kernel, frames, rows, cols), grid...]
    another operation x6 -> x1, local copies, waits for them, and re-layouts: 17.9 us -> 0.04 us  [first_weights(): jnp.stack([jnp.pad(plain, ((0, 0), (r, 1 - r), (0, 0), (0, 0), (0, 0))) f...]
    all_to_all x4 -> x0, starting transfers between devices: 15 us -> none  [the longest x1 4.23 us: local(): lax.all_to_all(flat_query, 'sp', split_axis=1, concat_axis=0, tiled=True)]
    dot_general x7 -> x0, matrix products: 14.8 us -> none  [the longest x1 10.6 us: local(): lax.dot_general(columns, lax.all_gather(second_kernel, 'grp', axis=1, til...]
    all_gather x1, blocking collectives: 5.43 us -> 16.6 us  [local(): gathered = lax.all_gather(latent, ('segment', 'sp'), axis=0, tiled=False)]
    all_to_all x7 -> x0, local copies, waits for them, and re-layouts: 9.84 us -> none  [the longest x2 3.12 us: local(): lax.all_to_all(flat_key, 'sp', split_axis=1, concat_axis=0, tiled=True)]
  transfers between devices with their start and end apart: 9 -> 5, of which waited for: 8 -> 3; matrix products, arithmetic and copies ran while one was open for 14% -> 8% of each run, Pallas kernels for 0% -> 11%
where the time goes in v1:
time: 128 us; the launch traced here: 127 us
  waiting for transfers between devices  52.5 us (41%)
  Pallas kernels  22.2 us (17%)
  local copies, waits for them, and re-layouts  16.7 us (13%)
  blocking collectives  16.6 us (13%)
  between operations  13.5 us (11%)
  starting transfers between devices  3.57 us (3%)
  other arithmetic  1.52 us (1%)
    all_gather x1, waiting for transfers between devices, local(): mine = lax.all_gather(share, 'grp', axis=0, tiled=False)  43.4 us
    all_gather x1, blocking collectives, local(): gathered = lax.all_gather(latent, ('segment', 'sp'), axis=0, tiled=False)  16.6 us
    unnamed x29, local copies, waits for them, and re-layouts  11.6 us
    pallas_call x1, Pallas kernels, decode(): pl.pallas_call(functools.partial(decode_kernel, frames, rows, cols), grid...  7.8 us
    ppermute x1, waiting for transfers between devices, split_attention(): other_level = lax.ppermute(level, 'sp', [(0, 1), (1, 0)])  6.87 us
    pallas_call x1, Pallas kernels, split_attention(): pl.pallas_call(other_kernel, grid=(HEADS // HEAD_BLOCK,), in_specs=[smem,...  6.22 us
    pallas_call x1, Pallas kernels, split_attention(): pl.pallas_call(own_kernel, grid=(HEADS // HEAD_BLOCK,), in_specs=[smem, s...  6.09 us
    transpose x2, local copies, waits for them, and re-layouts, first_weights(): wide.reshape(3, 2, 2, 2, 2, LAT, 2, CH).transpose(0, 1, 3, 2, 4, 5, 6, 7)  2.78 us
  transfers between devices with their start and end apart: 5, of which 3 were waited for; matrix products, arithmetic and copies ran while one was open for 8% of the time, Pallas kernels for 11%

profile of v1, /device:TPU:0, one launch (start us, length us, event | category | flops | bytes accessed | tf_op | source)
XLA Modules:
  0.0 126.5 jit_solution(6374401610813499077)
XLA Ops:
  6.5 0.0 copy-start
  6.5 0.0 copy-start.2
  6.5 0.0 copy-start.1
  6.5 0.0 all-gather.4.cloned.1.call-start
  6.6 1.1 copy-done
  7.7 0.8 constant_dynamic-slice_fusion
  8.6 0.0 all-gather.4.cloned.1.call-update
  8.6 43.4 %all-gather.4.cloned.1.call-done = bf16[108,64,128]{2,1,0:T(8,128)(2,1)} async-done(((bf16[27,64,128]{2,1,0:T(8,128)(2,1)}), bf16[108,64,128]{2,1,0:T(8,128)(2,1)}) %all-gather.4.cloned.1.call-update) | async-done | bytes 1769488 | tf_op jit(solution)/shard_map/all_gather | solution.py:458
  52.0 0.0 collective-permute-start.3
  52.0 1.5 %collective-permute-start = (bf16[256,2048]{1,0:T(8,128)(2,1)}, bf16[256,2048]{1,0:T(8,128)(2,1)}, u32[]{:S(2)}, u32[]{:S(2)}) collective-permute-start(bf16[256,2048]{1,0:T(8,128)(2,1)} %bitcast.32), channel_id=1, source_target_pairs={{0,1},{1,0},{2,3},{3,2},{4,5},{5,4},{6,7},{7,6},{8,9},{9,8},{10,11... | collective-permute-start | bytes 3145736 | tf_op jit(solution)/shard_map/ppermute | solution.py:109
  53.5 0.8 copy.29.counts_ref
  54.2 0.8 copy.28.tiles_ref
  55.0 1.2 copy.30.w_ref
  56.2 0.0 copy-done.2
  56.2 0.0 copy-done.1
  56.2 0.0 copy-start.3
  56.2 1.2 copy-done.3
  57.5 6.1 %own_keys.1 = (f32[16,256]{1,0:T(8,128)}, f32[16,64,256]{2,1,0:T(8,128)S(1)}) custom-call(s32[16,2,2]{2,1,0:T(2,128)S(1)} %copy.28.tiles_ref, s32[16,2]{1,0:T(8,128)S(1)} %copy.29.counts_ref, bf16[256,2048]{1,0:T(8,128)(2,1)S(1)} %bitcast.33, bf16[256,2048]{1,0:T(8,128)(2,1)S(1)} %bitcast.28, bf16[256,2048]{1,0:T(8,128)(2,1)S(1)} %bitcast.30, ...), custom_call_target="tpu_custom_call" | custom-call | flops 536870912 | bytes 3145728 | tf_op jit(solution)/shard_map/own_keys/pallas_call | solution.py:125
  63.5 0.0 copy-start.4
  63.6 0.6 collective-permute-start.1
  64.1 0.0 copy-done.9
  64.2 0.0 copy-start.11
  64.2 0.1 pad_maximum_fusion
  64.2 1.4 %fusion.1 = (bf16[3,4,4,16,2,256]{5,3,4,2,1,0:T(8,128)(2,1)}, bf16[3,4,4,16,2,256]{5,3,4,2,1,0:T(8,128)(2,1)}) fusion(bf16[3,4,3,16,2,256]{5,3,4,2,1,0:T(8,128)(2,1)S(1)} %pad_maximum_fusion), kind=kLoop, calls=%fused_computation.7 | loop fusion | bytes 2162688 | tf_op jit(solution)/shard_map/jit(_pad)/pad | solution.py:264
  65.6 0.0 copy-done.4
  65.6 0.0 copy-done.11
  65.6 0.7 fusion
  66.3 0.0 copy-start.8
  66.3 2.0 %copy.33 = bf16[3,2,2,2,2,16,2,256]{7,6,5,4,3,2,1,0:T(2,128)(2,1)S(1)} copy(bf16[3,2,2,2,2,16,2,256]{7,5,6,4,2,3,1,0:T(8,128)(2,1)} %bitcast.40) | data formatting | bytes 1572864 | tf_op jit(solution)/shard_map/transpose | solution.py:265
  68.3 1.1 copy.35
  69.4 0.0 copy-done.8
  69.4 0.8 copy.32
  70.2 1.1 copy.34
  71.2 6.9 %collective-permute-done.1.level_ref = f32[16,256]{1,0:T(8,128)S(1)} collective-permute-done((f32[16,256]{1,0:T(8,128)}, f32[16,256]{1,0:T(8,128)S(1)}, u32[]{:S(2)}, u32[]{:S(2)}) %collective-permute-start.1) | collective-permute-done | bytes 16416 | tf_op jit(solution)/shard_map/ppermute | solution.py:141
  78.1 0.0 collective-permute-done.q_ref
  78.1 6.2 %other_queries.1 = f32[80,256]{1,0:T(8,128)S(1)} custom-call(s32[16,2,2]{2,1,0:T(2,128)S(1)} %copy.28.tiles_ref, s32[16,2]{1,0:T(8,128)S(1)} %copy.29.counts_ref, bf16[256,2048]{1,0:T(8,128)(2,1)} %collective-permute-done.q_ref, bf16[256,2048]{1,0:T(8,128)(2,1)S(1)} %bitcast.29, bf16[256,2048]{1,0:T(8,128)(2,1)S(1)} %bitcast.31, ...), custom_call_target="tpu_custom_call" | custom-call | flops 536870912 | bytes 3145728 | tf_op jit(solution)/shard_map/other_queries/pallas_call | solution.py:142
  84.3 1.5 %collective-permute-start.2 = (f32[80,256]{1,0:T(8,128)S(1)}, f32[80,256]{1,0:T(8,128)S(1)}, u32[]{:S(2)}, u32[]{:S(2)}) collective-permute-start(f32[80,256]{1,0:T(8,128)S(1)} %other_queries.1), channel_id=1, source_target_pairs={{0,1},{1,0},{2,3},{3,2},{4,5},{5,4},{6,7},{7,6},{8,9},{9,8},{10,11... | collective-permute-start | bytes 245768 | tf_op jit(solution)/shard_map/ppermute | solution.py:152
  85.9 0.8 pad_add_fusion.place_ref
  86.6 2.2 %collective-permute-done.2.got_ref = f32[80,256]{1,0:T(8,128)S(1)} collective-permute-done((f32[80,256]{1,0:T(8,128)S(1)}, f32[80,256]{1,0:T(8,128)S(1)}, u32[]{:S(2)}, u32[]{:S(2)}) %collective-permute-start.2) | collective-permute-done | bytes 81952 | tf_op jit(solution)/shard_map/ppermute | solution.py:152
  88.9 0.0 copy-start.10
  88.9 0.6 copy-done.10
  89.5 2.1 %merge.1 = bf16[256,128]{1,0:T(8,128)(2,1)} custom-call(f32[80,256]{1,0:T(8,128)} %copy-done.10, f32[16,64,256]{2,1,0:T(8,128)} %copy-done.4), custom_call_target="tpu_custom_call" | custom-call | tf_op jit(solution)/shard_map/merge/pallas_call | solution.py:153
  91.6 16.6 %all-gather = bf16[2048,128]{1,0:T(8,128)(2,1)S(1)} all-gather(bf16[256,128]{1,0:T(8,128)(2,1)} %merge.1), channel_id=2, replica_groups=mesh['segment'=4,'grp'=4,'sp'=2] {'segment','sp'}, dimensions={0}, use_global_device_ids=true | all-gather | bytes 589824 | tf_op jit(solution)/shard_map/all_gather | solution.py:476
  108.1 0.0 collective-permute-done.3.theirs_ref
  108.1 1.1 copy-done.5
  109.3 1.1 copy-done.6
  110.4 1.5 %copy-done.7 = bf16[108,64,128]{2,1,0:T(8,128)(2,1)S(1)} copy-done((bf16[108,64,128]{2,1,0:T(8,128)(2,1)S(1)}, bf16[108,64,128]{2,1,0:T(8,128)(2,1)}, u32[]{:S(2)}) %copy-start.7) | copy-done | bytes 1769496
  111.9 7.8 %decode_block.1 = bf16[4,8,32,256]{3,2,1,0:T(8,128)(2,1)} custom-call(s32[4]{0:T(128)S(1)} %pad_add_fusion.place_ref, bf16[4,2,4,4,16,128]{5,4,3,2,1,0:T(8,128)(2,1)S(1)} %bitcast.36, bf16[768,512]{1,0:T(8,128)(2,1)S(1)} %bitcast.35, bf16[768,512]{1,0:T(8,128)(2,1)S(1)} %bitcast.34, bf16[4,27,64,128]{3,2,1,0:T(8,128)(2,1)S(1)} %bitcast.38, ...), custom_call_target="tpu_custom_call" | custom-call | flops 3623878656 | bytes 4063232 | tf_op jit(solution)/shard_map/decode_block/pallas_call | solution.py:424
  (5 shorter events, 0.0 us)
Async XLA Ops:
  6.5 1.2 copy-start
  6.5 49.7 %copy-start.2 = (bf16[1,1,4,4,16,2048]{5,4,3,2,1,0:T(8,128)(2,1)S(1)}, bf16[1,1,4,4,16,2048]{5,4,3,2,1,0:T(8,128)(2,1)}, u32[]{:S(2)}) copy-start(bf16[1,1,4,4,16,2048]{5,4,3,2,1,0:T(8,128)(2,1)} %param.11) | copy-start | bytes 3145732
  6.5 49.7 %copy-start.1 = (bf16[1,1,4,4,16,2048]{5,4,3,2,1,0:T(8,128)(2,1)S(1)}, bf16[1,1,4,4,16,2048]{5,4,3,2,1,0:T(8,128)(2,1)}, u32[]{:S(2)}) copy-start(bf16[1,1,4,4,16,2048]{5,4,3,2,1,0:T(8,128)(2,1)} %param.10) | copy-start | bytes 3145732
  6.5 45.4 %all-gather.4.cloned.1.call-start = ((), (), s32[]{:S(2)}) async-start(), calls=%async_computation | async-start | bytes 2211840 | tf_op jit(solution)/shard_map/all_gather | solution.py:458
  52.0 56.1 %collective-permute-start.3 = (bf16[4,27,64,128]{3,2,1,0:T(8,128)(2,1)}, bf16[4,27,64,128]{3,2,1,0:T(8,128)(2,1)}, u32[]{:S(2)}, u32[]{:S(2)}) collective-permute-start(bf16[4,27,64,128]{3,2,1,0:T(8,128)(2,1)} %bitcast.37), channel_id=1, source_target_pairs={{0,8},{8,0},{16,24},{24,16},{1,9},{9,1},{17,25},{25,17},{2,10},{10... | collective-permute-start | bytes 5308424 | tf_op jit(solution)/shard_map/ppermute | solution.py:459
  52.0 26.1 %collective-permute-start = (bf16[256,2048]{1,0:T(8,128)(2,1)}, bf16[256,2048]{1,0:T(8,128)(2,1)}, u32[]{:S(2)}, u32[]{:S(2)}) collective-permute-start(bf16[256,2048]{1,0:T(8,128)(2,1)} %bitcast.32), channel_id=1, source_target_pairs={{0,1},{1,0},{2,3},{3,2},{4,5},{5,4},{6,7},{7,6},{8,9},{9,8},{10,11... | collective-permute-start | bytes 3145736 | tf_op jit(solution)/shard_map/ppermute | solution.py:109
  56.2 1.2 copy-start.3
  57.5 6.6 %copy-start.9 = (bf16[27,16,256]{2,1,0:T(8,128)(2,1)S(1)}, bf16[27,16,256]{2,1,0:T(8,128)(2,1)}, u32[]{:S(2)}) copy-start(bf16[27,16,256]{2,1,0:T(8,128)(2,1)} %param.16) | copy-start | bytes 663556
  63.5 2.0 %copy-start.4 = (f32[16,64,256]{2,1,0:T(8,128)}, f32[16,64,256]{2,1,0:T(8,128)S(1)}, u32[]{:S(2)}) copy-start(f32[16,64,256]{2,1,0:T(8,128)S(1)} %get-tuple-element.8.mapped_ref) | copy-start | bytes 3145732
  63.6 14.6 %collective-permute-start.1 = (f32[16,256]{1,0:T(8,128)}, f32[16,256]{1,0:T(8,128)S(1)}, u32[]{:S(2)}, u32[]{:S(2)}) collective-permute-start(f32[16,256]{1,0:T(8,128)} %get-tuple-element.7), channel_id=1, source_target_pairs={{0,1},{1,0},{2,3},{3,2},{4,5},{5,4},{6,7},{7,6},{8,9},{9,8},{10,11... | collective-permute-start | bytes 49160 | tf_op jit(solution)/shard_map/ppermute | solution.py:141
  64.2 1.4 %copy-start.11 = (s32[4]{0:T(128)S(1)}, s32[4]{0:T(128)}, u32[]{:S(2)}) copy-start(s32[4]{0:T(128)} %param.15) | copy-start | bytes 52
  66.3 3.1 %copy-start.8 = (bf16[3,4,4,16,2,256]{5,3,4,2,1,0:T(8,128)(2,1)S(1)}, bf16[3,4,4,16,2,256]{5,3,4,2,1,0:T(8,128)(2,1)}, u32[]{:S(2)}) copy-start(bf16[3,4,4,16,2,256]{5,3,4,2,1,0:T(8,128)(2,1)} %get-tuple-element.10) | copy-start | bytes 2359300
  84.3 4.5 %collective-permute-start.2 = (f32[80,256]{1,0:T(8,128)S(1)}, f32[80,256]{1,0:T(8,128)S(1)}, u32[]{:S(2)}, u32[]{:S(2)}) collective-permute-start(f32[80,256]{1,0:T(8,128)S(1)} %other_queries.1), channel_id=1, source_target_pairs={{0,1},{1,0},{2,3},{3,2},{4,5},{5,4},{6,7},{7,6},{8,9},{9,8},{10,11... | collective-permute-start | bytes 245768 | tf_op jit(solution)/shard_map/ppermute | solution.py:152
  88.9 0.6 copy-start.10
  108.1 1.1 copy-start.5
  109.3 1.1 copy-start.6
  110.4 1.5 %copy-start.7 = (bf16[108,64,128]{2,1,0:T(8,128)(2,1)S(1)}, bf16[108,64,128]{2,1,0:T(8,128)(2,1)}, u32[]{:S(2)}) copy-start(bf16[108,64,128]{2,1,0:T(8,128)(2,1)} %all-gather.4.cloned.1.call-done) | copy-start | bytes 5308420
Sparse Core Ops, SparseCore 0:
  8.9 43.0 all-gather.3

commit v2 on v1

--- a/solution.py
+++ b/solution.py
@@ -24,8 +24,7 @@
 
 def partial_head(head, q, k, v, tiles_ref, counts_ref):
     keys, queries = k.shape[0], q.shape[0]
-    tile_count = tiles_ref.shape[1]
-    keep = tiles_ref.shape[2]
+    tile_count, keep = tiles_ref.shape[:2]
     scores = lax.dot_general(k, q, (((1,), (1,)), ((), ())), preferred_element_type=jnp.float32)
     lane = lax.broadcasted_iota(jnp.int32, (1, queries), 1)
     lane_tile = lax.rem(lax.div(lane, TW), tile_count)
@@ -36,7 +35,7 @@
             live = jnp.bool_(False)
             for slot in range(keep):
                 here = jnp.logical_and(
-                    tiles_ref[head, query_tile, slot] == key_tile, slot < counts_ref[head, query_tile]
+                    tiles_ref[query_tile, slot, head] == key_tile, slot < counts_ref[query_tile, head]
                 )
                 live = jnp.logical_or(live, here)
             row = jnp.where(lane_tile == query_tile, jnp.where(live, 0.0, -1e30), row)
@@ -64,7 +63,7 @@
         out = (out / total).astype(jnp.bfloat16)
         level_ref[pl.ds(head, 1), :] = top + jnp.log2(total)
         mapped_ref[i] = lax.dot_general(
-            w_ref[cols, :], out, (((0,), (0,)), ((), ())), preferred_element_type=jnp.float32
+            w_ref[:, cols], out, (((1,), (0,)), ((), ())), preferred_element_type=jnp.float32
         )
 
 
@@ -84,7 +83,7 @@
         out = (out * jnp.exp2(top - level)).astype(jnp.bfloat16)
         sent_ref[pl.ds(NARROW + head, 1), :] = jnp.exp2(theirs - level)
         mapped = mapped + lax.dot_general(
-            w_ref[cols, :], out, (((0,), (0,)), ((), ())), preferred_element_type=jnp.float32
+            w_ref[:, cols], out, (((1,), (0,)), ((), ())), preferred_element_type=jnp.float32
         )
 
     @pl.when(block == 0)
@@ -96,26 +95,37 @@
         sent_ref[0:NARROW, :] = sent_ref[0:NARROW, :] + mapped
 
 
-def merge_kernel(got_ref, mapped_ref, out_ref):
+def merge_kernel(frames, rows, cols, rank_ref, got_ref, mapped_ref, out_ref, rim_ref):
     total = got_ref[0:NARROW, :]
     for head in range(HEADS):
         total = total + mapped_ref[head] * got_ref[NARROW + head : NARROW + head + 1, :]
-    twice = jnp.concatenate([total, total], axis=0)
-    out_ref[...] = twice.T.astype(jnp.bfloat16)
-
-
-def split_attention(flat_query, flat_key, flat_value, kept_tiles, kept_counts, patch_weight):
-    tokens = flat_query.shape[0]
+    half = total.shape[1] // 2
+    packed = jnp.concatenate([total[:, :half], total[:, half:]], axis=0).T
+    out_ref[...] = packed.astype(jnp.bfloat16)
+    grid = packed.reshape(frames // 2, rows, cols, 2 * NARROW)
+    rim = jnp.where(rank_ref[0] == 0, grid[:, rows - 1], grid[:, 0])
+    rim_ref[...] = rim.reshape(-1, 2 * NARROW).astype(jnp.bfloat16)
+
+
+def split_attention(queries, key_states, value_states, kept_tiles, kept_counts, patch_weight, ready):
+    frames, rows, cols, feature_count = queries.shape[2:]
+    tokens = frames * rows * cols
+    flat_query = queries.reshape(tokens, feature_count)
+    flat_key = key_states.reshape(tokens, feature_count)
+    flat_value = value_states.reshape(tokens, feature_count)
     other_query = lax.ppermute(flat_query, "sp", [(0, 1), (1, 0)])
+    kept_tiles = kept_tiles.transpose(1, 2, 0)
+    kept_counts = kept_counts.T
+    patch_weight = patch_weight.T
     smem = pl.BlockSpec(memory_space=pltpu.SMEM)
     heads = pl.BlockSpec((tokens, HEAD_BLOCK * HD), lambda i: (0, i))
-    weight = pl.BlockSpec((HEAD_BLOCK * HD, NARROW), lambda i: (i, 0))
+    weight = pl.BlockSpec((NARROW, HEAD_BLOCK * HD), lambda i: (0, i))
 
     def whole(*shape):
         return pl.BlockSpec(shape, lambda i: (0,) * len(shape))
 
     params = pltpu.CompilerParams(
-        dimension_semantics=("arbitrary",), vmem_limit_bytes=32 * MIB
+        dimension_semantics=("arbitrary",), vmem_limit_bytes=24 * MIB
     )
     cost = pl.CostEstimate(
         flops=4 * HEADS * tokens * tokens * HD,
@@ -138,6 +148,7 @@
         cost_estimate=cost,
         name="own_keys",
     )(kept_tiles, kept_counts, flat_query, flat_key, flat_value, patch_weight)
+    level, ready = lax.optimization_barrier((level, ready))
     other_level = lax.ppermute(level, "sp", [(0, 1), (1, 0)])
     sent = pl.pallas_call(
         other_kernel,
@@ -150,11 +161,21 @@
         name="other_queries",
     )(kept_tiles, kept_counts, other_query, flat_key, flat_value, patch_weight, other_level)
     got = lax.ppermute(sent, "sp", [(0, 1), (1, 0)])
-    return pl.pallas_call(
-        merge_kernel,
-        out_shape=jax.ShapeDtypeStruct((tokens, 2 * NARROW), jnp.bfloat16),
+    rank = lax.axis_index("sp").astype(jnp.int32).reshape(1)
+    rim_tokens = frames // 2 * cols
+    latent, rim = pl.pallas_call(
+        functools.partial(merge_kernel, frames, rows, cols),
+        grid=(1,),
+        in_specs=[smem, whole(NARROW + HEADS, tokens), whole(HEADS, NARROW, tokens)],
+        out_specs=[whole(tokens // 2, 2 * NARROW), whole(rim_tokens, 2 * NARROW)],
+        out_shape=[
+            jax.ShapeDtypeStruct((tokens // 2, 2 * NARROW), jnp.bfloat16),
+            jax.ShapeDtypeStruct((rim_tokens, 2 * NARROW), jnp.bfloat16),
+        ],
+        compiler_params=params,
         name="merge",
-    )(got, mapped)
+    )(rank, got, mapped)
+    return latent, rim, ready
 
 
 def to_tiles(grid, tile_size):
@@ -251,7 +272,9 @@
     restored = lax.all_to_all(attended, "sp", split_axis=0, concat_axis=1, tiled=True)
     latent = jnp.dot(restored, patch_weight, preferred_element_type=jnp.float32)
     latent = latent.astype(jnp.bfloat16)
-    return jnp.concatenate([latent, latent], axis=1)
+    packed = jnp.concatenate([latent[: tokens // 2], latent[tokens // 2 :]], axis=1)
+    grid = packed.reshape(frame_count // 2, local_rows, token_cols, 2 * NARROW)
+    return packed, grid[:, 0].reshape(-1, 2 * NARROW), grid[:, -1].reshape(-1, 2 * NARROW)
 
 
 def first_weights(first_kernel):
@@ -260,11 +283,11 @@
         [jnp.pad(plain, ((0, 0), (r, 1 - r), (0, 0), (0, 0), (0, 0))) for r in range(2)], axis=4
     )
     matrices = []
-    for c in range(2):
+    for c in (1, 0):
         wide = jnp.pad(both_rows, ((0, 0), (0, 0), (c, 1 - c), (0, 0), (0, 0), (0, 0)))
         wide = wide.reshape(3, 2, 2, 2, 2, LAT, 2, CH).transpose(0, 1, 3, 2, 4, 5, 6, 7)
         matrices.append(wide.reshape(3 * 2 * 2 * NARROW, 2 * CH))
-    return matrices
+    return jnp.stack(matrices)
 
 
 def decode_kernel(
@@ -272,9 +295,10 @@
     rows,
     cols,
     place_ref,
-    latent_ref,
-    left_ref,
-    right_ref,
+    own_refs,
+    above_refs,
+    below_refs,
+    weight_hbm,
     mine_ref,
     theirs_ref,
     out_ref,
@@ -283,30 +307,44 @@
     first_ref,
     act_ref,
     wide_ref,
+    weight_ref,
     kernel_ref,
     sems,
 ):
-    rank = place_ref[1]
-    ranks = place_ref[2]
+    step = place_ref[0]
+    at_first = place_ref[1] == 0
+    at_last = place_ref[1] == place_ref[2] - 1
     half = place_ref[3]
     copies = [
-        pltpu.make_async_copy(mine_ref, kernel_ref.at[half], sems.at[0]),
-        pltpu.make_async_copy(theirs_ref, kernel_ref.at[1 - half], sems.at[1]),
+        pltpu.make_async_copy(weight_hbm, weight_ref, sems.at[0]),
+        pltpu.make_async_copy(mine_ref, kernel_ref.at[half], sems.at[1]),
+        pltpu.make_async_copy(theirs_ref, kernel_ref.at[1 - half], sems.at[2]),
     ]
     for copy in copies:
         copy.start()
-    at_first = rank == 0
-    at_last = rank == ranks - 1
-
+
+    lane = lax.broadcasted_iota(jnp.int32, (1, 1, 1, 2 * NARROW), 3)
+
+    def picked(refs, height):
+        chosen = refs[0][...]
+        for k in range(1, len(refs)):
+            chosen = jnp.where(step == k, refs[k][...], chosen)
+        chosen = chosen.astype(jnp.float32)
+        turned = pltpu.roll(chosen, NARROW, 1)
+        shape = (frames // 2, height, cols, 2 * NARROW)
+        chosen, turned = chosen.reshape(shape), turned.reshape(shape)
+        early = jnp.where(lane < NARROW, chosen, turned)
+        late = jnp.where(lane < NARROW, turned, chosen)
+        return jnp.concatenate([early, late], axis=0)
+
+    token_ref[:, 1 : 1 + rows, 8 : 8 + cols, :] = picked(own_refs, rows)
+    above = picked(above_refs, 1)
+    below = above if below_refs is above_refs else picked(below_refs, 1)
     for f in range(frames):
-        for r in range(rows):
-            token_ref[f, 1 + r, 8 : 8 + cols, :] = latent_ref[0, rank, f, r].astype(jnp.float32)
-        above = latent_ref[0, jnp.maximum(rank - 1, 0), f, rows - 1].astype(jnp.float32)
         edge = pltpu.roll(token_ref[f, 1, 8 : 8 + cols, :], 2 * LAT, 1)
-        token_ref[f, 0, 8 : 8 + cols, :] = jnp.where(at_first, edge, above)
-        below = latent_ref[0, jnp.minimum(rank + 1, ranks - 1), f, 0].astype(jnp.float32)
+        token_ref[f, 0, 8 : 8 + cols, :] = jnp.where(at_first, edge, above[f, 0])
         edge = pltpu.roll(token_ref[f, rows, 8 : 8 + cols, :], 2 * NARROW - 2 * LAT, 1)
-        token_ref[f, rows + 1, 8 : 8 + cols, :] = jnp.where(at_last, edge, below)
+        token_ref[f, rows + 1, 8 : 8 + cols, :] = jnp.where(at_last, edge, below[f, 0])
     for f in range(frames):
         for r in range(rows + 2):
             start = token_ref[f, r, 8:16, :]
@@ -314,7 +352,6 @@
             end = token_ref[f, r, cols : 8 + cols, :]
             token_ref[f, r, 8 + cols : 9 + cols, :] = pltpu.roll(end, 2 * NARROW - LAT, 1)[7:8]
 
-    lane = lax.broadcasted_iota(jnp.int32, (1, 1, cols, 2 * NARROW), 3)
     for side in range(2):
         pair = jnp.where(
             lane < NARROW,
@@ -325,8 +362,9 @@
         pair_ref[side, 0] = pair[0]
         pair_ref[side, 1] = pair[0]
 
+    copies[0].wait()
     gaps = rows + 1
-    for side, weight_ref in ((0, left_ref), (1, right_ref)):
+    for side in range(2):
         columns = jnp.concatenate(
             [
                 pair_ref[side, dt : dt + frames, rr : rr + gaps].reshape(frames * gaps * cols, 2 * NARROW)
@@ -335,7 +373,7 @@
             ],
             axis=1,
         )
-        first = jnp.dot(columns, weight_ref[...], preferred_element_type=jnp.float32) * VAE_SCALE
+        first = jnp.dot(columns, weight_ref[side], preferred_element_type=jnp.float32) * VAE_SCALE
         first = first.astype(jnp.bfloat16).astype(jnp.float32)
         act = first / (1.0 + jnp.exp(-first))
         first = first.reshape(frames, gaps, cols, 2 * CH)
@@ -367,7 +405,7 @@
             wide_ref[0, :, :, lanes] = shifted[0]
             wide_ref[1, :, :, lanes] = shifted[0]
 
-    for copy in copies:
+    for copy in copies[1:]:
         copy.wait()
     cells = frames * height * width
     total = None
@@ -393,23 +431,27 @@
         out_ref[:, :, :, lanes] = (total[:, :, :, lanes] + residual).astype(jnp.bfloat16)
 
 
-def decode(place, gathered, left, right, mine, theirs):
-    _, ranks, frames, rows, cols, _ = gathered.shape
+def decode(frames, rows, cols, place, own, above, below, weights, mine, theirs):
     height, width = 2 * rows, 2 * cols
+    steps = len(own)
+    rims = [above] if below is above else [above, below]
+    small = own + [part for rim in rims for part in rim]
 
     def whole(shape):
         return pl.BlockSpec(shape, lambda i, place: (0,) * len(shape))
+
+    def body(place_ref, *refs):
+        own_refs, above_refs = refs[:steps], refs[steps : 2 * steps]
+        below_refs = above_refs if len(rims) == 1 else refs[2 * steps : 3 * steps]
+        decode_kernel(
+            frames, rows, cols, place_ref, own_refs, above_refs, below_refs, *refs[len(small) :]
+        )
 
     grid_spec = pltpu.PrefetchScalarGridSpec(
         num_scalar_prefetch=1,
         grid=(1,),
-        in_specs=[
-            pl.BlockSpec((1,) + gathered.shape[1:], lambda i, place: (place[0], 0, 0, 0, 0, 0)),
-            whole(left.shape),
-            whole(right.shape),
-            pl.BlockSpec(memory_space=pl.ANY),
-            pl.BlockSpec(memory_space=pl.ANY),
-        ],
+        in_specs=[whole(part.shape) for part in small]
+        + [pl.BlockSpec(memory_space=space) for space in (pl.ANY, pltpu.HBM, pl.ANY)],
         out_specs=whole((frames, height, width, CH)),
         scratch_shapes=[
             pltpu.VMEM((frames, rows + 2, cols + 16, 2 * NARROW), jnp.float32),
@@ -417,22 +459,23 @@
             pltpu.VMEM((CH // 128, frames, height + 2, width + 16, 128), jnp.float32),
             pltpu.VMEM((CH // 128, frames, height + 2, width + 16, 128), jnp.float32),
             pltpu.VMEM((frames + 2, height + 2, width, 3 * CH), jnp.bfloat16),
+            pltpu.VMEM(weights.shape, jnp.bfloat16),
             pltpu.VMEM((2,) + mine.shape, jnp.bfloat16),
-            pltpu.SemaphoreType.DMA((2,)),
+            pltpu.SemaphoreType.DMA((3,)),
         ],
     )
     return pl.pallas_call(
-        functools.partial(decode_kernel, frames, rows, cols),
+        body,
         grid_spec=grid_spec,
         out_shape=jax.ShapeDtypeStruct((frames, height, width, CH), jnp.bfloat16),
-        compiler_params=pltpu.CompilerParams(vmem_limit_bytes=48 * MIB),
+        compiler_params=pltpu.CompilerParams(vmem_limit_bytes=32 * MIB),
         cost_estimate=pl.CostEstimate(
             flops=2 * frames * height * width * 27 * CH * CH,
             bytes_accessed=27 * CH * CH * 2 + frames * height * width * CH * 2,
             transcendentals=frames * height * width * CH,
         ),
         name="decode_block",
-    )(place, gathered, left, right, mine, theirs)
+    )(place, *small, weights, mine, theirs)
 
 
 def local(
@@ -446,8 +489,7 @@
     first_kernel,
     second_kernel,
 ):
-    frames, rows, cols, feature_count = queries.shape[2:]
-    tokens = frames * rows * cols
+    frames, rows, cols = queries.shape[2:5]
     sp_count = lax.axis_size("sp")
     sp_rank = lax.axis_index("sp")
     segment_count = lax.axis_size("segment")
@@ -456,29 +498,39 @@
     half = lax.rem(segment_rank, 2)
     share = lax.dynamic_slice_in_dim(second_kernel, half * (CH // 2), CH // 2, 2)
     mine = lax.all_gather(share, "grp", axis=0, tiled=False)
-    theirs = lax.ppermute(mine, "segment", [(i, i ^ 1) for i in range(segment_count)])
-    left, right = first_weights(first_kernel)[::-1]
-
-    if sp_count == 2 and rows * sp_count == TH and frames == TT:
-        latent = split_attention(
-            queries.reshape(tokens, feature_count),
-            key_states.reshape(tokens, feature_count),
-            value_states.reshape(tokens, feature_count),
-            kept_tiles,
-            kept_counts,
-            patch_weight,
-        )
-    else:
-        latent = exchanged_attention(
-            queries, key_states, value_states, kept_tiles, kept_counts, patch_weight
-        )
-
-    gathered = lax.all_gather(latent, ("segment", "sp"), axis=0, tiled=False)
-    gathered = gathered.reshape(segment_count, sp_count, frames, rows, cols, 2 * NARROW)
+
+    weights = first_weights(first_kernel)
     picks = (decode_slot == segment_rank).astype(jnp.int32)
     source = jnp.sum(jnp.arange(segment_count, dtype=jnp.int32) * picks)
-    place = jnp.stack([source, sp_rank, jnp.int32(sp_count), half]).astype(jnp.int32)
-    return decode(place, gathered, left, right, mine, theirs)[None, None]
+    step = lax.rem(segment_rank - source + segment_count, segment_count)
+    place = jnp.stack([step, sp_rank, jnp.int32(sp_count), half]).astype(jnp.int32)
+
+    arguments = (queries, key_states, value_states, kept_tiles, kept_counts, patch_weight)
+    if sp_count == 2 and rows * sp_count == TH and frames == TT:
+        latent, rim, (weights, place) = split_attention(*arguments, (weights, place))
+        rims = [(rim, [(0, 1), (1, 0)])]
+    else:
+        latent, top, bottom = exchanged_attention(*arguments)
+        rims = [
+            (bottom, [(i, i + 1) for i in range(sp_count - 1)]),
+            (top, [(i + 1, i) for i in range(sp_count - 1)]),
+        ]
+    mine, _ = lax.optimization_barrier((mine, latent))
+    theirs = lax.ppermute(mine, "segment", [(i, i ^ 1) for i in range(segment_count)])
+
+    def along_segment(part, step, moves):
+        pairs = [
+            (i * sp_count + a, (i + step) % segment_count * sp_count + b)
+            for i in range(segment_count)
+            for a, b in moves
+        ]
+        return lax.ppermute(part, ("segment", "sp"), pairs)
+
+    stay = [(i, i) for i in range(sp_count)]
+    own = [latent] + [along_segment(latent, step, stay) for step in range(1, segment_count)]
+    beside = [[along_segment(rim, step, moves) for step in range(segment_count)] for rim, moves in rims]
+    decoded = decode(frames, rows, cols, place, own, beside[0], beside[-1], weights, mine, theirs)
+    return decoded[None, None]
 
 
 def solution(mesh):

time: 128 us -> 85.9 us (0.67)
  waiting for transfers between devices: 52.5 us -> 22.4 us
  blocking collectives: 16.6 us -> 0 us
  starting transfers between devices: 3.57 us -> 10.1 us
  Pallas kernels: 22.2 us -> 19.5 us
    all_gather x1, waiting for transfers between devices: 43.4 us -> 5.1 us  [local(): mine = lax.all_gather(share, 'grp', axis=0, tiled=False)]
    all_gather x1 -> x0, blocking collectives: 16.6 us -> none  [local(): gathered = lax.all_gather(latent, ('segment', 'sp'), axis=0, tiled=False)]
    ppermute x0 -> x7, waiting for transfers between devices: none -> 10.1 us  [along_segment(): return lax.ppermute(part, ('segment', 'sp'), pairs)]
    unnamed x29 -> x22, local copies, waits for them, and re-layouts: 11.6 us -> 5.29 us
    ppermute x0 -> x7, starting transfers between devices: none -> 5.98 us  [along_segment(): return lax.ppermute(part, ('segment', 'sp'), pairs)]
    another operation x0 -> x2, local copies, waits for them, and re-layouts: none -> 4.52 us  [first_weights(): return jnp.stack(matrices)]
    ppermute x1, waiting for transfers between devices: 6.87 us -> 3.74 us  [split_attention(): other_level = lax.ppermute(level, 'sp', [(0, 1), (1, 0)])]
    pallas_call x2, Pallas kernels: 9.86 us -> 7.84 us  [the longest x1 7.69 us: decode(): pl.pallas_call(body, grid_spec=grid_spec, out_shape=jax.ShapeDtypeStruct(...]
  transfers between devices with their start and end apart: 5 -> 12, of which waited for: 3 -> 7; matrix products, arithmetic and copies ran while one was open for 8% -> 15% of each run, Pallas kernels for 11% -> 14%
where the time goes in v2:
time: 85.9 us; the launch traced here: 85.6 us
  waiting for transfers between devices  22.4 us (26%)
  Pallas kernels  19.5 us (23%)
  local copies, waits for them, and re-layouts  16.6 us (19%)
  between operations  14.2 us (17%)
  starting transfers between devices  10.1 us (12%)
  other arithmetic  2.78 us (3%)
    ppermute x7, waiting for transfers between devices, along_segment(): return lax.ppermute(part, ('segment', 'sp'), pairs)  10.1 us
    pallas_call x1, Pallas kernels, decode(): pl.pallas_call(body, grid_spec=grid_spec, out_shape=jax.ShapeDtypeStruct(...  7.69 us
    pallas_call x1, Pallas kernels, split_attention(): pl.pallas_call(other_kernel, grid=(HEADS // HEAD_BLOCK,), in_specs=[smem,...  6.19 us
    ppermute x7, starting transfers between devices, along_segment(): return lax.ppermute(part, ('segment', 'sp'), pairs)  5.98 us
    pallas_call x1, Pallas kernels, split_attention(): pl.pallas_call(own_kernel, grid=(HEADS // HEAD_BLOCK,), in_specs=[smem, s...  5.46 us
    unnamed x22, local copies, waits for them, and re-layouts  5.29 us
    all_gather x1, waiting for transfers between devices, local(): mine = lax.all_gather(share, 'grp', axis=0, tiled=False)  5.1 us
    another operation x2, local copies, waits for them, and re-layouts, first_weights(): return jnp.stack(matrices)  4.52 us
  transfers between devices with their start and end apart: 12, of which 7 were waited for; matrix products, arithmetic and copies ran while one was open for 15% of the time, Pallas kernels for 14%

profile of v2, /device:TPU:0, one launch (start us, length us, event | category | flops | bytes accessed | tf_op | source)
XLA Modules:
  0.0 85.6 jit_solution(15509296842781942779)
XLA Ops:
  6.5 0.0 copy-start
  6.5 1.2 %copy-done = bf16[27,64,256]{2,1,0:T(8,128)(2,1)S(1)} copy-done((bf16[27,64,256]{2,1,0:T(8,128)(2,1)S(1)}, bf16[27,64,256]{2,1,0:T(8,128)(2,1)}, u32[]{:S(2)}) %copy-start) | copy-done | bytes 884760
  7.7 0.8 constant_dynamic-slice_fusion
  8.6 0.0 all-gather.3.cloned.1.call-update
  8.6 3.0 %collective-permute-start = (bf16[256,2048]{1,0:T(8,128)(2,1)}, bf16[256,2048]{1,0:T(8,128)(2,1)}, u32[]{:S(2)}, u32[]{:S(2)}) collective-permute-start(bf16[256,2048]{1,0:T(8,128)(2,1)} %bitcast.28), channel_id=1, source_target_pairs={{0,1},{1,0},{2,3},{3,2},{4,5},{5,4},{6,7},{7,6},{8,9},{9,8},{10,11... | collective-permute-start | bytes 3145736 | tf_op jit(solution)/shard_map/ppermute | solution.py:116
  11.6 1.4 %fusion = s32[]{:T(128)} fusion(s32[4]{0:T(128)} %param.15, s32[]{:T(128)S(6)} %axis_index.27), kind=kLoop, calls=%fused_computation.5 | loop fusion | flops 11 | bytes 24 | tf_op jit(solution)/shard_map/reduce_sum | solution.py:504
  13.6 1.1 %pad_bitcast_fusion.1 = (bf16[3,4,3,16,1,256]{5,3,4,2,1,0:T(8,128)(2,1)S(1)}, bf16[3,4,3,16,1,256]{5,3,4,2,1,0:T(8,128)(2,1)S(1)}) fusion(bf16[3,3,3,16,256]{4,3,2,1,0:T(8,128)(2,1)} %bitcast.40), kind=kLoop, calls=%fused_computation.3 | loop fusion | bytes 811008 | tf_op jit(solution)/shard_map/stack | solution.py:282
  14.7 0.1 pad_maximum_fusion.1
  14.8 1.0 %fusion.1 = (bf16[3,4,4,16,2,256]{5,3,4,2,1,0:T(8,128)(2,1)S(1)}, bf16[3,4,4,16,2,256]{5,3,4,2,1,0:T(8,128)(2,1)}) fusion(bf16[3,4,3,16,2,256]{5,3,4,2,1,0:T(8,128)(2,1)S(1)} %pad_maximum_fusion.1), kind=kLoop, calls=%fused_computation.8 | loop fusion | bytes 2162688 | tf_op jit(solution)/shard_map/jit(_pad)/pad | solution.py:287
  15.8 0.8 copy.14
  16.6 1.4 %stack_reshape.6 = bf16[1,768,512]{2,1,0:T(8,128)(2,1)} reshape(bf16[3,2,2,2,2,16,2,256]{7,6,5,4,3,2,1,0:T(2,128)(2,1)S(1)} %copy.14) | data formatting | bytes 1572864 | tf_op jit(solution)/shard_map/stack;reshape | solution.py:290
  18.0 0.0 copy-start.7
  18.0 3.0 %copy.15 = bf16[3,2,2,2,2,16,2,256]{7,6,5,4,3,2,1,0:T(2,128)(2,1)} copy(bf16[3,2,2,2,2,16,2,256]{7,5,6,4,2,3,1,0:T(8,128)(2,1)} %bitcast.38) | data formatting | bytes 1572864 | tf_op jit(solution)/shard_map/transpose | solution.py:288
  21.1 3.1 %stack_reshape.7 = bf16[1,768,512]{2,1,0:T(8,128)(2,1)} reshape(bf16[3,2,2,2,2,16,2,256]{7,6,5,4,3,2,1,0:T(2,128)(2,1)} %copy.15) | data formatting | bytes 1572864 | tf_op jit(solution)/shard_map/stack;reshape | solution.py:290
  24.2 0.0 copy-done.6
  24.2 0.0 copy-done.7
  24.2 0.0 copy-start.4
  24.2 1.2 %copy-done.4 = bf16[1,1,4,4,16,2048]{5,4,3,2,1,0:T(8,128)(2,1)S(1)} copy-done((bf16[1,1,4,4,16,2048]{5,4,3,2,1,0:T(8,128)(2,1)S(1)}, bf16[1,1,4,4,16,2048]{5,4,3,2,1,0:T(8,128)(2,1)}, u32[]{:S(2)}) %copy-start.4) | copy-done | bytes 1048600
  25.4 5.5 %own_keys.1 = (f32[16,256]{1,0:T(8,128)S(1)}, f32[16,64,256]{2,1,0:T(8,128)S(1)}) custom-call(s32[2,2,16]{2,1,0:T(2,128)S(1)} %bitcast.32, s32[2,16]{1,0:T(2,128)S(1)} %bitcast.34, bf16[256,2048]{1,0:T(8,128)(2,1)S(1)} %bitcast.29, bf16[256,2048]{1,0:T(8,128)(2,1)S(1)} %bitcast.24, bf16[256,2048]{1,0:T(8,128)(2,1)S(1)} %bitcast.26, bf16[64,2048]{1,0:T(8,128)(2,1)S(1)} %bitcast.30), custom_call_target="tpu_custom_call" | custom-call | flops 536870912 | bytes 3145728 | tf_op jit(solution)/shard_map/own_keys/pallas_call | solution.py:135
  30.9 0.1 pad_add_fusion.place_ref
  31.0 1.3 %pad_maximum_fusion.refs_8_ = bf16[2,768,512]{2,1,0:T(8,128)(2,1)} fusion(bf16[1,768,512]{2,1,0:T(8,128)(2,1)S(1)} %copy-done.10, bf16[1,768,512]{2,1,0:T(8,128)(2,1)S(1)} %copy-done.9), kind=kLoop, calls=%fused_computation | loop fusion | flops 786432 | bytes 3145728 | tf_op jit(solution)/shard_map/stack | solution.py:290
  32.3 0.0 collective-permute-start.1
  32.3 3.7 %collective-permute-done.1.level_ref = f32[16,256]{1,0:T(8,128)S(1)} collective-permute-done((f32[16,256]{1,0:T(8,128)S(1)}, f32[16,256]{1,0:T(8,128)S(1)}, u32[]{:S(2)}, u32[]{:S(2)}) %collective-permute-start.1) | collective-permute-done | bytes 16416 | tf_op jit(solution)/shard_map/ppermute | solution.py:152
  36.0 0.0 collective-permute-done.q_ref
  36.0 6.2 %other_queries.1 = f32[80,256]{1,0:T(8,128)S(1)} custom-call(s32[2,2,16]{2,1,0:T(2,128)S(1)} %bitcast.33, s32[2,16]{1,0:T(2,128)S(1)} %bitcast.35, bf16[256,2048]{1,0:T(8,128)(2,1)} %collective-permute-done.q_ref, bf16[256,2048]{1,0:T(8,128)(2,1)S(1)} %bitcast.25, bf16[256,2048]{1,0:T(8,128)(2,1)S(1)} %bitcast.27, bf16[64,2048]{1,0:T(8,128)(2,1)S(1)} %bitcast.31, ...), custom_call_target="tpu_custom_call" | custom-call | flops 536870912 | bytes 3145728 | tf_op jit(solution)/shard_map/other_queries/pallas_call | solution.py:153
  42.2 1.1 %collective-permute-start.2 = (f32[80,256]{1,0:T(8,128)S(1)}, f32[80,256]{1,0:T(8,128)S(1)}, u32[]{:S(2)}, u32[]{:S(2)}) collective-permute-start(f32[80,256]{1,0:T(8,128)S(1)} %other_queries.1), channel_id=1, source_target_pairs={{0,1},{1,0},{2,3},{3,2},{4,5},{5,4},{6,7},{7,6},{8,9},{9,8},{10,11... | collective-permute-start | bytes 245768 | tf_op jit(solution)/shard_map/ppermute | solution.py:163
  43.3 3.4 %collective-permute-done.2.got_ref = f32[80,256]{1,0:T(8,128)S(1)} collective-permute-done((f32[80,256]{1,0:T(8,128)S(1)}, f32[80,256]{1,0:T(8,128)S(1)}, u32[]{:S(2)}, u32[]{:S(2)}) %collective-permute-start.2) | collective-permute-done | bytes 81952 | tf_op jit(solution)/shard_map/ppermute | solution.py:163
  46.7 0.2 merge.1
  46.9 5.1 %all-gather.3.cloned.1.call-done = bf16[108,64,128]{2,1,0:T(8,128)(2,1)} async-done(((bf16[27,64,128]{2,1,0:T(8,128)(2,1)}), bf16[108,64,128]{2,1,0:T(8,128)(2,1)}) %all-gather.3.cloned.1.call-update) | async-done | bytes 1769488 | tf_op jit(solution)/shard_map/all_gather | solution.py:500
  52.0 0.0 collective-permute-start.10
  52.0 2.5 %collective-permute-start.9 = (bf16[32,128]{1,0:T(8,128)(2,1)S(1)}, bf16[32,128]{1,0:T(8,128)(2,1)S(1)}, u32[]{:S(2)}, u32[]{:S(2)}) collective-permute-start(bf16[32,128]{1,0:T(8,128)(2,1)S(1)} %get-tuple-element.18), channel_id=1, source_target_pairs={{0,25},{1,24},{8,1},{9,0},{16,9},{17,8},{24,17},{25,16},{2,27},{3,... | collective-permute-start | bytes 24584 | tf_op jit(solution)/shard_map/ppermute | solution.py:527
  54.5 0.2 collective-permute-start.5
  54.6 0.6 collective-permute-start.4
  55.2 0.1 collective-permute-start.3
  55.3 0.6 collective-permute-done.9.refs_7_
  55.8 1.6 %collective-permute-start.8 = (bf16[32,128]{1,0:T(8,128)(2,1)S(1)}, bf16[32,128]{1,0:T(8,128)(2,1)S(1)}, u32[]{:S(2)}, u32[]{:S(2)}) collective-permute-start(bf16[32,128]{1,0:T(8,128)(2,1)S(1)} %get-tuple-element.18), channel_id=1, source_target_pairs={{0,17},{1,16},{8,25},{9,24},{16,1},{17,0},{24,9},{25,8},{2,19},{3,... | collective-permute-start | bytes 24584 | tf_op jit(solution)/shard_map/ppermute | solution.py:527
  57.4 3.0 %collective-permute-done.8.refs_6_ = bf16[32,128]{1,0:T(8,128)(2,1)S(1)} collective-permute-done((bf16[32,128]{1,0:T(8,128)(2,1)S(1)}, bf16[32,128]{1,0:T(8,128)(2,1)S(1)}, u32[]{:S(2)}, u32[]{:S(2)}) %collective-permute-start.8) | collective-permute-done | bytes 8224 | tf_op jit(solution)/shard_map/ppermute | solution.py:527
  60.5 0.5 collective-permute-start.7
  60.9 3.5 %collective-permute-done.7.refs_5_ = bf16[32,128]{1,0:T(8,128)(2,1)S(1)} collective-permute-done((bf16[32,128]{1,0:T(8,128)(2,1)S(1)}, bf16[32,128]{1,0:T(8,128)(2,1)S(1)}, u32[]{:S(2)}, u32[]{:S(2)}) %collective-permute-start.7) | collective-permute-done | bytes 8224 | tf_op jit(solution)/shard_map/ppermute | solution.py:527
  64.4 0.6 collective-permute-start.6
  65.1 3.0 %collective-permute-done.6.refs_4_ = bf16[32,128]{1,0:T(8,128)(2,1)S(1)} collective-permute-done((bf16[32,128]{1,0:T(8,128)(2,1)S(1)}, bf16[32,128]{1,0:T(8,128)(2,1)S(1)}, u32[]{:S(2)}, u32[]{:S(2)}) %collective-permute-start.6) | collective-permute-done | bytes 8224 | tf_op jit(solution)/shard_map/ppermute | solution.py:527
  68.1 0.0 collective-permute-done.5.refs_3_
  68.1 0.0 collective-permute-done.4.refs_2_
  68.1 0.0 collective-permute-done.3.refs_1_
  68.1 0.0 collective-permute-done.10.refs_10_
  68.1 1.4 %copy-done.3 = bf16[2,768,512]{2,1,0:T(8,128)(2,1)S(1)} copy-done((bf16[2,768,512]{2,1,0:T(8,128)(2,1)S(1)}, bf16[2,768,512]{2,1,0:T(8,128)(2,1)}, u32[]{:S(2)}) %copy-start.3) | copy-done | bytes 1572888
  69.5 1.5 %copy-done.8 = bf16[108,64,128]{2,1,0:T(8,128)(2,1)S(1)} copy-done((bf16[108,64,128]{2,1,0:T(8,128)(2,1)S(1)}, bf16[108,64,128]{2,1,0:T(8,128)(2,1)}, u32[]{:S(2)}) %copy-start.8) | copy-done | bytes 1769496
  71.0 7.7 %decode_block.1 = bf16[4,8,32,256]{3,2,1,0:T(8,128)(2,1)} custom-call(s32[4]{0:T(128)S(1)} %pad_add_fusion.place_ref, bf16[128,128]{1,0:T(8,128)(2,1)S(1)} %get-tuple-element.17.refs_0_, bf16[128,128]{1,0:T(8,128)(2,1)S(1)} %collective-permute-done.3.refs_1_, bf16[128,128]{1,0:T(8,128)(2,1)S(1)} %collective-permute-done.4.refs_2_, ...), custom_call_target="tpu_custom_call" | custom-call | flops 3623878656 | bytes 4063232 | tf_op jit(solution)/shard_map/decode_block/pallas_call | solution.py:467
  (14 shorter events, 0.0 us)
Async XLA Ops:
  6.5 1.2 %copy-start = (bf16[27,64,256]{2,1,0:T(8,128)(2,1)S(1)}, bf16[27,64,256]{2,1,0:T(8,128)(2,1)}, u32[]{:S(2)}) copy-start(bf16[27,64,256]{2,1,0:T(8,128)(2,1)} %param.17) | copy-start | bytes 2654212
  6.5 45.4 %all-gather.3.cloned.1.call-start = ((), (), s32[]{:S(2)}) async-start(), calls=%async_computation | async-start | bytes 2211840 | tf_op jit(solution)/shard_map/all_gather | solution.py:500
  8.6 27.4 %collective-permute-start = (bf16[256,2048]{1,0:T(8,128)(2,1)}, bf16[256,2048]{1,0:T(8,128)(2,1)}, u32[]{:S(2)}, u32[]{:S(2)}) collective-permute-start(bf16[256,2048]{1,0:T(8,128)(2,1)} %bitcast.28), channel_id=1, source_target_pairs={{0,1},{1,0},{2,3},{3,2},{4,5},{5,4},{6,7},{7,6},{8,9},{9,8},{10,11... | collective-permute-start | bytes 3145736 | tf_op jit(solution)/shard_map/ppermute | solution.py:116
  18.0 6.2 %copy-start.1 = (bf16[1,1,4,4,16,2048]{5,4,3,2,1,0:T(8,128)(2,1)S(1)}, bf16[1,1,4,4,16,2048]{5,4,3,2,1,0:T(8,128)(2,1)}, u32[]{:S(2)}) copy-start(bf16[1,1,4,4,16,2048]{5,4,3,2,1,0:T(8,128)(2,1)} %param.10) | copy-start | bytes 3145732
  18.0 6.2 %copy-start.2 = (bf16[1,1,4,4,16,2048]{5,4,3,2,1,0:T(8,128)(2,1)S(1)}, bf16[1,1,4,4,16,2048]{5,4,3,2,1,0:T(8,128)(2,1)}, u32[]{:S(2)}) copy-start(bf16[1,1,4,4,16,2048]{5,4,3,2,1,0:T(8,128)(2,1)} %param.11) | copy-start | bytes 3145732
  18.0 6.2 %copy-start.5 = (bf16[2048,64]{0,1:T(8,128)(2,1)S(1)}, bf16[2048,64]{0,1:T(8,128)(2,1)}, u32[]{:S(2)}) copy-start(bf16[2048,64]{0,1:T(8,128)(2,1)} %param.14) | copy-start | bytes 786436
  18.0 6.2 %copy-start.6 = (s32[16,2,2]{0,2,1:T(2,128)S(1)}, s32[16,2,2]{0,2,1:T(2,128)}, u32[]{:S(2)}) copy-start(s32[16,2,2]{0,2,1:T(2,128)} %param.12) | copy-start | bytes 772
  18.0 6.2 %copy-start.7 = (s32[16,2]{0,1:T(2,128)S(1)}, s32[16,2]{0,1:T(2,128)}, u32[]{:S(2)}) copy-start(s32[16,2]{0,1:T(2,128)} %param.13) | copy-start | bytes 388
  24.2 1.2 %copy-start.4 = (bf16[1,1,4,4,16,2048]{5,4,3,2,1,0:T(8,128)(2,1)S(1)}, bf16[1,1,4,4,16,2048]{5,4,3,2,1,0:T(8,128)(2,1)}, u32[]{:S(2)}) copy-start(bf16[1,1,4,4,16,2048]{5,4,3,2,1,0:T(8,128)(2,1)} %param.9) | copy-start | bytes 3145732
  25.4 5.6 %copy-start.9 = (bf16[1,768,512]{2,1,0:T(8,128)(2,1)S(1)}, bf16[1,768,512]{2,1,0:T(8,128)(2,1)}, u32[]{:S(2)}) copy-start(bf16[1,768,512]{2,1,0:T(8,128)(2,1)} %stack_reshape.6) | copy-start | bytes 2359300
  25.4 5.6 %copy-start.10 = (bf16[1,768,512]{2,1,0:T(8,128)(2,1)S(1)}, bf16[1,768,512]{2,1,0:T(8,128)(2,1)}, u32[]{:S(2)}) copy-start(bf16[1,768,512]{2,1,0:T(8,128)(2,1)} %stack_reshape.7) | copy-start | bytes 2359300
  32.3 3.7 %collective-permute-start.1 = (f32[16,256]{1,0:T(8,128)S(1)}, f32[16,256]{1,0:T(8,128)S(1)}, u32[]{:S(2)}, u32[]{:S(2)}) collective-permute-start(f32[16,256]{1,0:T(8,128)S(1)} %get-tuple-element.15), channel_id=1, source_target_pairs={{0,1},{1,0},{2,3},{3,2},{4,5},{5,4},{6,7},{7,6},{8,9},{9,8},{10,11... | collective-permute-start | bytes 49160 | tf_op jit(solution)/shard_map/ppermute | solution.py:152
  42.2 4.5 %collective-permute-start.2 = (f32[80,256]{1,0:T(8,128)S(1)}, f32[80,256]{1,0:T(8,128)S(1)}, u32[]{:S(2)}, u32[]{:S(2)}) collective-permute-start(f32[80,256]{1,0:T(8,128)S(1)} %other_queries.1), channel_id=1, source_target_pairs={{0,1},{1,0},{2,3},{3,2},{4,5},{5,4},{6,7},{7,6},{8,9},{9,8},{10,11... | collective-permute-start | bytes 245768 | tf_op jit(solution)/shard_map/ppermute | solution.py:163
  52.0 16.1 %collective-permute-start.10 = (bf16[4,27,64,128]{3,2,1,0:T(8,128)(2,1)}, bf16[4,27,64,128]{3,2,1,0:T(8,128)(2,1)S(1)}, u32[]{:S(2)}, u32[]{:S(2)}) collective-permute-start(bf16[4,27,64,128]{3,2,1,0:T(8,128)(2,1)} %bitcast.36), channel_id=1, source_target_pairs={{0,8},{8,0},{16,24},{24,16},{1,9},{9,1},{17,25},{25,17},{2,10},{10... | collective-permute-start | bytes 5308424 | tf_op jit(solution)/shard_map/ppermute | solution.py:519
  52.0 3.9 %collective-permute-start.9 = (bf16[32,128]{1,0:T(8,128)(2,1)S(1)}, bf16[32,128]{1,0:T(8,128)(2,1)S(1)}, u32[]{:S(2)}, u32[]{:S(2)}) collective-permute-start(bf16[32,128]{1,0:T(8,128)(2,1)S(1)} %get-tuple-element.18), channel_id=1, source_target_pairs={{0,25},{1,24},{8,1},{9,0},{16,9},{17,8},{24,17},{25,16},{2,27},{3,... | collective-permute-start | bytes 24584 | tf_op jit(solution)/shard_map/ppermute | solution.py:527
  54.5 13.6 %collective-permute-start.5 = (bf16[128,128]{1,0:T(8,128)(2,1)S(1)}, bf16[128,128]{1,0:T(8,128)(2,1)S(1)}, u32[]{:S(2)}, u32[]{:S(2)}) collective-permute-start(bf16[128,128]{1,0:T(8,128)(2,1)S(1)} %get-tuple-element.17.refs_0_), channel_id=1, source_target_pairs={{0,24},{1,25},{8,0},{9,1},{16,8},{17,9},{24,16},{25,17},{2,26},{3,... | collective-permute-start | bytes 98312 | tf_op jit(solution)/shard_map/ppermute | solution.py:527
  54.6 13.4 %collective-permute-start.4 = (bf16[128,128]{1,0:T(8,128)(2,1)S(1)}, bf16[128,128]{1,0:T(8,128)(2,1)S(1)}, u32[]{:S(2)}, u32[]{:S(2)}) collective-permute-start(bf16[128,128]{1,0:T(8,128)(2,1)S(1)} %get-tuple-element.17.refs_0_), channel_id=1, source_target_pairs={{0,16},{1,17},{8,24},{9,25},{16,0},{17,1},{24,8},{25,9},{2,18},{3,... | collective-permute-start | bytes 98312 | tf_op jit(solution)/shard_map/ppermute | solution.py:527
  55.2 12.9 %collective-permute-start.3 = (bf16[128,128]{1,0:T(8,128)(2,1)S(1)}, bf16[128,128]{1,0:T(8,128)(2,1)S(1)}, u32[]{:S(2)}, u32[]{:S(2)}) collective-permute-start(bf16[128,128]{1,0:T(8,128)(2,1)S(1)} %get-tuple-element.17.refs_0_), channel_id=1, source_target_pairs={{0,8},{1,9},{8,16},{9,17},{16,24},{17,25},{24,0},{25,1},{2,10},{3,... | collective-permute-start | bytes 98312 | tf_op jit(solution)/shard_map/ppermute | solution.py:527
  55.8 4.6 %collective-permute-start.8 = (bf16[32,128]{1,0:T(8,128)(2,1)S(1)}, bf16[32,128]{1,0:T(8,128)(2,1)S(1)}, u32[]{:S(2)}, u32[]{:S(2)}) collective-permute-start(bf16[32,128]{1,0:T(8,128)(2,1)S(1)} %get-tuple-element.18), channel_id=1, source_target_pairs={{0,17},{1,16},{8,25},{9,24},{16,1},{17,0},{24,9},{25,8},{2,19},{3,... | collective-permute-start | bytes 24584 | tf_op jit(solution)/shard_map/ppermute | solution.py:527
  60.5 4.0 %collective-permute-start.7 = (bf16[32,128]{1,0:T(8,128)(2,1)S(1)}, bf16[32,128]{1,0:T(8,128)(2,1)S(1)}, u32[]{:S(2)}, u32[]{:S(2)}) collective-permute-start(bf16[32,128]{1,0:T(8,128)(2,1)S(1)} %get-tuple-element.18), channel_id=1, source_target_pairs={{0,9},{1,8},{8,17},{9,16},{16,25},{17,24},{24,1},{25,0},{2,11},{3,... | collective-permute-start | bytes 24584 | tf_op jit(solution)/shard_map/ppermute | solution.py:527
  64.4 3.7 %collective-permute-start.6 = (bf16[32,128]{1,0:T(8,128)(2,1)S(1)}, bf16[32,128]{1,0:T(8,128)(2,1)S(1)}, u32[]{:S(2)}, u32[]{:S(2)}) collective-permute-start(bf16[32,128]{1,0:T(8,128)(2,1)S(1)} %get-tuple-element.18), channel_id=1, source_target_pairs={{0,1},{1,0},{8,9},{9,8},{16,17},{17,16},{24,25},{25,24},{2,3},{3,2... | collective-permute-start | bytes 24584 | tf_op jit(solution)/shard_map/ppermute | solution.py:527
  68.1 1.4 %copy-start.3 = (bf16[2,768,512]{2,1,0:T(8,128)(2,1)S(1)}, bf16[2,768,512]{2,1,0:T(8,128)(2,1)}, u32[]{:S(2)}) copy-start(bf16[2,768,512]{2,1,0:T(8,128)(2,1)} %pad_maximum_fusion.refs_8_) | copy-start | bytes 4718596
  69.5 1.5 %copy-start.8 = (bf16[108,64,128]{2,1,0:T(8,128)(2,1)S(1)}, bf16[108,64,128]{2,1,0:T(8,128)(2,1)}, u32[]{:S(2)}) copy-start(bf16[108,64,128]{2,1,0:T(8,128)(2,1)} %all-gather.3.cloned.1.call-done) | copy-start | bytes 5308420
Sparse Core Ops, SparseCore 0:
  8.9 43.0 all-gather.2

commit v3 on v2

--- a/solution.py
+++ b/solution.py
@@ -1,4 +1,5 @@
 import functools
+import itertools
 
 import jax
 import jax.numpy as jnp
@@ -18,6 +19,7 @@
 VAE_SCALE = 1.0 / 0.476986
 SCORE_UNIT = HD**-0.5 * 1.4426950408889634
 HEAD_BLOCK = 4
+HEAD_PARTS = (12, 4)
 NARROW = 4 * LAT
 MIB = 1 << 20
 
@@ -52,47 +54,37 @@
     return top * SCORE_UNIT, total, out
 
 
-def own_kernel(tiles_ref, counts_ref, q_ref, k_ref, v_ref, w_ref, level_ref, mapped_ref):
+def attend_kernel(offset, tiles_ref, counts_ref, q_ref, k_ref, v_ref, w_ref, level_ref, mapped_ref):
     block = pl.program_id(0)
     for i in range(HEAD_BLOCK):
         cols = slice(i * HD, (i + 1) * HD)
-        head = block * HEAD_BLOCK + i
+        row = block * HEAD_BLOCK + i
         top, total, out = partial_head(
-            head, q_ref[:, cols], k_ref[:, cols], v_ref[:, cols], tiles_ref, counts_ref
+            offset + row, q_ref[:, cols], k_ref[:, cols], v_ref[:, cols], tiles_ref, counts_ref
         )
         out = (out / total).astype(jnp.bfloat16)
-        level_ref[pl.ds(head, 1), :] = top + jnp.log2(total)
+        level_ref[pl.ds(row, 1), :] = top + jnp.log2(total)
         mapped_ref[i] = lax.dot_general(
             w_ref[:, cols], out, (((1,), (0,)), ((), ())), preferred_element_type=jnp.float32
         )
 
 
-def other_kernel(tiles_ref, counts_ref, q_ref, k_ref, v_ref, w_ref, level_ref, sent_ref):
-    block = pl.program_id(0)
-    mapped = jnp.zeros((NARROW, q_ref.shape[0]), jnp.float32)
-    for i in range(HEAD_BLOCK):
-        cols = slice(i * HD, (i + 1) * HD)
-        head = block * HEAD_BLOCK + i
-        top, total, out = partial_head(
-            head, q_ref[:, cols], k_ref[:, cols], v_ref[:, cols], tiles_ref, counts_ref
-        )
-        theirs = level_ref[pl.ds(head, 1), :]
-        mine = top + jnp.log2(total)
-        high = jnp.maximum(mine, theirs)
-        level = high + jnp.log2(jnp.exp2(mine - high) + jnp.exp2(theirs - high))
-        out = (out * jnp.exp2(top - level)).astype(jnp.bfloat16)
-        sent_ref[pl.ds(NARROW + head, 1), :] = jnp.exp2(theirs - level)
-        mapped = mapped + lax.dot_general(
-            w_ref[:, cols], out, (((1,), (0,)), ((), ())), preferred_element_type=jnp.float32
-        )
-
-    @pl.when(block == 0)
-    def _():
-        sent_ref[0:NARROW, :] = mapped
-
-    @pl.when(block > 0)
-    def _():
-        sent_ref[0:NARROW, :] = sent_ref[0:NARROW, :] + mapped
+def combine_kernel(parts, theirs_ref, *refs):
+    level_refs, mapped_refs, sent_ref = refs[:parts], refs[parts : 2 * parts], refs[-1]
+    theirs = theirs_ref[...]
+    mine = jnp.concatenate([ref[...] for ref in level_refs], axis=0)
+    high = jnp.maximum(mine, theirs)
+    level = high + jnp.log2(jnp.exp2(mine - high) + jnp.exp2(theirs - high))
+    mine = jnp.exp2(mine - level)
+    total = None
+    head = 0
+    for ref in mapped_refs:
+        for i in range(ref.shape[0]):
+            term = ref[i] * mine[head : head + 1]
+            total = term if total is None else total + term
+            head += 1
+    sent_ref[0:NARROW, :] = total
+    sent_ref[NARROW:, :] = jnp.exp2(theirs - level)
 
 
 def merge_kernel(frames, rows, cols, rank_ref, got_ref, mapped_ref, out_ref, rim_ref):
@@ -113,54 +105,75 @@
     flat_query = queries.reshape(tokens, feature_count)
     flat_key = key_states.reshape(tokens, feature_count)
     flat_value = value_states.reshape(tokens, feature_count)
-    other_query = lax.ppermute(flat_query, "sp", [(0, 1), (1, 0)])
+    swap = [(0, 1), (1, 0)]
+    ends = list(itertools.accumulate(HEAD_PARTS))
+    starts = [0] + ends[:-1]
+    other_queries = [
+        lax.ppermute(flat_query[:, start * HD : end * HD], "sp", swap) for start, end in zip(starts, ends)
+    ]
     kept_tiles = kept_tiles.transpose(1, 2, 0)
     kept_counts = kept_counts.T
     patch_weight = patch_weight.T
     smem = pl.BlockSpec(memory_space=pltpu.SMEM)
-    heads = pl.BlockSpec((tokens, HEAD_BLOCK * HD), lambda i: (0, i))
-    weight = pl.BlockSpec((NARROW, HEAD_BLOCK * HD), lambda i: (0, i))
+    params = pltpu.CompilerParams(
+        dimension_semantics=("arbitrary",), vmem_limit_bytes=24 * MIB
+    )
 
     def whole(*shape):
         return pl.BlockSpec(shape, lambda i: (0,) * len(shape))
 
-    params = pltpu.CompilerParams(
-        dimension_semantics=("arbitrary",), vmem_limit_bytes=24 * MIB
-    )
-    cost = pl.CostEstimate(
-        flops=4 * HEADS * tokens * tokens * HD,
-        bytes_accessed=3 * tokens * HEADS * HD * 2,
-        transcendentals=HEADS * tokens * tokens,
-    )
-    level, mapped = pl.pallas_call(
-        own_kernel,
-        grid=(HEADS // HEAD_BLOCK,),
-        in_specs=[smem, smem, heads, heads, heads, weight],
-        out_specs=[
-            whole(HEADS, tokens),
-            pl.BlockSpec((HEAD_BLOCK, NARROW, tokens), lambda i: (i, 0, 0)),
-        ],
-        out_shape=[
-            jax.ShapeDtypeStruct((HEADS, tokens), jnp.float32),
-            jax.ShapeDtypeStruct((HEADS, NARROW, tokens), jnp.float32),
-        ],
-        compiler_params=params,
-        cost_estimate=cost,
-        name="own_keys",
-    )(kept_tiles, kept_counts, flat_query, flat_key, flat_value, patch_weight)
+    def attend(part, start, name):
+        count = part.shape[1] // HD
+        first_block = start // HEAD_BLOCK
+        heads = pl.BlockSpec((tokens, HEAD_BLOCK * HD), lambda i: (0, first_block + i))
+        return pl.pallas_call(
+            functools.partial(attend_kernel, start),
+            grid=(count // HEAD_BLOCK,),
+            in_specs=[
+                smem,
+                smem,
+                pl.BlockSpec((tokens, HEAD_BLOCK * HD), lambda i: (0, i)),
+                heads,
+                heads,
+                pl.BlockSpec((NARROW, HEAD_BLOCK * HD), lambda i: (0, first_block + i)),
+            ],
+            out_specs=[
+                whole(count, tokens),
+                pl.BlockSpec((HEAD_BLOCK, NARROW, tokens), lambda i: (i, 0, 0)),
+            ],
+            out_shape=[
+                jax.ShapeDtypeStruct((count, tokens), jnp.float32),
+                jax.ShapeDtypeStruct((count, NARROW, tokens), jnp.float32),
+            ],
+            compiler_params=params,
+            cost_estimate=pl.CostEstimate(
+                flops=4 * count * tokens * tokens * HD,
+                bytes_accessed=3 * tokens * count * HD * 2,
+                transcendentals=count * tokens * tokens,
+            ),
+            name=name,
+        )(kept_tiles, kept_counts, part, flat_key, flat_value, patch_weight)
+
+    level, mapped = attend(flat_query, 0, "own_queries")
     level, ready = lax.optimization_barrier((level, ready))
-    other_level = lax.ppermute(level, "sp", [(0, 1), (1, 0)])
+    other_level = lax.ppermute(level, "sp", swap)
+    levels, shares = [], []
+    for part, start in zip(other_queries, starts):
+        if levels:
+            part, _ = lax.optimization_barrier((part, levels[-1]))
+        part_level, share = attend(part, start, "other_queries")
+        levels.append(part_level)
+        shares.append(share)
     sent = pl.pallas_call(
-        other_kernel,
-        grid=(HEADS // HEAD_BLOCK,),
-        in_specs=[smem, smem, heads, heads, heads, weight, whole(HEADS, tokens)],
+        functools.partial(combine_kernel, len(levels)),
+        grid=(1,),
+        in_specs=[whole(*part.shape) for part in (other_level, *levels, *shares)],
         out_specs=whole(NARROW + HEADS, tokens),
         out_shape=jax.ShapeDtypeStruct((NARROW + HEADS, tokens), jnp.float32),
         compiler_params=params,
-        cost_estimate=cost,
-        name="other_queries",
-    )(kept_tiles, kept_counts, other_query, flat_key, flat_value, patch_weight, other_level)
-    got = lax.ppermute(sent, "sp", [(0, 1), (1, 0)])
+        name="combine",
+    )(other_level, *levels, *shares)
+    got = lax.ppermute(sent, "sp", swap)
     rank = lax.axis_index("sp").astype(jnp.int32).reshape(1)
     rim_tokens = frames // 2 * cols
     latent, rim = pl.pallas_call(
@@ -277,17 +290,28 @@
     return packed, grid[:, 0].reshape(-1, 2 * NARROW), grid[:, -1].reshape(-1, 2 * NARROW)
 
 
+def spread_kernel(plain_ref, out_ref):
+    empty = jnp.zeros((LAT, CH), jnp.bfloat16)
+    for side in range(2):
+        blocks = itertools.product(range(3), range(2), range(2), range(2), range(2))
+        for position, (dt, rr, cc, u, w) in enumerate(blocks):
+            dz = 2 * cc + w - (1 - side)
+            for ro in range(2):
+                dy = 2 * rr + u - ro
+                inside = 0 <= dy < 3 and 0 <= dz < 3
+                block = plain_ref[(dt * 3 + dy) * 3 + dz] if inside else empty
+                out_ref[side, position * LAT : (position + 1) * LAT, ro * CH : (ro + 1) * CH] = block
+
+
 def first_weights(first_kernel):
-    plain = first_kernel.reshape(3, 3, 3, LAT, CH)
-    both_rows = jnp.stack(
-        [jnp.pad(plain, ((0, 0), (r, 1 - r), (0, 0), (0, 0), (0, 0))) for r in range(2)], axis=4
-    )
-    matrices = []
-    for c in (1, 0):
-        wide = jnp.pad(both_rows, ((0, 0), (0, 0), (c, 1 - c), (0, 0), (0, 0), (0, 0)))
-        wide = wide.reshape(3, 2, 2, 2, 2, LAT, 2, CH).transpose(0, 1, 3, 2, 4, 5, 6, 7)
-        matrices.append(wide.reshape(3 * 2 * 2 * NARROW, 2 * CH))
-    return jnp.stack(matrices)
+    return pl.pallas_call(
+        spread_kernel,
+        grid=(1,),
+        in_specs=[pl.BlockSpec(first_kernel.shape, lambda i: (0, 0, 0))],
+        out_specs=pl.BlockSpec((2, 12 * NARROW, 2 * CH), lambda i: (0, 0, 0)),
+        out_shape=jax.ShapeDtypeStruct((2, 12 * NARROW, 2 * CH), jnp.bfloat16),
+        name="spread_first_kernel",
+    )(first_kernel)
 
 
 def decode_kernel(
@@ -295,12 +319,11 @@
     rows,
     cols,
     place_ref,
-    own_refs,
-    above_refs,
-    below_refs,
+    own_ref,
+    above_ref,
+    below_ref,
     weight_hbm,
-    mine_ref,
-    theirs_ref,
+    kernel_hbm,
     out_ref,
     token_ref,
     pair_ref,
@@ -311,35 +334,29 @@
     kernel_ref,
     sems,
 ):
-    step = place_ref[0]
-    at_first = place_ref[1] == 0
-    at_last = place_ref[1] == place_ref[2] - 1
-    half = place_ref[3]
+    at_first = place_ref[0] == 0
+    at_last = place_ref[0] == place_ref[1] - 1
     copies = [
         pltpu.make_async_copy(weight_hbm, weight_ref, sems.at[0]),
-        pltpu.make_async_copy(mine_ref, kernel_ref.at[half], sems.at[1]),
-        pltpu.make_async_copy(theirs_ref, kernel_ref.at[1 - half], sems.at[2]),
+        pltpu.make_async_copy(kernel_hbm, kernel_ref, sems.at[1]),
     ]
     for copy in copies:
         copy.start()
 
     lane = lax.broadcasted_iota(jnp.int32, (1, 1, 1, 2 * NARROW), 3)
 
-    def picked(refs, height):
-        chosen = refs[0][...]
-        for k in range(1, len(refs)):
-            chosen = jnp.where(step == k, refs[k][...], chosen)
-        chosen = chosen.astype(jnp.float32)
-        turned = pltpu.roll(chosen, NARROW, 1)
+    def unpacked(ref, height):
+        plain = ref[...].astype(jnp.float32)
+        turned = pltpu.roll(plain, NARROW, 1)
         shape = (frames // 2, height, cols, 2 * NARROW)
-        chosen, turned = chosen.reshape(shape), turned.reshape(shape)
-        early = jnp.where(lane < NARROW, chosen, turned)
-        late = jnp.where(lane < NARROW, turned, chosen)
+        plain, turned = plain.reshape(shape), turned.reshape(shape)
+        early = jnp.where(lane < NARROW, plain, turned)
+        late = jnp.where(lane < NARROW, turned, plain)
         return jnp.concatenate([early, late], axis=0)
 
-    token_ref[:, 1 : 1 + rows, 8 : 8 + cols, :] = picked(own_refs, rows)
-    above = picked(above_refs, 1)
-    below = above if below_refs is above_refs else picked(below_refs, 1)
+    token_ref[:, 1 : 1 + rows, 8 : 8 + cols, :] = unpacked(own_ref, rows)
+    above = unpacked(above_ref, 1)
+    below = above if below_ref is above_ref else unpacked(below_ref, 1)
     for f in range(frames):
         edge = pltpu.roll(token_ref[f, 1, 8 : 8 + cols, :], 2 * LAT, 1)
         token_ref[f, 0, 8 : 8 + cols, :] = jnp.where(at_first, edge, above[f, 0])
@@ -413,14 +430,7 @@
         for dy in range(3):
             window = wide_ref[dt : dt + frames, dy : dy + height].reshape(cells, 3 * CH)
             weight = jnp.concatenate(
-                [
-                    jnp.concatenate(
-                        [kernel_ref[side, :, (dt * 3 + dy) * 3 + dz].reshape(CH, CH // 2) for side in range(2)],
-                        axis=1,
-                    )
-                    for dz in range(3)
-                ],
-                axis=0,
+                [kernel_ref[:, (dt * 3 + dy) * 3 + dz].reshape(CH, CH) for dz in range(3)], axis=0
             )
             product = jnp.dot(window, weight, preferred_element_type=jnp.float32)
             total = product if total is None else total + product
@@ -431,27 +441,24 @@
         out_ref[:, :, :, lanes] = (total[:, :, :, lanes] + residual).astype(jnp.bfloat16)
 
 
-def decode(frames, rows, cols, place, own, above, below, weights, mine, theirs):
+def decode(frames, rows, cols, place, own, rims, weights, kernel):
     height, width = 2 * rows, 2 * cols
-    steps = len(own)
-    rims = [above] if below is above else [above, below]
-    small = own + [part for rim in rims for part in rim]
+    small = [own, *rims]
 
     def whole(shape):
         return pl.BlockSpec(shape, lambda i, place: (0,) * len(shape))
 
-    def body(place_ref, *refs):
-        own_refs, above_refs = refs[:steps], refs[steps : 2 * steps]
-        below_refs = above_refs if len(rims) == 1 else refs[2 * steps : 3 * steps]
+    def body(place_ref, own_ref, *refs):
+        above_ref, below_ref = refs[0], refs[len(rims) - 1]
         decode_kernel(
-            frames, rows, cols, place_ref, own_refs, above_refs, below_refs, *refs[len(small) :]
+            frames, rows, cols, place_ref, own_ref, above_ref, below_ref, *refs[len(rims) :]
         )
 
     grid_spec = pltpu.PrefetchScalarGridSpec(
         num_scalar_prefetch=1,
         grid=(1,),
         in_specs=[whole(part.shape) for part in small]
-        + [pl.BlockSpec(memory_space=space) for space in (pl.ANY, pltpu.HBM, pl.ANY)],
+        + [pl.BlockSpec(memory_space=pl.ANY)] * 2,
         out_specs=whole((frames, height, width, CH)),
         scratch_shapes=[
             pltpu.VMEM((frames, rows + 2, cols + 16, 2 * NARROW), jnp.float32),
@@ -460,22 +467,22 @@
             pltpu.VMEM((CH // 128, frames, height + 2, width + 16, 128), jnp.float32),
             pltpu.VMEM((frames + 2, height + 2, width, 3 * CH), jnp.bfloat16),
             pltpu.VMEM(weights.shape, jnp.bfloat16),
-            pltpu.VMEM((2,) + mine.shape, jnp.bfloat16),
-            pltpu.SemaphoreType.DMA((3,)),
+            pltpu.VMEM(kernel.shape, jnp.bfloat16),
+            pltpu.SemaphoreType.DMA((2,)),
         ],
     )
     return pl.pallas_call(
         body,
         grid_spec=grid_spec,
         out_shape=jax.ShapeDtypeStruct((frames, height, width, CH), jnp.bfloat16),
-        compiler_params=pltpu.CompilerParams(vmem_limit_bytes=32 * MIB),
+        compiler_params=pltpu.CompilerParams(vmem_limit_bytes=56 * MIB),
         cost_estimate=pl.CostEstimate(
             flops=2 * frames * height * width * 27 * CH * CH,
             bytes_accessed=27 * CH * CH * 2 + frames * height * width * CH * 2,
             transcendentals=frames * height * width * CH,
         ),
         name="decode_block",
-    )(place, *small, weights, mine, theirs)
+    )(place, *small, weights, kernel)
 
 
 def local(
@@ -495,42 +502,45 @@
     segment_count = lax.axis_size("segment")
     segment_rank = lax.axis_index("segment")
 
-    half = lax.rem(segment_rank, 2)
-    share = lax.dynamic_slice_in_dim(second_kernel, half * (CH // 2), CH // 2, 2)
-    mine = lax.all_gather(share, "grp", axis=0, tiled=False)
-
+    taps, own_channels, channels = second_kernel.shape
+    share = taps * own_channels // segment_count
+    flat = second_kernel.reshape(taps * own_channels, channels)
+    flat = lax.dynamic_slice_in_dim(flat, segment_rank * share, share, 0)
+    kernel = lax.all_gather(flat, ("grp", "segment"), axis=0, tiled=True)
+    kernel = kernel.reshape(-1, taps, own_channels, channels)
     weights = first_weights(first_kernel)
-    picks = (decode_slot == segment_rank).astype(jnp.int32)
-    source = jnp.sum(jnp.arange(segment_count, dtype=jnp.int32) * picks)
-    step = lax.rem(segment_rank - source + segment_count, segment_count)
-    place = jnp.stack([step, sp_rank, jnp.int32(sp_count), half]).astype(jnp.int32)
+    place = jnp.stack([sp_rank, jnp.int32(sp_count)]).astype(jnp.int32)
+    orders = list(itertools.permutations(range(segment_count)))
+    same = jnp.all(decode_slot[None, :] == jnp.array(orders, jnp.int32), axis=1)
+    order = jnp.sum(jnp.where(same, jnp.arange(len(orders), dtype=jnp.int32), 0)).astype(jnp.int32)
 
     arguments = (queries, key_states, value_states, kept_tiles, kept_counts, patch_weight)
     if sp_count == 2 and rows * sp_count == TH and frames == TT:
-        latent, rim, (weights, place) = split_attention(*arguments, (weights, place))
-        rims = [(rim, [(0, 1), (1, 0)])]
+        latent, rim, (weights, place, order) = split_attention(*arguments, (weights, place, order))
+        moves = [(rim, [(0, 1), (1, 0)])]
     else:
         latent, top, bottom = exchanged_attention(*arguments)
-        rims = [
+        moves = [
             (bottom, [(i, i + 1) for i in range(sp_count - 1)]),
             (top, [(i + 1, i) for i in range(sp_count - 1)]),
         ]
-    mine, _ = lax.optimization_barrier((mine, latent))
-    theirs = lax.ppermute(mine, "segment", [(i, i ^ 1) for i in range(segment_count)])
-
-    def along_segment(part, step, moves):
-        pairs = [
-            (i * sp_count + a, (i + step) % segment_count * sp_count + b)
-            for i in range(segment_count)
-            for a, b in moves
-        ]
-        return lax.ppermute(part, ("segment", "sp"), pairs)
-
-    stay = [(i, i) for i in range(sp_count)]
-    own = [latent] + [along_segment(latent, step, stay) for step in range(1, segment_count)]
-    beside = [[along_segment(rim, step, moves) for step in range(segment_count)] for rim, moves in rims]
-    decoded = decode(frames, rows, cols, place, own, beside[0], beside[-1], weights, mine, theirs)
-    return decoded[None, None]
+    moves = [(latent, [(i, i) for i in range(sp_count)])] + moves
+
+    def ordered(slots):
+        def send(*parts):
+            return tuple(
+                lax.ppermute(
+                    part,
+                    ("segment", "sp"),
+                    [(i * sp_count + a, slots[i] * sp_count + b) for i in range(segment_count) for a, b in pairs],
+                )
+                for part, (_, pairs) in zip(parts, moves)
+            )
+
+        return send
+
+    own, *rims = lax.switch(order, [ordered(slots) for slots in orders], *[part for part, _ in moves])
+    return decode(frames, rows, cols, place, own, rims, weights, kernel)[None, None]
 
 
 def solution(mesh):

time: 85.9 us -> 75.7 us (0.88)
  local copies, waits for them, and re-layouts: 16.6 us -> 9.02 us
  waiting for transfers between devices: 22.4 us -> 15.7 us
  Pallas kernels: 19.5 us -> 23 us
  starting transfers between devices: 10.1 us -> 12 us
  other arithmetic: 2.78 us -> 1.35 us
    ppermute x11 -> x6, waiting for transfers between devices: 17.2 us -> 9.35 us  [the longest x2 4.03 us: split_attention(): lax.ppermute(flat_query[:, start * HD:end * HD], 'sp', swap)]
    another operation x3 -> x0, local copies, waits for them, and re-layouts: 5.6 us -> none  [the longest x2 4.52 us: first_weights(): return jnp.stack(matrices)]
    transpose x2 -> x0, local copies, waits for them, and re-layouts: 3.83 us -> none  [first_weights(): wide.reshape(3, 2, 2, 2, 2, LAT, 2, CH).transpose(0, 1, 3, 2, 4, 5, 6, 7)]
    slice x0 -> x2, local copies, waits for them, and re-layouts: none -> 3.74 us  [split_attention(): flat_query[:, start * HD:end * HD]]
    pallas_call x2 -> x5, Pallas kernels: 11.6 us -> 14 us  [the longest x3 11.7 us: attend(): pl.pallas_call(functools.partial(attend_kernel, start), grid=(count // HE...]
    ppermute x11 -> x6, starting transfers between devices: 10.1 us -> 12 us  [the longest x2 5.19 us: send(): lax.ppermute(part, ('segment', 'sp'), [(i * sp_count + a, slots[i] * sp_c...]
    all_gather x1, waiting for transfers between devices: 5.1 us -> 6.34 us  [local(): kernel = lax.all_gather(flat, ('grp', 'segment'), axis=0, tiled=True)]
    pallas_call x1, Pallas kernels: 7.69 us -> 8.86 us  [decode(): pl.pallas_call(body, grid_spec=grid_spec, out_shape=jax.ShapeDtypeStruct(...]
  transfers between devices with their start and end apart: 12 -> 7, of which waited for: 7 -> 5; matrix products, arithmetic and copies ran while one was open for 15% -> 7% of each run, Pallas kernels for 14% -> 19%
where the time goes in v3:
time: 75.7 us; the launch traced here: 75.3 us
  Pallas kernels  23 us (30%)
  waiting for transfers between devices  15.7 us (21%)
  between operations  14.1 us (19%)
  starting transfers between devices  12 us (16%)
  local copies, waits for them, and re-layouts  9.02 us (12%)
  other arithmetic  1.35 us (2%)
    pallas_call x3, Pallas kernels, attend(): pl.pallas_call(functools.partial(attend_kernel, start), grid=(count // HE...  11.7 us
    pallas_call x1, Pallas kernels, decode(): pl.pallas_call(body, grid_spec=grid_spec, out_shape=jax.ShapeDtypeStruct(...  8.86 us
    all_gather x1, waiting for transfers between devices, local(): kernel = lax.all_gather(flat, ('grp', 'segment'), axis=0, tiled=True)  6.34 us
    ppermute x2, starting transfers between devices, send(): lax.ppermute(part, ('segment', 'sp'), [(i * sp_count + a, slots[i] * sp_c...  5.19 us
    unnamed x22, local copies, waits for them, and re-layouts  4.56 us
    ppermute x2, waiting for transfers between devices, split_attention(): lax.ppermute(flat_query[:, start * HD:end * HD], 'sp', swap)  4.03 us
    slice x2, local copies, waits for them, and re-layouts, split_attention(): flat_query[:, start * HD:end * HD]  3.74 us
    ppermute x2, waiting for transfers between devices, send(): lax.ppermute(part, ('segment', 'sp'), [(i * sp_count + a, slots[i] * sp_c...  3.17 us
  transfers between devices with their start and end apart: 7, of which 5 were waited for; matrix products, arithmetic and copies ran while one was open for 7% of the time, Pallas kernels for 19%

profile of v3, /device:TPU:0, one launch (start us, length us, event | category | flops | bytes accessed | tf_op | source)
XLA Modules:
  0.0 75.3 jit_solution(17808114707940390196)
XLA Ops:
  6.5 0.0 copy-start
  6.5 0.0 copy-start.7
  6.5 0.0 copy-start.8
  6.5 0.0 copy-start.4
  6.6 0.0 all-gather.2.cloned.1.call-start
  6.6 1.1 %copy-done = bf16[27,64,256]{2,1,0:T(8,128)(2,1)S(1)} copy-done((bf16[27,64,256]{2,1,0:T(8,128)(2,1)S(1)}, bf16[27,64,256]{2,1,0:T(8,128)(2,1)}, u32[]{:S(2)}) %copy-start) | copy-done | bytes 884760
  7.7 0.7 constant_dynamic-slice_fusion
  8.4 0.0 all-gather.2.cloned.1.call-update
  8.4 0.0 copy-start.9
  8.5 0.0 copy-start.10
  8.5 2.1 %slice.8 = bf16[256,1536]{1,0:T(8,128)(2,1)} slice(bf16[256,2048]{1,0:T(8,128)(2,1)} %bitcast.17), slice={[0:256], [0:1536]} | slice | bytes 1572864 | tf_op jit(solution)/shard_map/slice | solution.py:112
  10.5 3.0 %collective-permute-start.49 = (bf16[256,1536]{1,0:T(8,128)(2,1)}, bf16[256,1536]{1,0:T(8,128)(2,1)}, u32[]{:S(2)}, u32[]{:S(2)}) collective-permute-start(bf16[256,1536]{1,0:T(8,128)(2,1)} %slice.8), channel_id=1, source_target_pairs={{0,1},{1,0},{2,3},{3,2},{4,5},{5,4},{6,7},{7,6},{8,9},{9,8},{10,11... | collective-permute-start | bytes 2359304 | tf_op jit(solution)/shard_map/ppermute | solution.py:112
  13.5 1.7 %slice.9 = bf16[256,512]{1,0:T(8,128)(2,1)} slice(bf16[256,2048]{1,0:T(8,128)(2,1)} %bitcast.18), slice={[0:256], [1536:2048]} | slice | bytes 524288 | tf_op jit(solution)/shard_map/slice | solution.py:112
  15.2 0.0 collective-permute-start.50
  15.2 2.2 %spread_first_kernel.1.refs_1_ = bf16[2,768,512]{2,1,0:T(8,128)(2,1)} custom-call(bf16[27,16,256]{2,1,0:T(8,128)(2,1)} %plain_ref.1), custom_call_target="tpu_custom_call" | custom-call | tf_op jit(solution)/shard_map/spread_first_kernel/pallas_call | solution.py:307
  17.4 0.0 copy-done.7
  17.4 0.0 copy-done.8
  17.4 0.0 copy-done.1
  17.4 0.0 copy-done.2
  17.4 0.0 copy-done.4
  17.4 0.0 copy-start.3
  17.4 1.2 %copy-done.3 = bf16[1,1,4,4,16,2048]{5,4,3,2,1,0:T(8,128)(2,1)S(1)} copy-done((bf16[1,1,4,4,16,2048]{5,4,3,2,1,0:T(8,128)(2,1)S(1)}, bf16[1,1,4,4,16,2048]{5,4,3,2,1,0:T(8,128)(2,1)}, u32[]{:S(2)}) %copy-start.3) | copy-done | bytes 1048600
  18.7 5.5 %own_queries.1 = (f32[16,256]{1,0:T(8,128)S(1)}, f32[16,64,256]{2,1,0:T(8,128)S(1)}) custom-call(s32[2,2,16]{2,1,0:T(2,128)S(1)} %bitcast.23, s32[2,16]{1,0:T(2,128)S(1)} %bitcast.26, bf16[256,2048]{1,0:T(8,128)(2,1)S(1)} %bitcast.19, bf16[256,2048]{1,0:T(8,128)(2,1)S(1)} %bitcast.11, bf16[256,2048]{1,0:T(8,128)(2,1)S(1)} %bitcast.14, ...), custom_call_target="tpu_custom_call" | custom-call | flops 536870912 | bytes 3145728 | tf_op jit(solution)/shard_map/own_queries/pallas_call | solution.py:129
  24.1 0.0 copy-start.5
  24.1 1.0 %copy-done.5 = f32[16,64,256]{2,1,0:T(8,128)} copy-done((f32[16,64,256]{2,1,0:T(8,128)}, f32[16,64,256]{2,1,0:T(8,128)S(1)}, u32[]{:S(2)}) %copy-start.5) | copy-done | bytes 1048600
  25.1 0.0 copy-done.9
  25.1 0.0 copy-done.10
  25.1 0.1 compare_reduce_fusion
  25.2 0.7 pad_add_fusion.place_ref
  25.9 0.6 select_reduce_fusion
  26.5 2.0 %collective-permute-start.48 = (f32[16,256]{1,0:T(8,128)S(1)}, f32[16,256]{1,0:T(8,128)S(1)}, u32[]{:S(2)}, u32[]{:S(2)}) collective-permute-start(f32[16,256]{1,0:T(8,128)S(1)} %get-tuple-element.165), channel_id=1, source_target_pairs={{0,1},{1,0},{2,3},{3,2},{4,5},{5,4},{6,7},{7,6},{8,9},{9,8},{10,11... | collective-permute-start | bytes 49160 | tf_op jit(solution)/shard_map/ppermute | solution.py:159
  28.5 3.7 %collective-permute-done.49.q_ref = bf16[256,1536]{1,0:T(8,128)(2,1)} collective-permute-done((bf16[256,1536]{1,0:T(8,128)(2,1)}, bf16[256,1536]{1,0:T(8,128)(2,1)}, u32[]{:S(2)}, u32[]{:S(2)}) %collective-permute-start.49) | collective-permute-done | bytes 786464 | tf_op jit(solution)/shard_map/ppermute | solution.py:112
  32.2 4.5 %other_queries.2 = (f32[12,256]{1,0:T(8,128)S(1)}, f32[12,64,256]{2,1,0:T(8,128)S(1)}) custom-call(s32[2,2,16]{2,1,0:T(2,128)S(1)} %bitcast.24, s32[2,16]{1,0:T(2,128)S(1)} %bitcast.27, bf16[256,1536]{1,0:T(8,128)(2,1)} %collective-permute-done.49.q_ref, bf16[256,2048]{1,0:T(8,128)(2,1)S(1)} %bitcast.12, bf16[256,2048]{1,0:T(8,128)(2,1)S(1)} %bitcast.15, ...), custom_call_target="tpu_custom_call" | custom-call | flops 402653184 | bytes 2359296 | tf_op jit(solution)/shard_map/other_queries/pallas_call | solution.py:129
  36.7 0.3 collective-permute-done.50.q_ref
  37.1 1.7 %other_queries.3 = (f32[4,256]{1,0:T(4,128)S(1)}, f32[4,64,256]{2,1,0:T(8,128)S(1)}) custom-call(s32[2,2,16]{2,1,0:T(2,128)S(1)} %bitcast.25, s32[2,16]{1,0:T(2,128)S(1)} %bitcast.28, bf16[256,512]{1,0:T(8,128)(2,1)S(1)} %collective-permute-done.50.q_ref, bf16[256,2048]{1,0:T(8,128)(2,1)S(1)} %bitcast.13, bf16[256,2048]{1,0:T(8,128)(2,1)S(1)} %bitcast.16, ...), custom_call_target="tpu_custom_call" | custom-call | flops 134217728 | bytes 786432 | tf_op jit(solution)/shard_map/other_queries/pallas_call | solution.py:129
  38.8 0.0 collective-permute-done.48.theirs_ref
  38.8 0.1 combine.1
  38.9 1.8 %collective-permute-start.51 = (f32[80,256]{1,0:T(8,128)S(1)}, f32[80,256]{1,0:T(8,128)S(1)}, u32[]{:S(2)}, u32[]{:S(2)}) collective-permute-start(f32[80,256]{1,0:T(8,128)S(1)} %combine.1), channel_id=1, source_target_pairs={{0,1},{1,0},{2,3},{3,2},{4,5},{5,4},{6,7},{7,6},{8,9},{9,8},{10,11... | collective-permute-start | bytes 245768 | tf_op jit(solution)/shard_map/ppermute | solution.py:176
  41.3 2.1 %collective-permute-done.51.got_ref = f32[80,256]{1,0:T(8,128)S(1)} collective-permute-done((f32[80,256]{1,0:T(8,128)S(1)}, f32[80,256]{1,0:T(8,128)S(1)}, u32[]{:S(2)}, u32[]{:S(2)}) %collective-permute-start.51) | collective-permute-done | bytes 81952 | tf_op jit(solution)/shard_map/ppermute | solution.py:176
  43.4 1.2 %copy-done.6 = f32[16,64,256]{2,1,0:T(8,128)S(1)} copy-done((f32[16,64,256]{2,1,0:T(8,128)S(1)}, f32[16,64,256]{2,1,0:T(8,128)}, u32[]{:S(2)}) %copy-start.6) | copy-done | bytes 1048600
  44.7 0.2 merge.1
  44.8 8.4 %conditional.1 = (bf16[128,128]{1,0:T(8,128)(2,1)}, bf16[32,128]{1,0:T(8,128)(2,1)}) conditional(s32[]{:T(128)} %clamp.3, (bf16[128,128]{1,0:T(8,128)(2,1)S(1)}, bf16[32,128]{1,0:T(8,128)(2,1)S(1)}) %merge.1, (bf16[128,128]{1,0:T(8,128)(2,1)S(1)}, bf16[32,128]{1,0:T(8,128)(2,1)S(1)}) %merge.1, ...), branch_computations={%region_2.3_spmd, %region_3.4_spmd, %region_4.5_spmd, %region_5.6_... | conditional | bytes 163936 | solution.py:542
  44.8 3.6 %collective-permute-start.28 = (bf16[128,128]{1,0:T(8,128)(2,1)S(1)}, bf16[128,128]{1,0:T(8,128)(2,1)}, u32[]{:S(2)}, u32[]{:S(2)}) collective-permute-start(bf16[128,128]{1,0:T(8,128)(2,1)S(1)} %get-tuple-element.129), channel_id=1, source_target_pairs={{0,16},{1,17},{8,8},{9,9},{16,0},{17,1},{24,24},{25,25},{2,18},{3,... | collective-permute-start | bytes 98312 | tf_op jit(solution)/shard_map/cond/branch_14_fun/ppermute | solution.py:532
  48.5 1.5 %collective-permute-start.29 = (bf16[32,128]{1,0:T(8,128)(2,1)S(1)}, bf16[32,128]{1,0:T(8,128)(2,1)}, u32[]{:S(2)}, u32[]{:S(2)}) collective-permute-start(bf16[32,128]{1,0:T(8,128)(2,1)S(1)} %get-tuple-element.130), channel_id=1, source_target_pairs={{0,17},{1,16},{8,9},{9,8},{16,1},{17,0},{24,25},{25,24},{2,19},{3,... | collective-permute-start | bytes 24584 | tf_op jit(solution)/shard_map/cond/branch_14_fun/ppermute | solution.py:532
  50.0 3.2 %collective-permute-done.29 = bf16[32,128]{1,0:T(8,128)(2,1)} collective-permute-done((bf16[32,128]{1,0:T(8,128)(2,1)S(1)}, bf16[32,128]{1,0:T(8,128)(2,1)}, u32[]{:S(2)}, u32[]{:S(2)}) %collective-permute-start.29) | collective-permute-done | bytes 8224 | tf_op jit(solution)/shard_map/cond/branch_14_fun/ppermute | solution.py:532
  53.2 0.0 collective-permute-done.28
  53.2 6.3 %all-gather.2.cloned.1.call-done = bf16[6912,256]{1,0:T(8,128)(2,1)} async-done(((bf16[432,256]{1,0:T(8,128)(2,1)}), bf16[6912,256]{1,0:T(8,128)(2,1)}) %all-gather.2.cloned.1.call-update) | async-done | bytes 3538960 | tf_op jit(solution)/shard_map/all_gather | solution.py:509
  59.6 8.9 %decode_block.1 = bf16[4,8,32,256]{3,2,1,0:T(8,128)(2,1)} custom-call(s32[2]{0:T(128)} %pad_add_fusion.place_ref, bf16[128,128]{1,0:T(8,128)(2,1)} %get-tuple-element.172.own_ref, bf16[32,128]{1,0:T(8,128)(2,1)} %get-tuple-element.173.refs_0_, bf16[2,768,512]{2,1,0:T(8,128)(2,1)} %spread_first_kernel.1.refs_1_, bf16[4,27,64,256]{3,2,1,0:T(8,128)(2,1)} %bitcast.29), custom_call_target="tpu_custom_call" | custom-call | flops 3623878656 | bytes 4063232 | tf_op jit(solution)/shard_map/decode_block/pallas_call | solution.py:474
  (3 shorter events, 0.0 us)
Async XLA Ops:
  6.5 1.2 %copy-start = (bf16[27,64,256]{2,1,0:T(8,128)(2,1)S(1)}, bf16[27,64,256]{2,1,0:T(8,128)(2,1)}, u32[]{:S(2)}) copy-start(bf16[27,64,256]{2,1,0:T(8,128)(2,1)} %param.42) | copy-start | bytes 2654212
  6.5 10.9 %copy-start.7 = (s32[16,2,2]{0,2,1:T(2,128)S(1)}, s32[16,2,2]{0,2,1:T(2,128)}, u32[]{:S(2)}) copy-start(s32[16,2,2]{0,2,1:T(2,128)} %param.37) | copy-start | bytes 772
  6.5 10.9 %copy-start.8 = (s32[16,2]{0,1:T(2,128)S(1)}, s32[16,2]{0,1:T(2,128)}, u32[]{:S(2)}) copy-start(s32[16,2]{0,1:T(2,128)} %param.38) | copy-start | bytes 388
  6.5 10.9 %copy-start.1 = (bf16[1,1,4,4,16,2048]{5,4,3,2,1,0:T(8,128)(2,1)S(1)}, bf16[1,1,4,4,16,2048]{5,4,3,2,1,0:T(8,128)(2,1)}, u32[]{:S(2)}) copy-start(bf16[1,1,4,4,16,2048]{5,4,3,2,1,0:T(8,128)(2,1)} %param.35) | copy-start | bytes 3145732
  6.5 10.9 %copy-start.2 = (bf16[1,1,4,4,16,2048]{5,4,3,2,1,0:T(8,128)(2,1)S(1)}, bf16[1,1,4,4,16,2048]{5,4,3,2,1,0:T(8,128)(2,1)}, u32[]{:S(2)}) copy-start(bf16[1,1,4,4,16,2048]{5,4,3,2,1,0:T(8,128)(2,1)} %param.36) | copy-start | bytes 3145732
  6.5 10.9 %copy-start.4 = (bf16[2048,64]{0,1:T(8,128)(2,1)S(1)}, bf16[2048,64]{0,1:T(8,128)(2,1)}, u32[]{:S(2)}) copy-start(bf16[2048,64]{0,1:T(8,128)(2,1)} %param.39) | copy-start | bytes 786436
  6.6 53.0 %all-gather.2.cloned.1.call-start = ((), (), s32[]{:S(2)}) async-start(), calls=%async_computation | async-start | bytes 3760128 | tf_op jit(solution)/shard_map/all_gather | solution.py:509
  8.4 16.7 %copy-start.9 = (s32[24,4]{0,1:T(4,128)S(1)}, s32[24,4]{0,1:T(4,128)}, u32[]{:S(2)}) copy-start(s32[24,4]{0,1:T(4,128)} %constant.23.clone) | copy-start | bytes 1156
  8.5 16.7 %copy-start.10 = (s32[4]{0:T(128)S(1)}, s32[4]{0:T(128)}, u32[]{:S(2)}) copy-start(s32[4]{0:T(128)} %param.40) | copy-start | bytes 52
  10.5 21.6 %collective-permute-start.49 = (bf16[256,1536]{1,0:T(8,128)(2,1)}, bf16[256,1536]{1,0:T(8,128)(2,1)}, u32[]{:S(2)}, u32[]{:S(2)}) collective-permute-start(bf16[256,1536]{1,0:T(8,128)(2,1)} %slice.8), channel_id=1, source_target_pairs={{0,1},{1,0},{2,3},{3,2},{4,5},{5,4},{6,7},{7,6},{8,9},{9,8},{10,11... | collective-permute-start | bytes 2359304 | tf_op jit(solution)/shard_map/ppermute | solution.py:112
  15.2 21.9 %collective-permute-start.50 = (bf16[256,512]{1,0:T(8,128)(2,1)}, bf16[256,512]{1,0:T(8,128)(2,1)S(1)}, u32[]{:S(2)}, u32[]{:S(2)}) collective-permute-start(bf16[256,512]{1,0:T(8,128)(2,1)} %slice.9), channel_id=1, source_target_pairs={{0,1},{1,0},{2,3},{3,2},{4,5},{5,4},{6,7},{7,6},{8,9},{9,8},{10,11... | collective-permute-start | bytes 786440 | tf_op jit(solution)/shard_map/ppermute | solution.py:112
  17.4 1.2 %copy-start.3 = (bf16[1,1,4,4,16,2048]{5,4,3,2,1,0:T(8,128)(2,1)S(1)}, bf16[1,1,4,4,16,2048]{5,4,3,2,1,0:T(8,128)(2,1)}, u32[]{:S(2)}) copy-start(bf16[1,1,4,4,16,2048]{5,4,3,2,1,0:T(8,128)(2,1)} %param.34) | copy-start | bytes 3145732
  24.1 1.0 %copy-start.5 = (f32[16,64,256]{2,1,0:T(8,128)}, f32[16,64,256]{2,1,0:T(8,128)S(1)}, u32[]{:S(2)}) copy-start(f32[16,64,256]{2,1,0:T(8,128)S(1)} %get-tuple-element.171.mapped_ref) | copy-start | bytes 3145732
  26.5 12.3 %collective-permute-start.48 = (f32[16,256]{1,0:T(8,128)S(1)}, f32[16,256]{1,0:T(8,128)S(1)}, u32[]{:S(2)}, u32[]{:S(2)}) collective-permute-start(f32[16,256]{1,0:T(8,128)S(1)} %get-tuple-element.165), channel_id=1, source_target_pairs={{0,1},{1,0},{2,3},{3,2},{4,5},{5,4},{6,7},{7,6},{8,9},{9,8},{10,11... | collective-permute-start | bytes 49160 | tf_op jit(solution)/shard_map/ppermute | solution.py:159
  38.9 4.5 %collective-permute-start.51 = (f32[80,256]{1,0:T(8,128)S(1)}, f32[80,256]{1,0:T(8,128)S(1)}, u32[]{:S(2)}, u32[]{:S(2)}) collective-permute-start(f32[80,256]{1,0:T(8,128)S(1)} %combine.1), channel_id=1, source_target_pairs={{0,1},{1,0},{2,3},{3,2},{4,5},{5,4},{6,7},{7,6},{8,9},{9,8},{10,11... | collective-permute-start | bytes 245768 | tf_op jit(solution)/shard_map/ppermute | solution.py:176
  43.4 1.2 %copy-start.6 = (f32[16,64,256]{2,1,0:T(8,128)S(1)}, f32[16,64,256]{2,1,0:T(8,128)}, u32[]{:S(2)}) copy-start(f32[16,64,256]{2,1,0:T(8,128)} %copy-done.5) | copy-start | bytes 3145732
  44.8 8.4 %collective-permute-start.28 = (bf16[128,128]{1,0:T(8,128)(2,1)S(1)}, bf16[128,128]{1,0:T(8,128)(2,1)}, u32[]{:S(2)}, u32[]{:S(2)}) collective-permute-start(bf16[128,128]{1,0:T(8,128)(2,1)S(1)} %get-tuple-element.129), channel_id=1, source_target_pairs={{0,16},{1,17},{8,8},{9,9},{16,0},{17,1},{24,24},{25,25},{2,18},{3,... | collective-permute-start | bytes 98312 | tf_op jit(solution)/shard_map/cond/branch_14_fun/ppermute | solution.py:532
  48.5 4.7 %collective-permute-start.29 = (bf16[32,128]{1,0:T(8,128)(2,1)S(1)}, bf16[32,128]{1,0:T(8,128)(2,1)}, u32[]{:S(2)}, u32[]{:S(2)}) collective-permute-start(bf16[32,128]{1,0:T(8,128)(2,1)S(1)} %get-tuple-element.130), channel_id=1, source_target_pairs={{0,17},{1,16},{8,9},{9,8},{16,1},{17,0},{24,25},{25,24},{2,19},{3,... | collective-permute-start | bytes 24584 | tf_op jit(solution)/shard_map/cond/branch_14_fun/ppermute | solution.py:532
Sparse Core Ops, SparseCore 0:
  9.7 49.8 all-gather.1

commit v4 on v3

--- a/solution.py
+++ b/solution.py
@@ -19,7 +19,8 @@
 VAE_SCALE = 1.0 / 0.476986
 SCORE_UNIT = HD**-0.5 * 1.4426950408889634
 HEAD_BLOCK = 4
-HEAD_PARTS = (12, 4)
+HEAD_PARTS = (4, 8, 4)
+TAP_PARTS = (15, 12)
 NARROW = 4 * LAT
 MIB = 1 << 20
 
@@ -54,8 +55,25 @@
     return top * SCORE_UNIT, total, out
 
 
-def attend_kernel(offset, tiles_ref, counts_ref, q_ref, k_ref, v_ref, w_ref, level_ref, mapped_ref):
+def row_choice(frames, rows, cols, row, lanes, start):
+    token = lax.broadcasted_iota(jnp.int32, (frames * rows * cols, lanes), 0)
+    lane = lax.broadcasted_iota(jnp.int32, (frames * rows * cols, lanes), 1) - start
+    wanted = lax.div(lane, cols) * (rows * cols) + row * cols + lax.rem(lane, cols)
+    inside = jnp.logical_and(lane >= 0, lane < frames * cols)
+    return jnp.where(jnp.logical_and(inside, token == wanted), 1.0, 0.0)
+
+
+def attend_kernel(
+    offset, grid, rank_ref, tiles_ref, counts_ref, q_ref, k_ref, v_ref, w_ref, level_ref, mapped_ref, *rim_refs
+):
     block = pl.program_id(0)
+    if rim_refs:
+        frames, rows, cols = grid
+        near = jnp.where(rank_ref[0] == 0, rows - 1, 0)
+        choices = [
+            row_choice(frames, rows, cols, near, 2 * NARROW, start).astype(jnp.bfloat16)
+            for start in (0, NARROW)
+        ]
     for i in range(HEAD_BLOCK):
         cols = slice(i * HD, (i + 1) * HD)
         row = block * HEAD_BLOCK + i
@@ -64,13 +82,19 @@
         )
         out = (out / total).astype(jnp.bfloat16)
         level_ref[pl.ds(row, 1), :] = top + jnp.log2(total)
-        mapped_ref[i] = lax.dot_general(
-            w_ref[:, cols], out, (((1,), (0,)), ((), ())), preferred_element_type=jnp.float32
-        )
-
-
-def combine_kernel(parts, theirs_ref, *refs):
-    level_refs, mapped_refs, sent_ref = refs[:parts], refs[parts : 2 * parts], refs[-1]
+        mapped = jnp.dot(w_ref[:, cols], out, preferred_element_type=jnp.float32)
+        mapped_ref[i] = mapped
+        if rim_refs:
+            rim = jnp.dot(mapped.astype(jnp.bfloat16), choices[i % 2], preferred_element_type=jnp.float32)
+            if i % 2 == 0:
+                even = rim
+            else:
+                rim_refs[0][i // 2] = (even + rim).astype(jnp.bfloat16)
+
+
+def combine_kernel(parts, grid, rank_ref, theirs_ref, rim_ref, *refs):
+    level_refs, mapped_refs = refs[:parts], refs[parts : 2 * parts]
+    sent_ref, beside_ref = refs[2 * parts :]
     theirs = theirs_ref[...]
     mine = jnp.concatenate([ref[...] for ref in level_refs], axis=0)
     high = jnp.maximum(mine, theirs)
@@ -83,20 +107,39 @@
             term = ref[i] * mine[head : head + 1]
             total = term if total is None else total + term
             head += 1
+    theirs = jnp.exp2(theirs - level)
     sent_ref[0:NARROW, :] = total
-    sent_ref[NARROW:, :] = jnp.exp2(theirs - level)
-
-
-def merge_kernel(frames, rows, cols, rank_ref, got_ref, mapped_ref, out_ref, rim_ref):
+    sent_ref[NARROW:, :] = theirs
+    frames, rows, cols = grid
+    near = jnp.where(rank_ref[0] == 0, 0, rows - 1)
+    choice = row_choice(frames, rows, cols, near, frames * cols, 0)
+    near_row = jnp.dot(
+        jnp.concatenate([total, theirs], axis=0),
+        choice,
+        preferred_element_type=jnp.float32,
+        precision=lax.Precision.HIGHEST,
+    )
+    beside = near_row[:NARROW]
+    for head in range(HEADS):
+        side = head % 2 * NARROW
+        mapped = rim_ref[head // 2][:, side : side + NARROW].astype(jnp.float32)
+        beside = beside + mapped * near_row[NARROW + head : NARROW + head + 1]
+    beside_ref[...] = packed_latents(beside)
+
+
+def packed_latents(latents):
+    half = latents.shape[1] // 2
+    packed = jnp.concatenate([latents[:, :half], latents[:, half:]], axis=0)
+    return packed.T.astype(jnp.bfloat16)
+
+
+def merge_kernel(got_ref, mapped_ref, beside_ref, out_ref):
     total = got_ref[0:NARROW, :]
     for head in range(HEADS):
         total = total + mapped_ref[head] * got_ref[NARROW + head : NARROW + head + 1, :]
-    half = total.shape[1] // 2
-    packed = jnp.concatenate([total[:, :half], total[:, half:]], axis=0).T
-    out_ref[...] = packed.astype(jnp.bfloat16)
-    grid = packed.reshape(frames // 2, rows, cols, 2 * NARROW)
-    rim = jnp.where(rank_ref[0] == 0, grid[:, rows - 1], grid[:, 0])
-    rim_ref[...] = rim.reshape(-1, 2 * NARROW).astype(jnp.bfloat16)
+    own = total.shape[1] // 2
+    out_ref[0:own, :] = packed_latents(total)
+    out_ref[own:, :] = beside_ref[...]
 
 
 def split_attention(queries, key_states, value_states, kept_tiles, kept_counts, patch_weight, ready):
@@ -122,14 +165,19 @@
     def whole(*shape):
         return pl.BlockSpec(shape, lambda i: (0,) * len(shape))
 
-    def attend(part, start, name):
+    grid = (frames, rows, cols)
+    rank = lax.axis_index("sp").astype(jnp.int32).reshape(1)
+    rim_tokens = frames * cols
+
+    def attend(part, start, name, with_rim=False):
         count = part.shape[1] // HD
         first_block = start // HEAD_BLOCK
         heads = pl.BlockSpec((tokens, HEAD_BLOCK * HD), lambda i: (0, first_block + i))
         return pl.pallas_call(
-            functools.partial(attend_kernel, start),
+            functools.partial(attend_kernel, start, grid),
             grid=(count // HEAD_BLOCK,),
             in_specs=[
+                smem,
                 smem,
                 smem,
                 pl.BlockSpec((tokens, HEAD_BLOCK * HD), lambda i: (0, i)),
@@ -140,11 +188,13 @@
             out_specs=[
                 whole(count, tokens),
                 pl.BlockSpec((HEAD_BLOCK, NARROW, tokens), lambda i: (i, 0, 0)),
-            ],
+                pl.BlockSpec((HEAD_BLOCK // 2, NARROW, 2 * rim_tokens), lambda i: (i, 0, 0)),
+            ][: 3 if with_rim else 2],
             out_shape=[
                 jax.ShapeDtypeStruct((count, tokens), jnp.float32),
                 jax.ShapeDtypeStruct((count, NARROW, tokens), jnp.float32),
-            ],
+                jax.ShapeDtypeStruct((count // 2, NARROW, 2 * rim_tokens), jnp.bfloat16),
+            ][: 3 if with_rim else 2],
             compiler_params=params,
             cost_estimate=pl.CostEstimate(
                 flops=4 * count * tokens * tokens * HD,
@@ -152,11 +202,12 @@
                 transcendentals=count * tokens * tokens,
             ),
             name=name,
-        )(kept_tiles, kept_counts, part, flat_key, flat_value, patch_weight)
-
-    level, mapped = attend(flat_query, 0, "own_queries")
+        )(rank, kept_tiles, kept_counts, part, flat_key, flat_value, patch_weight)
+
+    level, mapped, rim = attend(flat_query, 0, "own_queries", with_rim=True)
     level, ready = lax.optimization_barrier((level, ready))
     other_level = lax.ppermute(level, "sp", swap)
+    other_rim = lax.ppermute(rim, "sp", swap)
     levels, shares = [], []
     for part, start in zip(other_queries, starts):
         if levels:
@@ -164,31 +215,30 @@
         part_level, share = attend(part, start, "other_queries")
         levels.append(part_level)
         shares.append(share)
-    sent = pl.pallas_call(
-        functools.partial(combine_kernel, len(levels)),
+    operands = (other_level, other_rim, *levels, *shares)
+    sent, beside = pl.pallas_call(
+        functools.partial(combine_kernel, len(levels), grid),
         grid=(1,),
-        in_specs=[whole(*part.shape) for part in (other_level, *levels, *shares)],
-        out_specs=whole(NARROW + HEADS, tokens),
-        out_shape=jax.ShapeDtypeStruct((NARROW + HEADS, tokens), jnp.float32),
+        in_specs=[smem] + [whole(*part.shape) for part in operands],
+        out_specs=[whole(NARROW + HEADS, tokens), whole(rim_tokens // 2, 2 * NARROW)],
+        out_shape=[
+            jax.ShapeDtypeStruct((NARROW + HEADS, tokens), jnp.float32),
+            jax.ShapeDtypeStruct((rim_tokens // 2, 2 * NARROW), jnp.bfloat16),
+        ],
         compiler_params=params,
         name="combine",
-    )(other_level, *levels, *shares)
+    )(rank, *operands)
     got = lax.ppermute(sent, "sp", swap)
-    rank = lax.axis_index("sp").astype(jnp.int32).reshape(1)
-    rim_tokens = frames // 2 * cols
-    latent, rim = pl.pallas_call(
-        functools.partial(merge_kernel, frames, rows, cols),
+    message = pl.pallas_call(
+        merge_kernel,
         grid=(1,),
-        in_specs=[smem, whole(NARROW + HEADS, tokens), whole(HEADS, NARROW, tokens)],
-        out_specs=[whole(tokens // 2, 2 * NARROW), whole(rim_tokens, 2 * NARROW)],
-        out_shape=[
-            jax.ShapeDtypeStruct((tokens // 2, 2 * NARROW), jnp.bfloat16),
-            jax.ShapeDtypeStruct((rim_tokens, 2 * NARROW), jnp.bfloat16),
-        ],
+        in_specs=[whole(*part.shape) for part in (got, mapped, beside)],
+        out_specs=whole((tokens + rim_tokens) // 2, 2 * NARROW),
+        out_shape=jax.ShapeDtypeStruct(((tokens + rim_tokens) // 2, 2 * NARROW), jnp.bfloat16),
         compiler_params=params,
         name="merge",
-    )(rank, got, mapped)
-    return latent, rim, ready
+    )(got, mapped, beside)
+    return message, ready
 
 
 def to_tiles(grid, tile_size):
@@ -287,7 +337,10 @@
     latent = latent.astype(jnp.bfloat16)
     packed = jnp.concatenate([latent[: tokens // 2], latent[tokens // 2 :]], axis=1)
     grid = packed.reshape(frame_count // 2, local_rows, token_cols, 2 * NARROW)
-    return packed, grid[:, 0].reshape(-1, 2 * NARROW), grid[:, -1].reshape(-1, 2 * NARROW)
+    above = lax.ppermute(grid[:, -1], "sp", [(i, i + 1) for i in range(sp_count - 1)])
+    below = lax.ppermute(grid[:, 0], "sp", [(i + 1, i) for i in range(sp_count - 1)])
+    rims = [rim.reshape(-1, 2 * NARROW) for rim in (above, below)]
+    return jnp.concatenate([packed, *rims], axis=0)
 
 
 def spread_kernel(plain_ref, out_ref):
@@ -319,11 +372,10 @@
     rows,
     cols,
     place_ref,
-    own_ref,
-    above_ref,
-    below_ref,
+    message_refs,
     weight_hbm,
-    kernel_hbm,
+    mine_refs,
+    theirs_refs,
     out_ref,
     token_ref,
     pair_ref,
@@ -336,17 +388,30 @@
 ):
     at_first = place_ref[0] == 0
     at_last = place_ref[0] == place_ref[1] - 1
-    copies = [
-        pltpu.make_async_copy(weight_hbm, weight_ref, sems.at[0]),
-        pltpu.make_async_copy(kernel_hbm, kernel_ref, sems.at[1]),
-    ]
+    step = place_ref[2]
+    half = place_ref[3]
+    copies = [pltpu.make_async_copy(weight_hbm, weight_ref, sems.at[0])]
+    tap = 0
+    for mine_ref, theirs_ref in zip(mine_refs, theirs_refs):
+        taps = pl.ds(tap, mine_ref.shape[1])
+        for part_ref, side in ((mine_ref, half), (theirs_ref, 1 - half)):
+            copies.append(
+                pltpu.make_async_copy(part_ref, kernel_ref.at[side, :, taps], sems.at[len(copies)])
+            )
+        tap += mine_ref.shape[1]
     for copy in copies:
         copy.start()
 
     lane = lax.broadcasted_iota(jnp.int32, (1, 1, 1, 2 * NARROW), 3)
 
-    def unpacked(ref, height):
-        plain = ref[...].astype(jnp.float32)
+    message = message_refs[0][...]
+    for k in range(1, len(message_refs)):
+        message = jnp.where(step == k, message_refs[k][...], message)
+    own_count = frames // 2 * rows * cols
+    rim_count = frames // 2 * cols
+
+    def unpacked(packed, height):
+        plain = packed.astype(jnp.float32)
         turned = pltpu.roll(plain, NARROW, 1)
         shape = (frames // 2, height, cols, 2 * NARROW)
         plain, turned = plain.reshape(shape), turned.reshape(shape)
@@ -354,9 +419,9 @@
         late = jnp.where(lane < NARROW, turned, plain)
         return jnp.concatenate([early, late], axis=0)
 
-    token_ref[:, 1 : 1 + rows, 8 : 8 + cols, :] = unpacked(own_ref, rows)
-    above = unpacked(above_ref, 1)
-    below = above if below_ref is above_ref else unpacked(below_ref, 1)
+    token_ref[:, 1 : 1 + rows, 8 : 8 + cols, :] = unpacked(message[:own_count], rows)
+    above = unpacked(message[own_count : own_count + rim_count], 1)
+    below = unpacked(message[-rim_count:], 1)
     for f in range(frames):
         edge = pltpu.roll(token_ref[f, 1, 8 : 8 + cols, :], 2 * LAT, 1)
         token_ref[f, 0, 8 : 8 + cols, :] = jnp.where(at_first, edge, above[f, 0])
@@ -430,7 +495,14 @@
         for dy in range(3):
             window = wide_ref[dt : dt + frames, dy : dy + height].reshape(cells, 3 * CH)
             weight = jnp.concatenate(
-                [kernel_ref[:, (dt * 3 + dy) * 3 + dz].reshape(CH, CH) for dz in range(3)], axis=0
+                [
+                    jnp.concatenate(
+                        [kernel_ref[side, :, (dt * 3 + dy) * 3 + dz].reshape(CH, CH // 2) for side in range(2)],
+                        axis=1,
+                    )
+                    for dz in range(3)
+                ],
+                axis=0,
             )
             product = jnp.dot(window, weight, preferred_element_type=jnp.float32)
             total = product if total is None else total + product
@@ -441,24 +513,27 @@
         out_ref[:, :, :, lanes] = (total[:, :, :, lanes] + residual).astype(jnp.bfloat16)
 
 
-def decode(frames, rows, cols, place, own, rims, weights, kernel):
+def decode(frames, rows, cols, place, messages, weights, mine, theirs):
     height, width = 2 * rows, 2 * cols
-    small = [own, *rims]
+    count, parts = len(messages), len(mine)
+    groups, _, depth, _ = mine[0].shape
 
     def whole(shape):
         return pl.BlockSpec(shape, lambda i, place: (0,) * len(shape))
 
-    def body(place_ref, own_ref, *refs):
-        above_ref, below_ref = refs[0], refs[len(rims) - 1]
+    def body(place_ref, *refs):
+        message_refs, refs = refs[:count], refs[count:]
+        weight_hbm, mine_refs, theirs_refs = refs[0], refs[1 : 1 + parts], refs[1 + parts : 1 + 2 * parts]
         decode_kernel(
-            frames, rows, cols, place_ref, own_ref, above_ref, below_ref, *refs[len(rims) :]
+            frames, rows, cols, place_ref, message_refs, weight_hbm, mine_refs, theirs_refs,
+            *refs[1 + 2 * parts :],
         )
 
     grid_spec = pltpu.PrefetchScalarGridSpec(
         num_scalar_prefetch=1,
         grid=(1,),
-        in_specs=[whole(part.shape) for part in small]
-        + [pl.BlockSpec(memory_space=pl.ANY)] * 2,
+        in_specs=[whole(part.shape) for part in messages]
+        + [pl.BlockSpec(memory_space=pl.ANY)] * (1 + 2 * parts),
         out_specs=whole((frames, height, width, CH)),
         scratch_shapes=[
             pltpu.VMEM((frames, rows + 2, cols + 16, 2 * NARROW), jnp.float32),
@@ -467,22 +542,22 @@
             pltpu.VMEM((CH // 128, frames, height + 2, width + 16, 128), jnp.float32),
             pltpu.VMEM((frames + 2, height + 2, width, 3 * CH), jnp.bfloat16),
             pltpu.VMEM(weights.shape, jnp.bfloat16),
-            pltpu.VMEM(kernel.shape, jnp.bfloat16),
-            pltpu.SemaphoreType.DMA((2,)),
+            pltpu.VMEM((2, groups, 27, depth, CH // 2), jnp.bfloat16),
+            pltpu.SemaphoreType.DMA((1 + 2 * parts,)),
         ],
     )
     return pl.pallas_call(
         body,
         grid_spec=grid_spec,
         out_shape=jax.ShapeDtypeStruct((frames, height, width, CH), jnp.bfloat16),
-        compiler_params=pltpu.CompilerParams(vmem_limit_bytes=56 * MIB),
+        compiler_params=pltpu.CompilerParams(vmem_limit_bytes=32 * MIB),
         cost_estimate=pl.CostEstimate(
             flops=2 * frames * height * width * 27 * CH * CH,
             bytes_accessed=27 * CH * CH * 2 + frames * height * width * CH * 2,
             transcendentals=frames * height * width * CH,
         ),
         name="decode_block",
-    )(place, *small, weights, kernel)
+    )(place, *messages, weights, *mine, *theirs)
 
 
 def local(
@@ -502,45 +577,33 @@
     segment_count = lax.axis_size("segment")
     segment_rank = lax.axis_index("segment")
 
-    taps, own_channels, channels = second_kernel.shape
-    share = taps * own_channels // segment_count
-    flat = second_kernel.reshape(taps * own_channels, channels)
-    flat = lax.dynamic_slice_in_dim(flat, segment_rank * share, share, 0)
-    kernel = lax.all_gather(flat, ("grp", "segment"), axis=0, tiled=True)
-    kernel = kernel.reshape(-1, taps, own_channels, channels)
+    half = lax.rem(segment_rank, 2)
+    share = lax.dynamic_slice_in_dim(second_kernel, half * (CH // 2), CH // 2, 2)
+    ends = list(itertools.accumulate(TAP_PARTS))
+    mine = [
+        lax.all_gather(share[end - count : end], "grp", axis=0, tiled=False)
+        for end, count in zip(ends, TAP_PARTS)
+    ]
     weights = first_weights(first_kernel)
-    place = jnp.stack([sp_rank, jnp.int32(sp_count)]).astype(jnp.int32)
-    orders = list(itertools.permutations(range(segment_count)))
-    same = jnp.all(decode_slot[None, :] == jnp.array(orders, jnp.int32), axis=1)
-    order = jnp.sum(jnp.where(same, jnp.arange(len(orders), dtype=jnp.int32), 0)).astype(jnp.int32)
+    picks = (decode_slot == segment_rank).astype(jnp.int32)
+    source = jnp.sum(jnp.arange(segment_count, dtype=jnp.int32) * picks)
+    step = lax.rem(segment_rank - source + segment_count, segment_count)
+    place = jnp.stack([sp_rank, jnp.int32(sp_count), step, half]).astype(jnp.int32)
 
     arguments = (queries, key_states, value_states, kept_tiles, kept_counts, patch_weight)
     if sp_count == 2 and rows * sp_count == TH and frames == TT:
-        latent, rim, (weights, place, order) = split_attention(*arguments, (weights, place, order))
-        moves = [(rim, [(0, 1), (1, 0)])]
+        message, (weights, place) = split_attention(*arguments, (weights, place))
     else:
-        latent, top, bottom = exchanged_attention(*arguments)
-        moves = [
-            (bottom, [(i, i + 1) for i in range(sp_count - 1)]),
-            (top, [(i + 1, i) for i in range(sp_count - 1)]),
-        ]
-    moves = [(latent, [(i, i) for i in range(sp_count)])] + moves
-
-    def ordered(slots):
-        def send(*parts):
-            return tuple(
-                lax.ppermute(
-                    part,
-                    ("segment", "sp"),
-                    [(i * sp_count + a, slots[i] * sp_count + b) for i in range(segment_count) for a, b in pairs],
-                )
-                for part, (_, pairs) in zip(parts, moves)
-            )
-
-        return send
-
-    own, *rims = lax.switch(order, [ordered(slots) for slots in orders], *[part for part, _ in moves])
-    return decode(frames, rows, cols, place, own, rims, weights, kernel)[None, None]
+        message = exchanged_attention(*arguments)
+    messages = [message] + [
+        lax.ppermute(message, "segment", [(i, (i + step) % segment_count) for i in range(segment_count)])
+        for step in range(1, segment_count)
+    ]
+    *mine, _ = lax.optimization_barrier((*mine, messages[-1]))
+    theirs = [
+        lax.ppermute(part, "segment", [(i, i ^ 1) for i in range(segment_count)]) for part in mine
+    ]
+    return decode(frames, rows, cols, place, messages, weights, mine, theirs)[None, None]
 
 
 def solution(mesh):

time: 75.7 us -> 92.9 us (1.23)
  blocking collectives: 0 us -> 40.5 us
  between operations: 14.1 us -> 0.74 us
  waiting for transfers between devices: 15.7 us -> 7.34 us
  Pallas kernels: 23 us -> 26.5 us
  starting transfers between devices: 12 us -> 9.67 us
  local copies, waits for them, and re-layouts: 9.02 us -> 7.16 us
    all_gather x0 -> x2, blocking collectives: none -> 40.5 us  [local(): lax.all_gather(share[end - count:end], 'grp', axis=0, tiled=False)]
    all_gather x1 -> x0, waiting for transfers between devices: 6.34 us -> none  [local(): kernel = lax.all_gather(flat, ('grp', 'segment'), axis=0, tiled=True)]
    pallas_call x5 -> x6, Pallas kernels: 12 us -> 16.9 us  [the longest x4 15.2 us: attend(): pl.pallas_call(functools.partial(attend_kernel, start, grid), grid=(count...]
    ppermute x2 -> x3, waiting for transfers between devices: 4.03 us -> 0.01 us  [split_attention(): lax.ppermute(flat_query[:, start * HD:end * HD], 'sp', swap)]
    ppermute x2 -> x6, starting transfers between devices: 5.19 us -> 2.09 us  [the longest x3 1.55 us: local(): lax.ppermute(message, 'segment', [(i, (i + step) % segment_count) for i i...]
    ppermute x2 -> x3, starting transfers between devices: 2.97 us -> 5 us  [split_attention(): lax.ppermute(flat_query[:, start * HD:end * HD], 'sp', swap)]
    ppermute x1, waiting for transfers between devices: 2.14 us -> 3.89 us  [split_attention(): got = lax.ppermute(sent, 'sp', swap)]
    pallas_call x1, Pallas kernels: 8.86 us -> 7.32 us  [decode(): pl.pallas_call(body, grid_spec=grid_spec, out_shape=jax.ShapeDtypeStruct(...]
  transfers between devices with their start and end apart: 7 -> 11, of which waited for: 5 -> 3; matrix products, arithmetic and copies ran while one was open for 7% -> 3% of each run, Pallas kernels for 19% -> 19%
where the time goes in v4:
time: 92.9 us; the launch traced here: 92.6 us
  blocking collectives  40.5 us (44%)
  Pallas kernels  26.5 us (29%)
  starting transfers between devices  9.67 us (10%)
  waiting for transfers between devices  7.34 us (8%)
  local copies, waits for them, and re-layouts  7.16 us (8%)
    all_gather x2, blocking collectives, local(): lax.all_gather(share[end - count:end], 'grp', axis=0, tiled=False)  40.5 us
    pallas_call x4, Pallas kernels, attend(): pl.pallas_call(functools.partial(attend_kernel, start, grid), grid=(count...  15.2 us
    pallas_call x1, Pallas kernels, decode(): pl.pallas_call(body, grid_spec=grid_spec, out_shape=jax.ShapeDtypeStruct(...  7.32 us
    ppermute x3, starting transfers between devices, split_attention(): lax.ppermute(flat_query[:, start * HD:end * HD], 'sp', swap)  5 us
    ppermute x1, waiting for transfers between devices, split_attention(): got = lax.ppermute(sent, 'sp', swap)  3.89 us
    slice x2, local copies, waits for them, and re-layouts, split_attention(): flat_query[:, start * HD:end * HD]  3.89 us
    ppermute x3, waiting for transfers between devices, local(): lax.ppermute(message, 'segment', [(i, (i + step) % segment_count) for i i...  3.43 us
    unnamed x26, local copies, waits for them, and re-layouts  3.19 us
  transfers between devices with their start and end apart: 11, of which 3 were waited for; matrix products, arithmetic and copies ran while one was open for 3% of the time, Pallas kernels for 19%

profile of v4, /device:TPU:0, one launch (start us, length us, event | category | flops | bytes accessed | tf_op | source)
XLA Modules:
  0.0 92.6 jit_solution(15692635992909293048)
XLA Ops:
  0.0 0.0 copy-start
  0.0 0.0 copy-start.1
  0.0 2.0 %fusion.1 = (bf16[256,512]{1,0:T(8,128)(2,1)}, bf16[256,512]{1,0:T(8,128)(2,1)}) fusion(bf16[256,2048]{1,0:T(8,128)(2,1)} %bitcast.24), kind=kLoop, calls=%fused_computation.5 | loop fusion | bytes 1048576 | tf_op jit(solution)/shard_map/slice | solution.py:155
  2.0 3.0 %collective-permute-start.4 = (bf16[256,512]{1,0:T(8,128)(2,1)}, bf16[256,512]{1,0:T(8,128)(2,1)S(1)}, u32[]{:S(2)}, u32[]{:S(2)}) collective-permute-start(bf16[256,512]{1,0:T(8,128)(2,1)} %get-tuple-element.41), channel_id=1, source_target_pairs={{0,1},{1,0},{2,3},{3,2},{4,5},{5,4},{6,7},{7,6},{8,9},{9,8},{10,11... | collective-permute-start | bytes 786440 | tf_op jit(solution)/shard_map/ppermute | solution.py:155
  5.0 0.0 collective-permute-start.2
  5.1 1.9 %slice.21 = bf16[256,1024]{1,0:T(8,128)(2,1)} slice(bf16[256,2048]{1,0:T(8,128)(2,1)} %bitcast.25), slice={[0:256], [512:1536]} | slice | bytes 1048576 | tf_op jit(solution)/shard_map/slice | solution.py:155
  6.9 2.0 %collective-permute-start.3 = (bf16[256,1024]{1,0:T(8,128)(2,1)}, bf16[256,1024]{1,0:T(8,128)(2,1)}, u32[]{:S(2)}, u32[]{:S(2)}) collective-permute-start(bf16[256,1024]{1,0:T(8,128)(2,1)} %slice.21), channel_id=1, source_target_pairs={{0,1},{1,0},{2,3},{3,2},{4,5},{5,4},{6,7},{7,6},{8,9},{9,8},{10,11... | collective-permute-start | bytes 1572872 | tf_op jit(solution)/shard_map/ppermute | solution.py:155
  8.9 0.0 copy-done.11
  8.9 0.0 copy-done.10
  8.9 0.0 copy-done.2
  8.9 0.0 copy-done.1
  8.9 0.0 copy-start.3
  8.9 0.9 %copy-done.3 = bf16[2048,64]{0,1:T(8,128)(2,1)S(1)} copy-done((bf16[2048,64]{0,1:T(8,128)(2,1)S(1)}, bf16[2048,64]{0,1:T(8,128)(2,1)}, u32[]{:S(2)}) %copy-start.3) | copy-done | bytes 262168
  9.9 1.2 %copy-done.5 = bf16[1,1,4,4,16,2048]{5,4,3,2,1,0:T(8,128)(2,1)S(1)} copy-done((bf16[1,1,4,4,16,2048]{5,4,3,2,1,0:T(8,128)(2,1)S(1)}, bf16[1,1,4,4,16,2048]{5,4,3,2,1,0:T(8,128)(2,1)}, u32[]{:S(2)}) %copy-start.5) | copy-done | bytes 1048600
  11.1 8.0 %own_queries.1 = (f32[16,256]{1,0:T(8,128)S(1)}, f32[16,64,256]{2,1,0:T(8,128)S(1)}, bf16[8,64,128]{2,1,0:T(8,128)(2,1)}) custom-call(s32[1]{0:T(128)} %bitcast.rank_ref, s32[2,2,16]{2,1,0:T(2,128)S(1)} %bitcast.31, s32[2,16]{1,0:T(2,128)S(1)} %bitcast.35, bf16[256,2048]{1,0:T(8,128)(2,1)S(1)} %bitcast.26, bf16[256,2048]{1,0:T(8,128)(2,1)S(1)} %bitcast.12, ...), custom_call_target="tpu_custom_call" | custom-call | flops 536870912 | bytes 3145728 | tf_op jit(solution)/shard_map/own_queries/pallas_call | solution.py:176
  19.1 1.0 %copy-done.7 = f32[16,64,256]{2,1,0:T(8,128)} copy-done((f32[16,64,256]{2,1,0:T(8,128)}, f32[16,64,256]{2,1,0:T(8,128)S(1)}, u32[]{:S(2)}) %copy-start.7) | copy-done | bytes 1048600
  20.1 0.0 collective-permute-start.1
  20.2 0.0 copy-done.12
  20.2 0.6 fusion
  21.4 0.1 pad_add_fusion.place_ref
  21.5 2.3 %spread_first_kernel.1.refs_4_ = bf16[2,768,512]{2,1,0:T(8,128)(2,1)} custom-call(bf16[27,16,256]{2,1,0:T(8,128)(2,1)} %plain_ref.1), custom_call_target="tpu_custom_call" | custom-call | tf_op jit(solution)/shard_map/spread_first_kernel/pallas_call | solution.py:360
  23.7 2.0 %collective-permute-start = (f32[16,256]{1,0:T(8,128)S(1)}, f32[16,256]{1,0:T(8,128)S(1)}, u32[]{:S(2)}, u32[]{:S(2)}) collective-permute-start(f32[16,256]{1,0:T(8,128)S(1)} %get-tuple-element.25), channel_id=1, source_target_pairs={{0,1},{1,0},{2,3},{3,2},{4,5},{5,4},{6,7},{7,6},{8,9},{9,8},{10,11... | collective-permute-start | bytes 49160 | tf_op jit(solution)/shard_map/ppermute | solution.py:209
  25.8 22.6 %all-gather = bf16[60,64,128]{2,1,0:T(8,128)(2,1)} all-gather(bf16[15,64,128]{2,1,0:T(8,128)(2,1)S(1)} %constant_dynamic-slice_fusion), channel_id=2, replica_groups=mesh['segment'=4,'grp'=4,'sp'=2] {'grp'}, dimensions={0}, use_global_device_ids=true | all-gather | bytes 1228800 | tf_op jit(solution)/shard_map/all_gather | solution.py:584
  48.3 0.0 collective-permute-done.2.q_ref
  48.4 2.1 %other_queries.3 = (f32[4,256]{1,0:T(4,128)S(1)}, f32[4,64,256]{2,1,0:T(8,128)S(1)}) custom-call(s32[1]{0:T(128)} %bitcast.rank_ref, s32[2,2,16]{2,1,0:T(2,128)S(1)} %bitcast.32, s32[2,16]{1,0:T(2,128)S(1)} %bitcast.36, bf16[256,512]{1,0:T(8,128)(2,1)} %collective-permute-done.2.q_ref, bf16[256,2048]{1,0:T(8,128)(2,1)S(1)} %bitcast.13, ...), custom_call_target="tpu_custom_call" | custom-call | flops 134217728 | bytes 786432 | tf_op jit(solution)/shard_map/other_queries/pallas_call | solution.py:176
  50.5 0.0 collective-permute-done.3.q_ref
  50.5 3.3 %other_queries.4 = (f32[8,256]{1,0:T(8,128)S(1)}, f32[8,64,256]{2,1,0:T(8,128)S(1)}) custom-call(s32[1]{0:T(128)} %bitcast.rank_ref, s32[2,2,16]{2,1,0:T(2,128)S(1)} %bitcast.33, s32[2,16]{1,0:T(2,128)S(1)} %bitcast.37, bf16[256,1024]{1,0:T(8,128)(2,1)} %collective-permute-done.3.q_ref, bf16[256,2048]{1,0:T(8,128)(2,1)S(1)} %bitcast.14, ...), custom_call_target="tpu_custom_call" | custom-call | flops 268435456 | bytes 1572864 | tf_op jit(solution)/shard_map/other_queries/pallas_call | solution.py:176
  53.8 0.0 collective-permute-done.4.q_ref
  53.9 1.7 %other_queries.5 = (f32[4,256]{1,0:T(4,128)S(1)}, f32[4,64,256]{2,1,0:T(8,128)S(1)}) custom-call(s32[1]{0:T(128)} %bitcast.rank_ref, s32[2,2,16]{2,1,0:T(2,128)S(1)} %bitcast.34, s32[2,16]{1,0:T(2,128)S(1)} %bitcast.38, bf16[256,512]{1,0:T(8,128)(2,1)S(1)} %collective-permute-done.4.q_ref, bf16[256,2048]{1,0:T(8,128)(2,1)S(1)} %bitcast.15, ...), custom_call_target="tpu_custom_call" | custom-call | flops 134217728 | bytes 786432 | tf_op jit(solution)/shard_map/other_queries/pallas_call | solution.py:176
  55.6 0.0 collective-permute-done.theirs_ref
  55.6 0.0 collective-permute-done.1.rim_ref
  55.6 1.6 %combine.1 = (f32[80,256]{1,0:T(8,128)S(1)}, bf16[32,128]{1,0:T(8,128)(2,1)S(1)}) custom-call(s32[1]{0:T(128)} %bitcast.rank_ref, f32[16,256]{1,0:T(8,128)S(1)} %collective-permute-done.theirs_ref, bf16[8,64,128]{2,1,0:T(8,128)(2,1)} %collective-permute-done.1.rim_ref, f32[4,256]{1,0:T(4,128)S(1)} %get-tuple-element.27.refs_0_, ...), custom_call_target="tpu_custom_call" | custom-call | tf_op jit(solution)/shard_map/combine/pallas_call | solution.py:219
  57.2 0.0 copy-start.6
  57.2 0.6 collective-permute-start.5
  57.8 3.9 %collective-permute-done.5.got_ref = f32[80,256]{1,0:T(8,128)S(1)} collective-permute-done((f32[80,256]{1,0:T(8,128)S(1)}, f32[80,256]{1,0:T(8,128)S(1)}, u32[]{:S(2)}, u32[]{:S(2)}) %collective-permute-start.5) | collective-permute-done | bytes 81952 | tf_op jit(solution)/shard_map/ppermute | solution.py:231
  61.7 0.2 merge.1.refs_0_
  61.9 0.1 collective-permute-start.8
  61.9 17.9 %all-gather.1 = bf16[48,64,128]{2,1,0:T(8,128)(2,1)S(1)} all-gather(bf16[12,64,128]{2,1,0:T(8,128)(2,1)S(1)} %constant_dynamic-slice_fusion.1), channel_id=3, replica_groups=mesh['segment'=4,'grp'=4,'sp'=2] {'grp'}, dimensions={0}, use_global_device_ids=true | all-gather | bytes 983040 | tf_op jit(solution)/shard_map/all_gather | solution.py:584
  79.8 0.0 collective-permute-done.8.refs_3_
  79.8 0.0 collective-permute-start.9
  79.8 0.5 collective-permute-start.10
  80.3 1.5 %collective-permute-start.7 = (bf16[160,128]{1,0:T(8,128)(2,1)S(1)}, bf16[160,128]{1,0:T(8,128)(2,1)S(1)}, u32[]{:S(2)}, u32[]{:S(2)}) collective-permute-start(bf16[160,128]{1,0:T(8,128)(2,1)S(1)} %merge.1.refs_0_), channel_id=1, source_target_pairs={{0,16},{8,24},{16,0},{24,8},{1,17},{9,25},{17,1},{25,9},{2,18},{10... | collective-permute-start | bytes 122888 | tf_op jit(solution)/shard_map/ppermute | solution.py:599
  81.8 0.0 collective-permute-start.6
  81.8 2.5 %collective-permute-done.7.refs_2_ = bf16[160,128]{1,0:T(8,128)(2,1)S(1)} collective-permute-done((bf16[160,128]{1,0:T(8,128)(2,1)S(1)}, bf16[160,128]{1,0:T(8,128)(2,1)S(1)}, u32[]{:S(2)}, u32[]{:S(2)}) %collective-permute-start.7) | collective-permute-done | bytes 40992 | tf_op jit(solution)/shard_map/ppermute | solution.py:599
  84.3 0.9 collective-permute-done.6.refs_1_
  85.3 0.0 collective-permute-done.10.refs_8_
  85.3 0.0 collective-permute-done.9.refs_7_
  85.3 7.3 %decode_block.1 = bf16[4,8,32,256]{3,2,1,0:T(8,128)(2,1)} custom-call(s32[4]{0:T(128)S(1)} %pad_add_fusion.place_ref, bf16[160,128]{1,0:T(8,128)(2,1)S(1)} %merge.1.refs_0_, bf16[160,128]{1,0:T(8,128)(2,1)S(1)} %collective-permute-done.6.refs_1_, bf16[160,128]{1,0:T(8,128)(2,1)S(1)} %collective-permute-done.7.refs_2_, ...), custom_call_target="tpu_custom_call" | custom-call | flops 3623878656 | bytes 4063232 | tf_op jit(solution)/shard_map/decode_block/pallas_call | solution.py:549
  (16 shorter events, 0.1 us)
Async XLA Ops:
  0.0 25.7 %copy-start = (bf16[27,64,256]{2,1,0:T(8,128)(2,1)S(1)}, bf16[27,64,256]{2,1,0:T(8,128)(2,1)}, u32[]{:S(2)}) copy-start(bf16[27,64,256]{2,1,0:T(8,128)(2,1)} %param.17) | copy-start | bytes 2654212
  0.0 8.9 %copy-start.11 = (s32[16,2]{0,1:T(2,128)S(1)}, s32[16,2]{0,1:T(2,128)}, u32[]{:S(2)}) copy-start(s32[16,2]{0,1:T(2,128)} %param.13) | copy-start | bytes 388
  0.0 8.9 %copy-start.10 = (s32[16,2,2]{0,2,1:T(2,128)S(1)}, s32[16,2,2]{0,2,1:T(2,128)}, u32[]{:S(2)}) copy-start(s32[16,2,2]{0,2,1:T(2,128)} %param.12) | copy-start | bytes 772
  0.0 8.9 %copy-start.2 = (bf16[1,1,4,4,16,2048]{5,4,3,2,1,0:T(8,128)(2,1)S(1)}, bf16[1,1,4,4,16,2048]{5,4,3,2,1,0:T(8,128)(2,1)}, u32[]{:S(2)}) copy-start(bf16[1,1,4,4,16,2048]{5,4,3,2,1,0:T(8,128)(2,1)} %param.11) | copy-start | bytes 3145732
  0.0 8.9 %copy-start.1 = (bf16[1,1,4,4,16,2048]{5,4,3,2,1,0:T(8,128)(2,1)S(1)}, bf16[1,1,4,4,16,2048]{5,4,3,2,1,0:T(8,128)(2,1)}, u32[]{:S(2)}) copy-start(bf16[1,1,4,4,16,2048]{5,4,3,2,1,0:T(8,128)(2,1)} %param.10) | copy-start | bytes 3145732
  2.0 51.8 %collective-permute-start.4 = (bf16[256,512]{1,0:T(8,128)(2,1)}, bf16[256,512]{1,0:T(8,128)(2,1)S(1)}, u32[]{:S(2)}, u32[]{:S(2)}) collective-permute-start(bf16[256,512]{1,0:T(8,128)(2,1)} %get-tuple-element.41), channel_id=1, source_target_pairs={{0,1},{1,0},{2,3},{3,2},{4,5},{5,4},{6,7},{7,6},{8,9},{9,8},{10,11... | collective-permute-start | bytes 786440 | tf_op jit(solution)/shard_map/ppermute | solution.py:155
  5.0 43.3 %collective-permute-start.2 = (bf16[256,512]{1,0:T(8,128)(2,1)}, bf16[256,512]{1,0:T(8,128)(2,1)}, u32[]{:S(2)}, u32[]{:S(2)}) collective-permute-start(bf16[256,512]{1,0:T(8,128)(2,1)} %get-tuple-element.42), channel_id=1, source_target_pairs={{0,1},{1,0},{2,3},{3,2},{4,5},{5,4},{6,7},{7,6},{8,9},{9,8},{10,11... | collective-permute-start | bytes 786440 | tf_op jit(solution)/shard_map/ppermute | solution.py:155
  6.9 43.6 %collective-permute-start.3 = (bf16[256,1024]{1,0:T(8,128)(2,1)}, bf16[256,1024]{1,0:T(8,128)(2,1)}, u32[]{:S(2)}, u32[]{:S(2)}) collective-permute-start(bf16[256,1024]{1,0:T(8,128)(2,1)} %slice.21), channel_id=1, source_target_pairs={{0,1},{1,0},{2,3},{3,2},{4,5},{5,4},{6,7},{7,6},{8,9},{9,8},{10,11... | collective-permute-start | bytes 1572872 | tf_op jit(solution)/shard_map/ppermute | solution.py:155
  8.9 1.0 %copy-start.3 = (bf16[2048,64]{0,1:T(8,128)(2,1)S(1)}, bf16[2048,64]{0,1:T(8,128)(2,1)}, u32[]{:S(2)}) copy-start(bf16[2048,64]{0,1:T(8,128)(2,1)} %param.14) | copy-start | bytes 786436
  9.9 1.2 %copy-start.5 = (bf16[1,1,4,4,16,2048]{5,4,3,2,1,0:T(8,128)(2,1)S(1)}, bf16[1,1,4,4,16,2048]{5,4,3,2,1,0:T(8,128)(2,1)}, u32[]{:S(2)}) copy-start(bf16[1,1,4,4,16,2048]{5,4,3,2,1,0:T(8,128)(2,1)} %param.9) | copy-start | bytes 3145732
  11.1 9.0 %copy-start.12 = (s32[4]{0:T(128)S(1)}, s32[4]{0:T(128)}, u32[]{:S(2)}) copy-start(s32[4]{0:T(128)} %param.15) | copy-start | bytes 52
  19.1 1.0 %copy-start.7 = (f32[16,64,256]{2,1,0:T(8,128)}, f32[16,64,256]{2,1,0:T(8,128)S(1)}, u32[]{:S(2)}) copy-start(f32[16,64,256]{2,1,0:T(8,128)S(1)} %get-tuple-element.36.mapped_ref) | copy-start | bytes 3145732
  20.1 35.5 %collective-permute-start.1 = (bf16[8,64,128]{2,1,0:T(8,128)(2,1)}, bf16[8,64,128]{2,1,0:T(8,128)(2,1)}, u32[]{:S(2)}, u32[]{:S(2)}) collective-permute-start(bf16[8,64,128]{2,1,0:T(8,128)(2,1)} %get-tuple-element.26), channel_id=1, source_target_pairs={{0,1},{1,0},{2,3},{3,2},{4,5},{5,4},{6,7},{7,6},{8,9},{9,8},{10,11... | collective-permute-start | bytes 393224 | tf_op jit(solution)/shard_map/ppermute | solution.py:210
  21.5 26.9 %copy-start.4 = (bf16[2048,64]{0,1:T(8,128)(2,1)S(1)}, bf16[2048,64]{0,1:T(8,128)(2,1)}, u32[]{:S(2)}) copy-start(bf16[2048,64]{0,1:T(8,128)(2,1)} %param.14) | copy-start | bytes 786436
  23.7 31.9 %collective-permute-start = (f32[16,256]{1,0:T(8,128)S(1)}, f32[16,256]{1,0:T(8,128)S(1)}, u32[]{:S(2)}, u32[]{:S(2)}) collective-permute-start(f32[16,256]{1,0:T(8,128)S(1)} %get-tuple-element.25), channel_id=1, source_target_pairs={{0,1},{1,0},{2,3},{3,2},{4,5},{5,4},{6,7},{7,6},{8,9},{9,8},{10,11... | collective-permute-start | bytes 49160 | tf_op jit(solution)/shard_map/ppermute | solution.py:209
  53.8 7.9 %copy-start.8 = (f32[16,64,256]{2,1,0:T(8,128)S(1)}, f32[16,64,256]{2,1,0:T(8,128)}, u32[]{:S(2)}) copy-start(f32[16,64,256]{2,1,0:T(8,128)} %copy-done.7) | copy-start | bytes 3145732
  57.2 22.7 %copy-start.9 = (bf16[60,64,128]{2,1,0:T(8,128)(2,1)S(1)}, bf16[60,64,128]{2,1,0:T(8,128)(2,1)}, u32[]{:S(2)}) copy-start(bf16[60,64,128]{2,1,0:T(8,128)(2,1)} %all-gather) | copy-start | bytes 2949124
  57.2 28.1 %copy-start.6 = (bf16[2,768,512]{2,1,0:T(8,128)(2,1)S(1)}, bf16[2,768,512]{2,1,0:T(8,128)(2,1)}, u32[]{:S(2)}) copy-start(bf16[2,768,512]{2,1,0:T(8,128)(2,1)} %spread_first_kernel.1.refs_4_) | copy-start | bytes 4718596
  57.2 4.5 %collective-permute-start.5 = (f32[80,256]{1,0:T(8,128)S(1)}, f32[80,256]{1,0:T(8,128)S(1)}, u32[]{:S(2)}, u32[]{:S(2)}) collective-permute-start(f32[80,256]{1,0:T(8,128)S(1)} %get-tuple-element.35), channel_id=1, source_target_pairs={{0,1},{1,0},{2,3},{3,2},{4,5},{5,4},{6,7},{7,6},{8,9},{9,8},{10,11... | collective-permute-start | bytes 245768 | tf_op jit(solution)/shard_map/ppermute | solution.py:231
  61.9 18.0 %collective-permute-start.8 = (bf16[160,128]{1,0:T(8,128)(2,1)S(1)}, bf16[160,128]{1,0:T(8,128)(2,1)S(1)}, u32[]{:S(2)}, u32[]{:S(2)}) collective-permute-start(bf16[160,128]{1,0:T(8,128)(2,1)S(1)} %merge.1.refs_0_), channel_id=1, source_target_pairs={{0,24},{8,0},{16,8},{24,16},{1,25},{9,1},{17,9},{25,17},{2,26},{10... | collective-permute-start | bytes 122888 | tf_op jit(solution)/shard_map/ppermute | solution.py:599
  79.8 5.4 %collective-permute-start.9 = (bf16[4,15,64,128]{3,2,1,0:T(8,128)(2,1)S(1)}, bf16[4,15,64,128]{3,2,1,0:T(8,128)(2,1)S(1)}, u32[]{:S(2)}, u32[]{:S(2)}) collective-permute-start(bf16[4,15,64,128]{3,2,1,0:T(8,128)(2,1)S(1)} %bitcast.27), channel_id=1, source_target_pairs={{0,8},{8,0},{16,24},{24,16},{1,9},{9,1},{17,25},{25,17},{2,10},{10... | collective-permute-start | bytes 2949128 | tf_op jit(solution)/shard_map/ppermute | solution.py:604
  79.8 5.4 %collective-permute-start.10 = (bf16[4,12,64,128]{3,2,1,0:T(8,128)(2,1)S(1)}, bf16[4,12,64,128]{3,2,1,0:T(8,128)(2,1)S(1)}, u32[]{:S(2)}, u32[]{:S(2)}) collective-permute-start(bf16[4,12,64,128]{3,2,1,0:T(8,128)(2,1)S(1)} %bitcast.29), channel_id=1, source_target_pairs={{0,8},{8,0},{16,24},{24,16},{1,9},{9,1},{17,25},{25,17},{2,10},{10... | collective-permute-start | bytes 2359304 | tf_op jit(solution)/shard_map/ppermute | solution.py:604
  80.3 4.0 %collective-permute-start.7 = (bf16[160,128]{1,0:T(8,128)(2,1)S(1)}, bf16[160,128]{1,0:T(8,128)(2,1)S(1)}, u32[]{:S(2)}, u32[]{:S(2)}) collective-permute-start(bf16[160,128]{1,0:T(8,128)(2,1)S(1)} %merge.1.refs_0_), channel_id=1, source_target_pairs={{0,16},{8,24},{16,0},{24,8},{1,17},{9,25},{17,1},{25,9},{2,18},{10... | collective-permute-start | bytes 122888 | tf_op jit(solution)/shard_map/ppermute | solution.py:599
  81.8 3.4 %collective-permute-start.6 = (bf16[160,128]{1,0:T(8,128)(2,1)S(1)}, bf16[160,128]{1,0:T(8,128)(2,1)S(1)}, u32[]{:S(2)}, u32[]{:S(2)}) collective-permute-start(bf16[160,128]{1,0:T(8,128)(2,1)S(1)} %merge.1.refs_0_), channel_id=1, source_target_pairs={{0,8},{8,16},{16,24},{24,0},{1,9},{9,17},{17,25},{25,1},{2,10},{10... | collective-permute-start | bytes 122888 | tf_op jit(solution)/shard_map/ppermute | solution.py:599

commit v5 on v4

--- a/solution.py
+++ b/solution.py
@@ -20,7 +20,6 @@
 SCORE_UNIT = HD**-0.5 * 1.4426950408889634
 HEAD_BLOCK = 4
 HEAD_PARTS = (4, 8, 4)
-TAP_PARTS = (15, 12)
 NARROW = 4 * LAT
 MIB = 1 << 20
 
@@ -64,10 +63,11 @@
 
 
 def attend_kernel(
-    offset, grid, rank_ref, tiles_ref, counts_ref, q_ref, k_ref, v_ref, w_ref, level_ref, mapped_ref, *rim_refs
+    offset, grid, rank_ref, tiles_ref, counts_ref, q_ref, k_ref, v_ref, w_ref, level_ref, mapped_ref, *note_refs
 ):
     block = pl.program_id(0)
-    if rim_refs:
+    if note_refs:
+        note_ref = note_refs[0]
         frames, rows, cols = grid
         near = jnp.where(rank_ref[0] == 0, rows - 1, 0)
         choices = [
@@ -84,18 +84,33 @@
         level_ref[pl.ds(row, 1), :] = top + jnp.log2(total)
         mapped = jnp.dot(w_ref[:, cols], out, preferred_element_type=jnp.float32)
         mapped_ref[i] = mapped
-        if rim_refs:
+        if note_refs:
             rim = jnp.dot(mapped.astype(jnp.bfloat16), choices[i % 2], preferred_element_type=jnp.float32)
             if i % 2 == 0:
                 even = rim
             else:
-                rim_refs[0][i // 2] = (even + rim).astype(jnp.bfloat16)
-
-
-def combine_kernel(parts, grid, rank_ref, theirs_ref, rim_ref, *refs):
-    level_refs, mapped_refs = refs[:parts], refs[parts : 2 * parts]
-    sent_ref, beside_ref = refs[2 * parts :]
-    theirs = theirs_ref[...]
+                pair = pl.multiple_of((row // 2) * NARROW, NARROW)
+                note_ref[pl.ds(pair, NARROW), :] = (even + rim).astype(jnp.bfloat16)
+    if note_refs:
+
+        @pl.when(block == pl.num_programs(0) - 1)
+        def _():
+            rest = level_ref[...]
+            rest = jnp.concatenate([rest[:, :128], rest[:, 128:]], axis=0)
+            start = HEADS // 2 * NARROW
+            for _ in range(3):
+                part = rest.astype(jnp.bfloat16)
+                note_ref[start : start + 2 * HEADS, :] = part
+                rest = rest - part.astype(jnp.float32)
+                start += 2 * HEADS
+
+
+def combine_kernel(parts, note_ref, *refs):
+    level_refs, mapped_refs, sent_ref = refs[:parts], refs[parts : 2 * parts], refs[-1]
+    start = HEADS // 2 * NARROW
+    theirs = [note_ref[start + k * 2 * HEADS : start + (k + 1) * 2 * HEADS, :] for k in range(3)]
+    theirs = theirs[0].astype(jnp.float32) + theirs[1].astype(jnp.float32) + theirs[2].astype(jnp.float32)
+    theirs = jnp.concatenate([theirs[:HEADS], theirs[HEADS:]], axis=1)
     mine = jnp.concatenate([ref[...] for ref in level_refs], axis=0)
     high = jnp.maximum(mine, theirs)
     level = high + jnp.log2(jnp.exp2(mine - high) + jnp.exp2(theirs - high))
@@ -107,14 +122,16 @@
             term = ref[i] * mine[head : head + 1]
             total = term if total is None else total + term
             head += 1
-    theirs = jnp.exp2(theirs - level)
     sent_ref[0:NARROW, :] = total
-    sent_ref[NARROW:, :] = theirs
+    sent_ref[NARROW:, :] = jnp.exp2(theirs - level)
+
+
+def beside_kernel(grid, rank_ref, sent_ref, note_ref, beside_ref):
     frames, rows, cols = grid
     near = jnp.where(rank_ref[0] == 0, 0, rows - 1)
     choice = row_choice(frames, rows, cols, near, frames * cols, 0)
     near_row = jnp.dot(
-        jnp.concatenate([total, theirs], axis=0),
+        sent_ref[...],
         choice,
         preferred_element_type=jnp.float32,
         precision=lax.Precision.HIGHEST,
@@ -122,7 +139,8 @@
     beside = near_row[:NARROW]
     for head in range(HEADS):
         side = head % 2 * NARROW
-        mapped = rim_ref[head // 2][:, side : side + NARROW].astype(jnp.float32)
+        pair = head // 2 * NARROW
+        mapped = note_ref[pair : pair + NARROW, side : side + NARROW].astype(jnp.float32)
         beside = beside + mapped * near_row[NARROW + head : NARROW + head + 1]
     beside_ref[...] = packed_latents(beside)
 
@@ -151,9 +169,13 @@
     swap = [(0, 1), (1, 0)]
     ends = list(itertools.accumulate(HEAD_PARTS))
     starts = [0] + ends[:-1]
-    other_queries = [
-        lax.ppermute(flat_query[:, start * HD : end * HD], "sp", swap) for start, end in zip(starts, ends)
-    ]
+    parts = []
+    source = flat_query
+    for start, end in zip(starts, ends):
+        parts.append(source[:, start * HD : end * HD])
+        if start == 0:
+            source, _ = lax.optimization_barrier((source, parts[0]))
+    other_queries = [lax.ppermute(part, "sp", swap) for part in parts]
     kept_tiles = kept_tiles.transpose(1, 2, 0)
     kept_counts = kept_counts.T
     patch_weight = patch_weight.T
@@ -169,7 +191,9 @@
     rank = lax.axis_index("sp").astype(jnp.int32).reshape(1)
     rim_tokens = frames * cols
 
-    def attend(part, start, name, with_rim=False):
+    note_rows = HEADS // 2 * NARROW + 6 * HEADS
+
+    def attend(part, start, name, with_note=False):
         count = part.shape[1] // HD
         first_block = start // HEAD_BLOCK
         heads = pl.BlockSpec((tokens, HEAD_BLOCK * HD), lambda i: (0, first_block + i))
@@ -188,47 +212,50 @@
             out_specs=[
                 whole(count, tokens),
                 pl.BlockSpec((HEAD_BLOCK, NARROW, tokens), lambda i: (i, 0, 0)),
-                pl.BlockSpec((HEAD_BLOCK // 2, NARROW, 2 * rim_tokens), lambda i: (i, 0, 0)),
-            ][: 3 if with_rim else 2],
+                whole(note_rows, 2 * NARROW),
+            ][: 3 if with_note else 2],
             out_shape=[
                 jax.ShapeDtypeStruct((count, tokens), jnp.float32),
                 jax.ShapeDtypeStruct((count, NARROW, tokens), jnp.float32),
-                jax.ShapeDtypeStruct((count // 2, NARROW, 2 * rim_tokens), jnp.bfloat16),
-            ][: 3 if with_rim else 2],
+                jax.ShapeDtypeStruct((note_rows, 2 * NARROW), jnp.bfloat16),
+            ][: 3 if with_note else 2],
             compiler_params=params,
             cost_estimate=pl.CostEstimate(
-                flops=4 * count * tokens * tokens * HD,
-                bytes_accessed=3 * tokens * count * HD * 2,
-                transcendentals=count * tokens * tokens,
+                flops=count * tokens, bytes_accessed=count * tokens, transcendentals=0
             ),
             name=name,
         )(rank, kept_tiles, kept_counts, part, flat_key, flat_value, patch_weight)
 
-    level, mapped, rim = attend(flat_query, 0, "own_queries", with_rim=True)
-    level, ready = lax.optimization_barrier((level, ready))
-    other_level = lax.ppermute(level, "sp", swap)
-    other_rim = lax.ppermute(rim, "sp", swap)
+    flat_query, *_ = lax.optimization_barrier((flat_query, *parts))
+    _, mapped, note = attend(flat_query, 0, "own_queries", with_note=True)
+    note, ready = lax.optimization_barrier((note, ready))
+    other_note = lax.ppermute(note, "sp", swap)
     levels, shares = [], []
     for part, start in zip(other_queries, starts):
-        if levels:
-            part, _ = lax.optimization_barrier((part, levels[-1]))
+        part, _ = lax.optimization_barrier((part, levels[-1] if levels else note))
         part_level, share = attend(part, start, "other_queries")
         levels.append(part_level)
         shares.append(share)
-    operands = (other_level, other_rim, *levels, *shares)
-    sent, beside = pl.pallas_call(
-        functools.partial(combine_kernel, len(levels), grid),
+    operands = (other_note, *levels, *shares)
+    sent = pl.pallas_call(
+        functools.partial(combine_kernel, len(levels)),
         grid=(1,),
-        in_specs=[smem] + [whole(*part.shape) for part in operands],
-        out_specs=[whole(NARROW + HEADS, tokens), whole(rim_tokens // 2, 2 * NARROW)],
-        out_shape=[
-            jax.ShapeDtypeStruct((NARROW + HEADS, tokens), jnp.float32),
-            jax.ShapeDtypeStruct((rim_tokens // 2, 2 * NARROW), jnp.bfloat16),
-        ],
+        in_specs=[whole(*part.shape) for part in operands],
+        out_specs=whole(NARROW + HEADS, tokens),
+        out_shape=jax.ShapeDtypeStruct((NARROW + HEADS, tokens), jnp.float32),
         compiler_params=params,
         name="combine",
-    )(rank, *operands)
+    )(*operands)
     got = lax.ppermute(sent, "sp", swap)
+    beside = pl.pallas_call(
+        functools.partial(beside_kernel, grid),
+        grid=(1,),
+        in_specs=[smem, whole(*sent.shape), whole(*other_note.shape)],
+        out_specs=whole(rim_tokens // 2, 2 * NARROW),
+        out_shape=jax.ShapeDtypeStruct((rim_tokens // 2, 2 * NARROW), jnp.bfloat16),
+        compiler_params=params,
+        name="beside",
+    )(rank, sent, other_note)
     message = pl.pallas_call(
         merge_kernel,
         grid=(1,),
@@ -238,7 +265,7 @@
         compiler_params=params,
         name="merge",
     )(got, mapped, beside)
-    return message, ready
+    return message, got, ready
 
 
 def to_tiles(grid, tile_size):
@@ -374,8 +401,7 @@
     place_ref,
     message_refs,
     weight_hbm,
-    mine_refs,
-    theirs_refs,
+    shard_refs,
     out_ref,
     token_ref,
     pair_ref,
@@ -389,18 +415,25 @@
     at_first = place_ref[0] == 0
     at_last = place_ref[0] == place_ref[1] - 1
     step = place_ref[2]
-    half = place_ref[3]
-    copies = [pltpu.make_async_copy(weight_hbm, weight_ref, sems.at[0])]
-    tap = 0
-    for mine_ref, theirs_ref in zip(mine_refs, theirs_refs):
-        taps = pl.ds(tap, mine_ref.shape[1])
-        for part_ref, side in ((mine_ref, half), (theirs_ref, 1 - half)):
-            copies.append(
-                pltpu.make_async_copy(part_ref, kernel_ref.at[side, :, taps], sems.at[len(copies)])
-            )
-        tap += mine_ref.shape[1]
-    for copy in copies:
-        copy.start()
+    weight_copy = pltpu.make_async_copy(weight_hbm, weight_ref, sems.at[0])
+    weight_copy.start()
+    if len(shard_refs) == 1:
+        shard_copies = [pltpu.make_async_copy(shard_refs[0], kernel_ref, sems.at[1])]
+    else:
+        shard_copies = [
+            pltpu.make_async_copy(ref, kernel_ref.at[place_ref[3 + k]], sems.at[1 + k])
+            for k, ref in enumerate(shard_refs)
+        ]
+    direct = place_ref[3 + len(shard_refs)]
+
+    def each_shard(act):
+        for k, copy in enumerate(shard_copies):
+            if len(shard_copies) - k > 2 or len(shard_copies) == 1:
+                act(copy)
+            else:
+                pl.when(direct == len(shard_copies) - 1 - k)(functools.partial(act, copy))
+
+    each_shard(lambda copy: copy.start())
 
     lane = lax.broadcasted_iota(jnp.int32, (1, 1, 1, 2 * NARROW), 3)
 
@@ -444,7 +477,7 @@
         pair_ref[side, 0] = pair[0]
         pair_ref[side, 1] = pair[0]
 
-    copies[0].wait()
+    weight_copy.wait()
     gaps = rows + 1
     for side in range(2):
         columns = jnp.concatenate(
@@ -487,22 +520,14 @@
             wide_ref[0, :, :, lanes] = shifted[0]
             wide_ref[1, :, :, lanes] = shifted[0]
 
-    for copy in copies[1:]:
-        copy.wait()
+    each_shard(lambda copy: copy.wait())
     cells = frames * height * width
     total = None
     for dt in range(3):
         for dy in range(3):
             window = wide_ref[dt : dt + frames, dy : dy + height].reshape(cells, 3 * CH)
             weight = jnp.concatenate(
-                [
-                    jnp.concatenate(
-                        [kernel_ref[side, :, (dt * 3 + dy) * 3 + dz].reshape(CH, CH // 2) for side in range(2)],
-                        axis=1,
-                    )
-                    for dz in range(3)
-                ],
-                axis=0,
+                [kernel_ref[:, (dt * 3 + dy) * 3 + dz].reshape(CH, CH) for dz in range(3)], axis=0
             )
             product = jnp.dot(window, weight, preferred_element_type=jnp.float32)
             total = product if total is None else total + product
@@ -513,27 +538,26 @@
         out_ref[:, :, :, lanes] = (total[:, :, :, lanes] + residual).astype(jnp.bfloat16)
 
 
-def decode(frames, rows, cols, place, messages, weights, mine, theirs):
+def decode(frames, rows, cols, place, messages, weights, groups, shards):
     height, width = 2 * rows, 2 * cols
-    count, parts = len(messages), len(mine)
-    groups, _, depth, _ = mine[0].shape
+    count = len(messages)
+    taps, depth = shards[0].shape[-3:-1]
 
     def whole(shape):
         return pl.BlockSpec(shape, lambda i, place: (0,) * len(shape))
 
     def body(place_ref, *refs):
         message_refs, refs = refs[:count], refs[count:]
-        weight_hbm, mine_refs, theirs_refs = refs[0], refs[1 : 1 + parts], refs[1 + parts : 1 + 2 * parts]
+        weight_hbm, shard_refs = refs[0], refs[1 : 1 + len(shards)]
         decode_kernel(
-            frames, rows, cols, place_ref, message_refs, weight_hbm, mine_refs, theirs_refs,
-            *refs[1 + 2 * parts :],
+            frames, rows, cols, place_ref, message_refs, weight_hbm, shard_refs, *refs[1 + len(shards) :]
         )
 
     grid_spec = pltpu.PrefetchScalarGridSpec(
         num_scalar_prefetch=1,
         grid=(1,),
         in_specs=[whole(part.shape) for part in messages]
-        + [pl.BlockSpec(memory_space=pl.ANY)] * (1 + 2 * parts),
+        + [pl.BlockSpec(memory_space=pl.ANY)] * (1 + len(shards)),
         out_specs=whole((frames, height, width, CH)),
         scratch_shapes=[
             pltpu.VMEM((frames, rows + 2, cols + 16, 2 * NARROW), jnp.float32),
@@ -542,8 +566,8 @@
             pltpu.VMEM((CH // 128, frames, height + 2, width + 16, 128), jnp.float32),
             pltpu.VMEM((frames + 2, height + 2, width, 3 * CH), jnp.bfloat16),
             pltpu.VMEM(weights.shape, jnp.bfloat16),
-            pltpu.VMEM((2, groups, 27, depth, CH // 2), jnp.bfloat16),
-            pltpu.SemaphoreType.DMA((1 + 2 * parts,)),
+            pltpu.VMEM((groups, taps, depth, CH), jnp.bfloat16),
+            pltpu.SemaphoreType.DMA((1 + len(shards),)),
         ],
     )
     return pl.pallas_call(
@@ -557,7 +581,26 @@
             transcendentals=frames * height * width * CH,
         ),
         name="decode_block",
-    )(place, *messages, weights, *mine, *theirs)
+    )(place, *messages, weights, *shards)
+
+
+def trade_shards(shard, segment_count):
+    segments = range(segment_count)
+    near = [(s * 4 + g, s * 4 + (g ^ (1 + s % 2))) for s in segments for g in range(4)]
+    far = [(s * 4 + g, s * 4 + (g ^ 3)) for s in segments for g in ((1, 2), (0, 3))[s % 2]]
+    return [lax.ppermute(shard, ("segment", "grp"), pairs) for pairs in (near, far)]
+
+
+def swap_shards(near, far, ready, segment_count):
+    near, far, _ = lax.optimization_barrier((near, far, ready))
+    segments = range(segment_count)
+    pairs = [(s * 4 + g, (s ^ 1) * 4 + g) for s in segments for g in ((1, 2), (0, 3))[s % 2]]
+    return (
+        near,
+        lax.ppermute(near, "segment", [(s, s ^ 1) for s in segments]),
+        far,
+        lax.ppermute(far, ("segment", "grp"), pairs),
+    )
 
 
 def local(
@@ -577,33 +620,38 @@
     segment_count = lax.axis_size("segment")
     segment_rank = lax.axis_index("segment")
 
-    half = lax.rem(segment_rank, 2)
-    share = lax.dynamic_slice_in_dim(second_kernel, half * (CH // 2), CH // 2, 2)
-    ends = list(itertools.accumulate(TAP_PARTS))
-    mine = [
-        lax.all_gather(share[end - count : end], "grp", axis=0, tiled=False)
-        for end, count in zip(ends, TAP_PARTS)
-    ]
     weights = first_weights(first_kernel)
     picks = (decode_slot == segment_rank).astype(jnp.int32)
     source = jnp.sum(jnp.arange(segment_count, dtype=jnp.int32) * picks)
     step = lax.rem(segment_rank - source + segment_count, segment_count)
-    place = jnp.stack([sp_rank, jnp.int32(sp_count), step, half]).astype(jnp.int32)
+    group_count = lax.axis_size("grp")
+    group = lax.axis_index("grp")
+    core = lax.rem(segment_rank, 2)
+    line = group_count == 4 and segment_count % 2 == 0
+    places = [sp_rank, jnp.int32(sp_count), step]
+    if line:
+        inner = jnp.logical_or(group == 1, group == 2)
+        places += [group, group ^ (1 + core), group ^ (2 - core), group ^ 3, group ^ 3]
+        places.append((inner == (core == 0)).astype(jnp.int32))
+        traded = trade_shards(second_kernel, segment_count)
+    else:
+        places += [jnp.int32(0)] * 2
+    place = jnp.stack(places).astype(jnp.int32)
 
     arguments = (queries, key_states, value_states, kept_tiles, kept_counts, patch_weight)
     if sp_count == 2 and rows * sp_count == TH and frames == TT:
-        message, (weights, place) = split_attention(*arguments, (weights, place))
+        message, got, (weights, place) = split_attention(*arguments, (weights, place))
     else:
-        message = exchanged_attention(*arguments)
+        message = got = exchanged_attention(*arguments)
+    if line:
+        shards = [second_kernel, *swap_shards(*traded, got, segment_count)]
+    else:
+        shards = [lax.all_gather(second_kernel, "grp", axis=0, tiled=False)]
     messages = [message] + [
         lax.ppermute(message, "segment", [(i, (i + step) % segment_count) for i in range(segment_count)])
         for step in range(1, segment_count)
     ]
-    *mine, _ = lax.optimization_barrier((*mine, messages[-1]))
-    theirs = [
-        lax.ppermute(part, "segment", [(i, i ^ 1) for i in range(segment_count)]) for part in mine
-    ]
-    return decode(frames, rows, cols, place, messages, weights, mine, theirs)[None, None]
+    return decode(frames, rows, cols, place, messages, weights, group_count, shards)[None, None]
 
 
 def solution(mesh):

time: 92.9 us -> 60 us (0.65)
  the two profiles are of different devices: /device:TPU:0 before, /device:TPU:11 now
where the time goes in v5:
time: 60 us; the launch traced here: 59.5 us
  Pallas kernels  26.1 us (44%)
  starting transfers between devices  16.9 us (28%)
  local copies, waits for them, and re-layouts  8.18 us (14%)
  waiting for transfers between devices  6.92 us (12%)
  between operations  0.78 us (1%)
  other arithmetic  0.64 us (1%)
    pallas_call x4, Pallas kernels, attend(): pl.pallas_call(functools.partial(attend_kernel, start, grid), grid=(count...  15.5 us
    pallas_call x1, Pallas kernels, decode(): pl.pallas_call(body, grid_spec=grid_spec, out_shape=jax.ShapeDtypeStruct(...  7.53 us
    slice x3, local copies, waits for them, and re-layouts, split_attention(): parts.append(source[:, start * HD:end * HD])  5.23 us
    ppermute x1, starting transfers between devices, swap_shards(): lax.ppermute(near, 'segment', [(s, s ^ 1) for s in segments])  4.79 us
    ppermute x2, starting transfers between devices, trade_shards(): lax.ppermute(shard, ('segment', 'grp'), pairs)  3.94 us
    ppermute x3, waiting for transfers between devices, local(): lax.ppermute(message, 'segment', [(i, (i + step) % segment_count) for i i...  3.42 us
    unnamed x22, local copies, waits for them, and re-layouts  2.87 us
    ppermute x3, starting transfers between devices, split_attention(): other_queries = [lax.ppermute(part, 'sp', swap) for part in parts]  2.71 us
  transfers between devices with their start and end apart: 12, of which 4 were waited for; matrix products, arithmetic and copies ran while one was open for 10% of the time, Pallas kernels for 31%

profile of v5, /device:TPU:11, one launch (start us, length us, event | category | flops | bytes accessed | tf_op | source)
XLA Modules:
  0.0 59.5 jit_solution(8482882370272830575)
XLA Ops:
  0.0 0.0 copy-start.1
  0.0 2.4 %collective-permute-start.8 = (bf16[27,64,256]{2,1,0:T(8,128)(2,1)}, bf16[27,64,256]{2,1,0:T(8,128)(2,1)}, u32[]{:S(2)}, u32[]{:S(2)}) collective-permute-start(bf16[27,64,256]{2,1,0:T(8,128)(2,1)} %refs_5_.1), channel_id=1, source_target_pairs={{0,2},{2,0},{4,6},{6,4},{8,12},{10,14},{12,8},{14,10},{16,18},{18,... | collective-permute-start | bytes 2654216 | tf_op jit(solution)/shard_map/ppermute | solution.py:591
  2.4 1.6 %collective-permute-start.9 = (bf16[27,64,256]{2,1,0:T(8,128)(2,1)}, bf16[27,64,256]{2,1,0:T(8,128)(2,1)}, u32[]{:S(2)}, u32[]{:S(2)}) collective-permute-start(bf16[27,64,256]{2,1,0:T(8,128)(2,1)} %refs_5_.1), channel_id=1, source_target_pairs={{2,4},{4,2},{8,14},{14,8},{18,20},{20,18},{24,30},{30,24},{3,5},{5... | collective-permute-start | bytes 2654216 | tf_op jit(solution)/shard_map/ppermute | solution.py:591
  4.0 1.7 %slice.12 = bf16[256,512]{1,0:T(8,128)(2,1)} slice(bf16[256,2048]{1,0:T(8,128)(2,1)} %bitcast.26), slice={[0:256], [0:512]} | slice | bytes 524288 | tf_op jit(solution)/shard_map/slice | solution.py:175
  5.6 1.9 %slice.10 = bf16[256,1024]{1,0:T(8,128)(2,1)} slice(bf16[256,2048]{1,0:T(8,128)(2,1)} %bitcast.27), slice={[0:256], [512:1536]} | slice | bytes 1048576 | tf_op jit(solution)/shard_map/slice | solution.py:175
  7.5 1.2 %collective-permute-start.2 = (bf16[256,1024]{1,0:T(8,128)(2,1)}, bf16[256,1024]{1,0:T(8,128)(2,1)}, u32[]{:S(2)}, u32[]{:S(2)}) collective-permute-start(bf16[256,1024]{1,0:T(8,128)(2,1)} %slice.10), channel_id=1, source_target_pairs={{0,1},{1,0},{2,3},{3,2},{4,5},{5,4},{6,7},{7,6},{8,9},{9,8},{10,11... | collective-permute-start | bytes 1572872 | tf_op jit(solution)/shard_map/ppermute | solution.py:178
  8.7 0.2 collective-permute-start.1
  9.0 1.7 %slice.11 = bf16[256,512]{1,0:T(8,128)(2,1)} slice(bf16[256,2048]{1,0:T(8,128)(2,1)} %bitcast.28), slice={[0:256], [1536:2048]} | slice | bytes 524288 | tf_op jit(solution)/shard_map/slice | solution.py:175
  10.7 1.2 %collective-permute-start.3 = (bf16[256,512]{1,0:T(8,128)(2,1)}, bf16[256,512]{1,0:T(8,128)(2,1)}, u32[]{:S(2)}, u32[]{:S(2)}) collective-permute-start(bf16[256,512]{1,0:T(8,128)(2,1)} %slice.11), channel_id=1, source_target_pairs={{0,1},{1,0},{2,3},{3,2},{4,5},{5,4},{6,7},{7,6},{8,9},{9,8},{10,11... | collective-permute-start | bytes 786440 | tf_op jit(solution)/shard_map/ppermute | solution.py:178
  11.9 0.0 copy-done.6
  11.9 0.0 copy-done.1
  11.9 0.0 copy-start.2
  11.9 0.9 %copy-done.2 = bf16[2048,64]{0,1:T(8,128)(2,1)S(1)} copy-done((bf16[2048,64]{0,1:T(8,128)(2,1)S(1)}, bf16[2048,64]{0,1:T(8,128)(2,1)}, u32[]{:S(2)}) %copy-start.2) | copy-done | bytes 262168
  12.9 1.2 %copy-done.4 = bf16[1,1,4,4,16,2048]{5,4,3,2,1,0:T(8,128)(2,1)S(1)} copy-done((bf16[1,1,4,4,16,2048]{5,4,3,2,1,0:T(8,128)(2,1)S(1)}, bf16[1,1,4,4,16,2048]{5,4,3,2,1,0:T(8,128)(2,1)}, u32[]{:S(2)}) %copy-start.4) | copy-done | bytes 1048600
  14.1 8.0 %own_queries.1 = (f32[16,256]{1,0:T(8,128)}, f32[16,64,256]{2,1,0:T(8,128)S(1)}, bf16[608,128]{1,0:T(8,128)(2,1)S(1)}) custom-call(s32[1]{0:T(128)} %bitcast.rank_ref, s32[2,2,16]{2,1,0:T(2,128)S(1)} %bitcast.30, s32[2,16]{1,0:T(2,128)S(1)} %bitcast.34, bf16[256,2048]{1,0:T(8,128)(2,1)S(1)} %bitcast.29, bf16[256,2048]{1,0:T(8,128)(2,1)S(1)} %bitcast.14, ...), custom_call_target="tpu_custom_call" | custom-call | flops 4096 | bytes 4096 | tf_op jit(solution)/shard_map/own_queries/pallas_call | solution.py:200
  22.1 0.7 %copy-done.9 = bf16[608,128]{1,0:T(8,128)(2,1)} copy-done((bf16[608,128]{1,0:T(8,128)(2,1)}, bf16[608,128]{1,0:T(8,128)(2,1)S(1)}, u32[]{:S(2)}) %copy-start.9) | copy-done | bytes 155672
  22.7 0.6 %fusion = s32[]{:T(128)} fusion(s32[4]{0:T(128)S(1)} %copy-done.10, s32[]{:T(128)S(6)} %axis_index.39), kind=kLoop, calls=%fused_computation.1 | loop fusion | flops 11 | bytes 24 | tf_op jit(solution)/shard_map/reduce_sum | solution.py:625
  24.0 2.2 %spread_first_kernel.1.refs_4_ = bf16[2,768,512]{2,1,0:T(8,128)(2,1)} custom-call(bf16[27,16,256]{2,1,0:T(8,128)(2,1)} %plain_ref.1), custom_call_target="tpu_custom_call" | custom-call | tf_op jit(solution)/shard_map/spread_first_kernel/pallas_call | solution.py:387
  26.2 0.1 stack.33.place_ref
  26.3 0.0 collective-permute-done.1.q_ref
  26.3 0.3 collective-permute-start
  26.6 2.1 %other_queries.3 = (f32[4,256]{1,0:T(4,128)S(1)}, f32[4,64,256]{2,1,0:T(8,128)S(1)}) custom-call(s32[1]{0:T(128)} %bitcast.rank_ref, s32[2,2,16]{2,1,0:T(2,128)S(1)} %bitcast.31, s32[2,16]{1,0:T(2,128)S(1)} %bitcast.35, bf16[256,512]{1,0:T(8,128)(2,1)} %collective-permute-done.1.q_ref, bf16[256,2048]{1,0:T(8,128)(2,1)S(1)} %bitcast.15, ...), custom_call_target="tpu_custom_call" | custom-call | flops 1024 | bytes 1024 | tf_op jit(solution)/shard_map/other_queries/pallas_call | solution.py:200
  28.7 0.0 collective-permute-done.2.q_ref
  28.7 3.3 %other_queries.4 = (f32[8,256]{1,0:T(8,128)S(1)}, f32[8,64,256]{2,1,0:T(8,128)S(1)}) custom-call(s32[1]{0:T(128)} %bitcast.rank_ref, s32[2,2,16]{2,1,0:T(2,128)S(1)} %bitcast.32, s32[2,16]{1,0:T(2,128)S(1)} %bitcast.36, bf16[256,1024]{1,0:T(8,128)(2,1)} %collective-permute-done.2.q_ref, bf16[256,2048]{1,0:T(8,128)(2,1)S(1)} %bitcast.16, ...), custom_call_target="tpu_custom_call" | custom-call | flops 2048 | bytes 2048 | tf_op jit(solution)/shard_map/other_queries/pallas_call | solution.py:200
  32.1 0.0 collective-permute-done.3.q_ref
  32.1 2.1 %other_queries.5 = (f32[4,256]{1,0:T(4,128)S(1)}, f32[4,64,256]{2,1,0:T(8,128)S(1)}) custom-call(s32[1]{0:T(128)} %bitcast.rank_ref, s32[2,2,16]{2,1,0:T(2,128)S(1)} %bitcast.33, s32[2,16]{1,0:T(2,128)S(1)} %bitcast.37, bf16[256,512]{1,0:T(8,128)(2,1)} %collective-permute-done.3.q_ref, bf16[256,2048]{1,0:T(8,128)(2,1)S(1)} %bitcast.17, ...), custom_call_target="tpu_custom_call" | custom-call | flops 1024 | bytes 1024 | tf_op jit(solution)/shard_map/other_queries/pallas_call | solution.py:200
  34.2 0.0 copy-start.5
  34.2 0.0 copy-start.8
  34.2 0.0 collective-permute-done.note_ref
  34.2 0.1 combine.1.sent_ref
  34.4 1.3 %collective-permute-start.4 = (f32[80,256]{1,0:T(8,128)S(1)}, f32[80,256]{1,0:T(8,128)S(1)}, u32[]{:S(2)}, u32[]{:S(2)}) collective-permute-start(f32[80,256]{1,0:T(8,128)S(1)} %combine.1.sent_ref), channel_id=1, source_target_pairs={{0,1},{1,0},{2,3},{3,2},{4,5},{5,4},{6,7},{7,6},{8,9},{9,8},{10,11... | collective-permute-start | bytes 245768 | tf_op jit(solution)/shard_map/ppermute | solution.py:249
  35.7 2.4 %collective-permute-done.4.got_ref = f32[80,256]{1,0:T(8,128)S(1)} collective-permute-done((f32[80,256]{1,0:T(8,128)S(1)}, f32[80,256]{1,0:T(8,128)S(1)}, u32[]{:S(2)}, u32[]{:S(2)}) %collective-permute-start.4) | collective-permute-done | bytes 81952 | tf_op jit(solution)/shard_map/ppermute | solution.py:249
  38.1 1.0 %collective-permute-done.8.refs_6_ = bf16[27,64,256]{2,1,0:T(8,128)(2,1)} collective-permute-done((bf16[27,64,256]{2,1,0:T(8,128)(2,1)}, bf16[27,64,256]{2,1,0:T(8,128)(2,1)}, u32[]{:S(2)}, u32[]{:S(2)}) %collective-permute-start.8) | collective-permute-done | bytes 884768 | tf_op jit(solution)/shard_map/ppermute | solution.py:591
  39.2 0.0 collective-permute-done.9.refs_8_
  39.2 4.8 %collective-permute-start.10 = (bf16[27,64,256]{2,1,0:T(8,128)(2,1)}, bf16[27,64,256]{2,1,0:T(8,128)(2,1)S(1)}, u32[]{:S(2)}, u32[]{:S(2)}) collective-permute-start(bf16[27,64,256]{2,1,0:T(8,128)(2,1)} %collective-permute-done.8.refs_6_), channel_id=1, source_target_pairs={{0,8},{8,0},{16,24},{24,16},{1,9},{9,1},{17,25},{25,17},{2,10},{10... | collective-permute-start | bytes 2654216 | tf_op jit(solution)/shard_map/ppermute | solution.py:600
  44.0 1.3 %collective-permute-start.11 = (bf16[27,64,256]{2,1,0:T(8,128)(2,1)}, bf16[27,64,256]{2,1,0:T(8,128)(2,1)S(1)}, u32[]{:S(2)}, u32[]{:S(2)}) collective-permute-start(bf16[27,64,256]{2,1,0:T(8,128)(2,1)} %collective-permute-done.9.refs_8_), channel_id=1, source_target_pairs={{2,10},{4,12},{8,0},{14,6},{18,26},{20,28},{24,16},{30,22},{3,11},... | collective-permute-start | bytes 2654216 | tf_op jit(solution)/shard_map/ppermute | solution.py:602
  45.3 0.5 beside.1.beside_ref
  45.8 0.2 merge.1.refs_0_
  46.0 1.4 %collective-permute-start.5 = (bf16[160,128]{1,0:T(8,128)(2,1)S(1)}, bf16[160,128]{1,0:T(8,128)(2,1)S(1)}, u32[]{:S(2)}, u32[]{:S(2)}) collective-permute-start(bf16[160,128]{1,0:T(8,128)(2,1)S(1)} %merge.1.refs_0_), channel_id=1, source_target_pairs={{0,8},{8,16},{16,24},{24,0},{1,9},{9,17},{17,25},{25,1},{2,10},{10... | collective-permute-start | bytes 122888 | tf_op jit(solution)/shard_map/ppermute | solution.py:651
  47.3 1.2 %collective-permute-start.6 = (bf16[160,128]{1,0:T(8,128)(2,1)S(1)}, bf16[160,128]{1,0:T(8,128)(2,1)S(1)}, u32[]{:S(2)}, u32[]{:S(2)}) collective-permute-start(bf16[160,128]{1,0:T(8,128)(2,1)S(1)} %merge.1.refs_0_), channel_id=1, source_target_pairs={{0,16},{8,24},{16,0},{24,8},{1,17},{9,25},{17,1},{25,9},{2,18},{10... | collective-permute-start | bytes 122888 | tf_op jit(solution)/shard_map/ppermute | solution.py:651
  48.5 0.0 collective-permute-start.7
  48.5 0.0 collective-permute-done.5.refs_1_
  48.6 2.4 %collective-permute-done.6.refs_2_ = bf16[160,128]{1,0:T(8,128)(2,1)S(1)} collective-permute-done((bf16[160,128]{1,0:T(8,128)(2,1)S(1)}, bf16[160,128]{1,0:T(8,128)(2,1)S(1)}, u32[]{:S(2)}, u32[]{:S(2)}) %collective-permute-start.6) | collective-permute-done | bytes 40992 | tf_op jit(solution)/shard_map/ppermute | solution.py:651
  50.9 1.0 %collective-permute-done.7.refs_3_ = bf16[160,128]{1,0:T(8,128)(2,1)S(1)} collective-permute-done((bf16[160,128]{1,0:T(8,128)(2,1)S(1)}, bf16[160,128]{1,0:T(8,128)(2,1)S(1)}, u32[]{:S(2)}, u32[]{:S(2)}) %collective-permute-start.7) | collective-permute-done | bytes 40992 | tf_op jit(solution)/shard_map/ppermute | solution.py:651
  52.0 0.0 collective-permute-done.10.refs_7_
  52.0 0.0 collective-permute-done.11.refs_9_
  52.0 0.0 copy-done.8
  52.0 7.5 %decode_block.1 = bf16[4,8,32,256]{3,2,1,0:T(8,128)(2,1)} custom-call(s32[9]{0:T(128)S(1)} %stack.33.place_ref, bf16[160,128]{1,0:T(8,128)(2,1)S(1)} %merge.1.refs_0_, bf16[160,128]{1,0:T(8,128)(2,1)S(1)} %collective-permute-done.5.refs_1_, bf16[160,128]{1,0:T(8,128)(2,1)S(1)} %collective-permute-done.6.refs_2_, ...), custom_call_target="tpu_custom_call" | custom-call | flops 3623878656 | bytes 4063232 | tf_op jit(solution)/shard_map/decode_block/pallas_call | solution.py:573
  (12 shorter events, 0.0 us)
Async XLA Ops:
  0.0 11.9 %copy-start.6 = (s32[16,2,2]{0,2,1:T(2,128)S(1)}, s32[16,2,2]{0,2,1:T(2,128)}, u32[]{:S(2)}) copy-start(s32[16,2,2]{0,2,1:T(2,128)} %param.12) | copy-start | bytes 772
  0.0 11.9 %copy-start.7 = (s32[16,2]{0,1:T(2,128)S(1)}, s32[16,2]{0,1:T(2,128)}, u32[]{:S(2)}) copy-start(s32[16,2]{0,1:T(2,128)} %param.13) | copy-start | bytes 388
  0.0 11.9 %copy-start = (bf16[1,1,4,4,16,2048]{5,4,3,2,1,0:T(8,128)(2,1)S(1)}, bf16[1,1,4,4,16,2048]{5,4,3,2,1,0:T(8,128)(2,1)}, u32[]{:S(2)}) copy-start(bf16[1,1,4,4,16,2048]{5,4,3,2,1,0:T(8,128)(2,1)} %param.10) | copy-start | bytes 3145732
  0.0 11.9 %copy-start.1 = (bf16[1,1,4,4,16,2048]{5,4,3,2,1,0:T(8,128)(2,1)S(1)}, bf16[1,1,4,4,16,2048]{5,4,3,2,1,0:T(8,128)(2,1)}, u32[]{:S(2)}) copy-start(bf16[1,1,4,4,16,2048]{5,4,3,2,1,0:T(8,128)(2,1)} %param.11) | copy-start | bytes 3145732
  0.0 39.1 %collective-permute-start.8 = (bf16[27,64,256]{2,1,0:T(8,128)(2,1)}, bf16[27,64,256]{2,1,0:T(8,128)(2,1)}, u32[]{:S(2)}, u32[]{:S(2)}) collective-permute-start(bf16[27,64,256]{2,1,0:T(8,128)(2,1)} %refs_5_.1), channel_id=1, source_target_pairs={{0,2},{2,0},{4,6},{6,4},{8,12},{10,14},{12,8},{14,10},{16,18},{18,... | collective-permute-start | bytes 2654216 | tf_op jit(solution)/shard_map/ppermute | solution.py:591
  2.4 36.8 %collective-permute-start.9 = (bf16[27,64,256]{2,1,0:T(8,128)(2,1)}, bf16[27,64,256]{2,1,0:T(8,128)(2,1)}, u32[]{:S(2)}, u32[]{:S(2)}) collective-permute-start(bf16[27,64,256]{2,1,0:T(8,128)(2,1)} %refs_5_.1), channel_id=1, source_target_pairs={{2,4},{4,2},{8,14},{14,8},{18,20},{20,18},{24,30},{30,24},{3,5},{5... | collective-permute-start | bytes 2654216 | tf_op jit(solution)/shard_map/ppermute | solution.py:591
  7.5 21.2 %collective-permute-start.2 = (bf16[256,1024]{1,0:T(8,128)(2,1)}, bf16[256,1024]{1,0:T(8,128)(2,1)}, u32[]{:S(2)}, u32[]{:S(2)}) collective-permute-start(bf16[256,1024]{1,0:T(8,128)(2,1)} %slice.10), channel_id=1, source_target_pairs={{0,1},{1,0},{2,3},{3,2},{4,5},{5,4},{6,7},{7,6},{8,9},{9,8},{10,11... | collective-permute-start | bytes 1572872 | tf_op jit(solution)/shard_map/ppermute | solution.py:178
  8.7 17.6 %collective-permute-start.1 = (bf16[256,512]{1,0:T(8,128)(2,1)}, bf16[256,512]{1,0:T(8,128)(2,1)}, u32[]{:S(2)}, u32[]{:S(2)}) collective-permute-start(bf16[256,512]{1,0:T(8,128)(2,1)} %slice.12), channel_id=1, source_target_pairs={{0,1},{1,0},{2,3},{3,2},{4,5},{5,4},{6,7},{7,6},{8,9},{9,8},{10,11... | collective-permute-start | bytes 786440 | tf_op jit(solution)/shard_map/ppermute | solution.py:178
  10.7 21.4 %collective-permute-start.3 = (bf16[256,512]{1,0:T(8,128)(2,1)}, bf16[256,512]{1,0:T(8,128)(2,1)}, u32[]{:S(2)}, u32[]{:S(2)}) collective-permute-start(bf16[256,512]{1,0:T(8,128)(2,1)} %slice.11), channel_id=1, source_target_pairs={{0,1},{1,0},{2,3},{3,2},{4,5},{5,4},{6,7},{7,6},{8,9},{9,8},{10,11... | collective-permute-start | bytes 786440 | tf_op jit(solution)/shard_map/ppermute | solution.py:178
  11.9 1.0 %copy-start.2 = (bf16[2048,64]{0,1:T(8,128)(2,1)S(1)}, bf16[2048,64]{0,1:T(8,128)(2,1)}, u32[]{:S(2)}) copy-start(bf16[2048,64]{0,1:T(8,128)(2,1)} %param.14) | copy-start | bytes 786436
  12.9 1.2 %copy-start.4 = (bf16[1,1,4,4,16,2048]{5,4,3,2,1,0:T(8,128)(2,1)S(1)}, bf16[1,1,4,4,16,2048]{5,4,3,2,1,0:T(8,128)(2,1)}, u32[]{:S(2)}) copy-start(bf16[1,1,4,4,16,2048]{5,4,3,2,1,0:T(8,128)(2,1)} %param.9) | copy-start | bytes 3145732
  14.1 8.7 %copy-start.10 = (s32[4]{0:T(128)S(1)}, s32[4]{0:T(128)}, u32[]{:S(2)}) copy-start(s32[4]{0:T(128)} %param.15) | copy-start | bytes 52
  22.1 0.7 %copy-start.9 = (bf16[608,128]{1,0:T(8,128)(2,1)}, bf16[608,128]{1,0:T(8,128)(2,1)S(1)}, u32[]{:S(2)}) copy-start(bf16[608,128]{1,0:T(8,128)(2,1)S(1)} %get-tuple-element.27) | copy-start | bytes 466948
  22.7 3.9 %copy-start.3 = (bf16[2048,64]{0,1:T(8,128)(2,1)S(1)}, bf16[2048,64]{0,1:T(8,128)(2,1)}, u32[]{:S(2)}) copy-start(bf16[2048,64]{0,1:T(8,128)(2,1)} %param.14) | copy-start | bytes 786436
  26.3 7.9 %collective-permute-start = (bf16[608,128]{1,0:T(8,128)(2,1)}, bf16[608,128]{1,0:T(8,128)(2,1)S(1)}, u32[]{:S(2)}, u32[]{:S(2)}) collective-permute-start(bf16[608,128]{1,0:T(8,128)(2,1)} %copy-done.9), channel_id=1, source_target_pairs={{0,1},{1,0},{2,3},{3,2},{4,5},{5,4},{6,7},{7,6},{8,9},{9,8},{10,11... | collective-permute-start | bytes 466952 | tf_op jit(solution)/shard_map/ppermute | solution.py:232
  34.2 17.8 %copy-start.5 = (bf16[2,768,512]{2,1,0:T(8,128)(2,1)S(1)}, bf16[2,768,512]{2,1,0:T(8,128)(2,1)}, u32[]{:S(2)}) copy-start(bf16[2,768,512]{2,1,0:T(8,128)(2,1)} %spread_first_kernel.1.refs_4_) | copy-start | bytes 4718596
  34.2 17.8 %copy-start.8 = (bf16[27,64,256]{2,1,0:T(8,128)(2,1)S(1)}, bf16[27,64,256]{2,1,0:T(8,128)(2,1)}, u32[]{:S(2)}) copy-start(bf16[27,64,256]{2,1,0:T(8,128)(2,1)} %refs_5_.1) | copy-start | bytes 2654212
  34.4 3.8 %collective-permute-start.4 = (f32[80,256]{1,0:T(8,128)S(1)}, f32[80,256]{1,0:T(8,128)S(1)}, u32[]{:S(2)}, u32[]{:S(2)}) collective-permute-start(f32[80,256]{1,0:T(8,128)S(1)} %combine.1.sent_ref), channel_id=1, source_target_pairs={{0,1},{1,0},{2,3},{3,2},{4,5},{5,4},{6,7},{7,6},{8,9},{9,8},{10,11... | collective-permute-start | bytes 245768 | tf_op jit(solution)/shard_map/ppermute | solution.py:249
  39.2 12.8 %collective-permute-start.10 = (bf16[27,64,256]{2,1,0:T(8,128)(2,1)}, bf16[27,64,256]{2,1,0:T(8,128)(2,1)S(1)}, u32[]{:S(2)}, u32[]{:S(2)}) collective-permute-start(bf16[27,64,256]{2,1,0:T(8,128)(2,1)} %collective-permute-done.8.refs_6_), channel_id=1, source_target_pairs={{0,8},{8,0},{16,24},{24,16},{1,9},{9,1},{17,25},{25,17},{2,10},{10... | collective-permute-start | bytes 2654216 | tf_op jit(solution)/shard_map/ppermute | solution.py:600
  44.0 8.0 %collective-permute-start.11 = (bf16[27,64,256]{2,1,0:T(8,128)(2,1)}, bf16[27,64,256]{2,1,0:T(8,128)(2,1)S(1)}, u32[]{:S(2)}, u32[]{:S(2)}) collective-permute-start(bf16[27,64,256]{2,1,0:T(8,128)(2,1)} %collective-permute-done.9.refs_8_), channel_id=1, source_target_pairs={{2,10},{4,12},{8,0},{14,6},{18,26},{20,28},{24,16},{30,22},{3,11},... | collective-permute-start | bytes 2654216 | tf_op jit(solution)/shard_map/ppermute | solution.py:602
  46.0 2.6 %collective-permute-start.5 = (bf16[160,128]{1,0:T(8,128)(2,1)S(1)}, bf16[160,128]{1,0:T(8,128)(2,1)S(1)}, u32[]{:S(2)}, u32[]{:S(2)}) collective-permute-start(bf16[160,128]{1,0:T(8,128)(2,1)S(1)} %merge.1.refs_0_), channel_id=1, source_target_pairs={{0,8},{8,16},{16,24},{24,0},{1,9},{9,17},{17,25},{25,1},{2,10},{10... | collective-permute-start | bytes 122888 | tf_op jit(solution)/shard_map/ppermute | solution.py:651
  47.3 3.6 %collective-permute-start.6 = (bf16[160,128]{1,0:T(8,128)(2,1)S(1)}, bf16[160,128]{1,0:T(8,128)(2,1)S(1)}, u32[]{:S(2)}, u32[]{:S(2)}) collective-permute-start(bf16[160,128]{1,0:T(8,128)(2,1)S(1)} %merge.1.refs_0_), channel_id=1, source_target_pairs={{0,16},{8,24},{16,0},{24,8},{1,17},{9,25},{17,1},{25,9},{2,18},{10... | collective-permute-start | bytes 122888 | tf_op jit(solution)/shard_map/ppermute | solution.py:651
  48.5 3.4 %collective-permute-start.7 = (bf16[160,128]{1,0:T(8,128)(2,1)S(1)}, bf16[160,128]{1,0:T(8,128)(2,1)S(1)}, u32[]{:S(2)}, u32[]{:S(2)}) collective-permute-start(bf16[160,128]{1,0:T(8,128)(2,1)S(1)} %merge.1.refs_0_), channel_id=1, source_target_pairs={{0,24},{8,0},{16,8},{24,16},{1,25},{9,1},{17,9},{25,17},{2,26},{10... | collective-permute-start | bytes 122888 | tf_op jit(solution)/shard_map/ppermute | solution.py:651

commit v6 on v5

--- a/solution.py
+++ b/solution.py
@@ -19,7 +19,7 @@
 VAE_SCALE = 1.0 / 0.476986
 SCORE_UNIT = HD**-0.5 * 1.4426950408889634
 HEAD_BLOCK = 4
-HEAD_PARTS = (4, 8, 4)
+HEAD_PARTS = (16,)
 NARROW = 4 * LAT
 MIB = 1 << 20
 
@@ -122,8 +122,16 @@
             term = ref[i] * mine[head : head + 1]
             total = term if total is None else total + term
             head += 1
-    sent_ref[0:NARROW, :] = total
-    sent_ref[NARROW:, :] = jnp.exp2(theirs - level)
+    theirs = jnp.exp2(theirs - level)
+    high = theirs.astype(jnp.bfloat16)
+    sent_ref[0:NARROW, :] = total.astype(jnp.bfloat16)
+    sent_ref[NARROW : NARROW + HEADS, :] = high
+    sent_ref[NARROW + HEADS :, :] = (theirs - high.astype(jnp.float32)).astype(jnp.bfloat16)
+
+
+def unpacked_share(sent_ref):
+    sent = sent_ref[...].astype(jnp.float32)
+    return sent[:NARROW], sent[NARROW : NARROW + HEADS] + sent[NARROW + HEADS :]
 
 
 def beside_kernel(grid, rank_ref, sent_ref, note_ref, beside_ref):
@@ -131,17 +139,15 @@
     near = jnp.where(rank_ref[0] == 0, 0, rows - 1)
     choice = row_choice(frames, rows, cols, near, frames * cols, 0)
     near_row = jnp.dot(
-        sent_ref[...],
-        choice,
-        preferred_element_type=jnp.float32,
-        precision=lax.Precision.HIGHEST,
+        sent_ref[...], choice.astype(jnp.bfloat16), preferred_element_type=jnp.float32
     )
     beside = near_row[:NARROW]
+    weights = near_row[NARROW : NARROW + HEADS] + near_row[NARROW + HEADS :]
     for head in range(HEADS):
         side = head % 2 * NARROW
         pair = head // 2 * NARROW
         mapped = note_ref[pair : pair + NARROW, side : side + NARROW].astype(jnp.float32)
-        beside = beside + mapped * near_row[NARROW + head : NARROW + head + 1]
+        beside = beside + mapped * weights[head : head + 1]
     beside_ref[...] = packed_latents(beside)
 
 
@@ -152,9 +158,9 @@
 
 
 def merge_kernel(got_ref, mapped_ref, beside_ref, out_ref):
-    total = got_ref[0:NARROW, :]
+    total, weights = unpacked_share(got_ref)
     for head in range(HEADS):
-        total = total + mapped_ref[head] * got_ref[NARROW + head : NARROW + head + 1, :]
+        total = total + mapped_ref[head] * weights[head : head + 1]
     own = total.shape[1] // 2
     out_ref[0:own, :] = packed_latents(total)
     out_ref[own:, :] = beside_ref[...]
@@ -241,8 +247,8 @@
         functools.partial(combine_kernel, len(levels)),
         grid=(1,),
         in_specs=[whole(*part.shape) for part in operands],
-        out_specs=whole(NARROW + HEADS, tokens),
-        out_shape=jax.ShapeDtypeStruct((NARROW + HEADS, tokens), jnp.float32),
+        out_specs=whole(NARROW + 2 * HEADS, tokens),
+        out_shape=jax.ShapeDtypeStruct((NARROW + 2 * HEADS, tokens), jnp.bfloat16),
         compiler_params=params,
         name="combine",
     )(*operands)
@@ -265,7 +271,7 @@
         compiler_params=params,
         name="merge",
     )(got, mapped, beside)
-    return message, got, ready
+    return message, ready
 
 
 def to_tiles(grid, tile_size):
@@ -640,11 +646,11 @@
 
     arguments = (queries, key_states, value_states, kept_tiles, kept_counts, patch_weight)
     if sp_count == 2 and rows * sp_count == TH and frames == TT:
-        message, got, (weights, place) = split_attention(*arguments, (weights, place))
+        message, (weights, place) = split_attention(*arguments, (weights, place))
     else:
-        message = got = exchanged_attention(*arguments)
+        message = exchanged_attention(*arguments)
     if line:
-        shards = [second_kernel, *swap_shards(*traded, got, segment_count)]
+        shards = [second_kernel, *swap_shards(*traded, message, segment_count)]
     else:
         shards = [lax.all_gather(second_kernel, "grp", axis=0, tiled=False)]
     messages = [message] + [

time: 60 us -> 58.7 us (0.978)
  the two profiles are of different devices: /device:TPU:11 before, /device:TPU:17 now
where the time goes in v6:
time: 58.7 us; the launch traced here: 58.3 us
  Pallas kernels  24.2 us (41%)
  starting transfers between devices  14 us (24%)
  waiting for transfers between devices  12 us (20%)
  local copies, waits for them, and re-layouts  6.76 us (12%)
  between operations  0.77 us (1%)
  other arithmetic  0.64 us (1%)
    pallas_call x2, Pallas kernels, attend(): pl.pallas_call(functools.partial(attend_kernel, start, grid), grid=(count...  13.7 us
    pallas_call x1, Pallas kernels, decode(): pl.pallas_call(body, grid_spec=grid_spec, out_shape=jax.ShapeDtypeStruct(...  7.53 us
    unnamed x30, local copies, waits for them, and re-layouts  6.68 us
    ppermute x1, starting transfers between devices, swap_shards(): lax.ppermute(near, 'segment', [(s, s ^ 1) for s in segments])  5.53 us
    ppermute x2, waiting for transfers between devices, trade_shards(): lax.ppermute(shard, ('segment', 'grp'), pairs)  4.1 us
    ppermute x3, waiting for transfers between devices, local(): lax.ppermute(message, 'segment', [(i, (i + step) % segment_count) for i i...  3.21 us
    ppermute x1, waiting for transfers between devices, split_attention(): other_queries = [lax.ppermute(part, 'sp', swap) for part in parts]  3.03 us
    ppermute x3, starting transfers between devices, local(): lax.ppermute(message, 'segment', [(i, (i + step) % segment_count) for i i...  2.8 us
  transfers between devices with their start and end apart: 10, of which 6 were waited for; matrix products, arithmetic and copies ran while one was open for 1% of the time, Pallas kernels for 29%

profile of v6, /device:TPU:17, one launch (start us, length us, event | category | flops | bytes accessed | tf_op | source)
XLA Modules:
  0.0 58.3 jit_solution(6705442811207178248)
XLA Ops:
  0.0 1.2 %collective-permute-start.1 = (bf16[256,2048]{1,0:T(8,128)(2,1)}, bf16[256,2048]{1,0:T(8,128)(2,1)}, u32[]{:S(2)}, u32[]{:S(2)}) collective-permute-start(bf16[256,2048]{1,0:T(8,128)(2,1)} %bitcast.20), channel_id=1, source_target_pairs={{0,1},{1,0},{2,3},{3,2},{4,5},{5,4},{6,7},{7,6},{8,9},{9,8},{10,11... | collective-permute-start | bytes 3145736 | tf_op jit(solution)/shard_map/ppermute | solution.py:184
  1.2 0.1 collective-permute-start.6
  1.3 1.6 %collective-permute-start.7 = (bf16[27,64,256]{2,1,0:T(8,128)(2,1)}, bf16[27,64,256]{2,1,0:T(8,128)(2,1)}, u32[]{:S(2)}, u32[]{:S(2)}) collective-permute-start(bf16[27,64,256]{2,1,0:T(8,128)(2,1)} %refs_5_.1), channel_id=1, source_target_pairs={{2,4},{4,2},{8,14},{14,8},{18,20},{20,18},{24,30},{30,24},{3,5},{5... | collective-permute-start | bytes 2654216 | tf_op jit(solution)/shard_map/ppermute | solution.py:597
  2.9 0.0 copy-start
  2.9 1.2 %copy-done = bf16[1,1,4,4,16,2048]{5,4,3,2,1,0:T(8,128)(2,1)S(1)} copy-done((bf16[1,1,4,4,16,2048]{5,4,3,2,1,0:T(8,128)(2,1)S(1)}, bf16[1,1,4,4,16,2048]{5,4,3,2,1,0:T(8,128)(2,1)}, u32[]{:S(2)}) %copy-start) | copy-done | bytes 1048600
  4.1 0.0 copy-start.2
  4.1 1.2 %copy-done.2 = bf16[1,1,4,4,16,2048]{5,4,3,2,1,0:T(8,128)(2,1)S(1)} copy-done((bf16[1,1,4,4,16,2048]{5,4,3,2,1,0:T(8,128)(2,1)S(1)}, bf16[1,1,4,4,16,2048]{5,4,3,2,1,0:T(8,128)(2,1)}, u32[]{:S(2)}) %copy-start.2) | copy-done | bytes 1048600
  5.3 0.9 %copy-done.5 = bf16[2048,64]{0,1:T(8,128)(2,1)S(1)} copy-done((bf16[2048,64]{0,1:T(8,128)(2,1)S(1)}, bf16[2048,64]{0,1:T(8,128)(2,1)}, u32[]{:S(2)}) %copy-start.5) | copy-done | bytes 262168
  6.3 1.2 %copy-done.7 = bf16[1,1,4,4,16,2048]{5,4,3,2,1,0:T(8,128)(2,1)S(1)} copy-done((bf16[1,1,4,4,16,2048]{5,4,3,2,1,0:T(8,128)(2,1)S(1)}, bf16[1,1,4,4,16,2048]{5,4,3,2,1,0:T(8,128)(2,1)}, u32[]{:S(2)}) %copy-start.7) | copy-done | bytes 1048600
  7.5 0.7 %copy-done.8 = s32[16,2,2]{0,2,1:T(2,128)S(1)} copy-done((s32[16,2,2]{0,2,1:T(2,128)S(1)}, s32[16,2,2]{0,2,1:T(2,128)}, u32[]{:S(2)}) %copy-start.8) | copy-done | bytes 280
  8.2 0.7 %copy-done.10 = s32[16,2]{0,1:T(2,128)S(1)} copy-done((s32[16,2]{0,1:T(2,128)S(1)}, s32[16,2]{0,1:T(2,128)}, u32[]{:S(2)}) %copy-start.10) | copy-done | bytes 152
  8.9 8.0 %own_queries.1 = (f32[16,256]{1,0:T(8,128)}, f32[16,64,256]{2,1,0:T(8,128)S(1)}, bf16[608,128]{1,0:T(8,128)(2,1)S(1)}) custom-call(s32[1]{0:T(128)} %bitcast.rank_ref, s32[2,2,16]{2,1,0:T(2,128)S(1)} %bitcast.22, s32[2,16]{1,0:T(2,128)S(1)} %bitcast.24, bf16[256,2048]{1,0:T(8,128)(2,1)S(1)} %bitcast.21, bf16[256,2048]{1,0:T(8,128)(2,1)S(1)} %bitcast.14, ...), custom_call_target="tpu_custom_call" | custom-call | flops 4096 | bytes 4096 | tf_op jit(solution)/shard_map/own_queries/pallas_call | solution.py:206
  16.9 0.7 %copy-done.13 = bf16[608,128]{1,0:T(8,128)(2,1)} copy-done((bf16[608,128]{1,0:T(8,128)(2,1)}, bf16[608,128]{1,0:T(8,128)(2,1)S(1)}, u32[]{:S(2)}) %copy-start.13) | copy-done | bytes 155672
  17.5 0.0 copy-done.14
  17.6 0.6 %fusion = s32[]{:T(128)} fusion(s32[4]{0:T(128)S(1)} %copy-done.14, s32[]{:T(128)S(6)} %axis_index.39), kind=kLoop, calls=%fused_computation.1 | loop fusion | flops 11 | bytes 24 | tf_op jit(solution)/shard_map/reduce_sum | solution.py:631
  18.8 2.2 %spread_first_kernel.1.refs_4_ = bf16[2,768,512]{2,1,0:T(8,128)(2,1)} custom-call(bf16[27,16,256]{2,1,0:T(8,128)(2,1)} %plain_ref.1), custom_call_target="tpu_custom_call" | custom-call | tf_op jit(solution)/shard_map/spread_first_kernel/pallas_call | solution.py:393
  21.0 0.1 stack.33.place_ref
  21.1 0.2 collective-permute-start
  21.3 3.0 %collective-permute-done.1.q_ref = bf16[256,2048]{1,0:T(8,128)(2,1)} collective-permute-done((bf16[256,2048]{1,0:T(8,128)(2,1)}, bf16[256,2048]{1,0:T(8,128)(2,1)}, u32[]{:S(2)}, u32[]{:S(2)}) %collective-permute-start.1) | collective-permute-done | bytes 1048608 | tf_op jit(solution)/shard_map/ppermute | solution.py:184
  24.3 0.0 copy-done.3
  24.3 0.0 copy-done.1
  24.3 0.0 copy-done.6
  24.4 0.0 copy-done.9
  24.4 0.0 copy-done.11
  24.4 5.8 %other_queries.1 = (f32[16,256]{1,0:T(8,128)S(1)}, f32[16,64,256]{2,1,0:T(8,128)S(1)}) custom-call(s32[1]{0:T(128)} %bitcast.rank_ref, s32[2,2,16]{2,1,0:T(2,128)S(1)} %bitcast.23, s32[2,16]{1,0:T(2,128)S(1)} %bitcast.25, bf16[256,2048]{1,0:T(8,128)(2,1)} %collective-permute-done.1.q_ref, bf16[256,2048]{1,0:T(8,128)(2,1)S(1)} %bitcast.15, ...), custom_call_target="tpu_custom_call" | custom-call | flops 4096 | bytes 4096 | tf_op jit(solution)/shard_map/other_queries/pallas_call | solution.py:206
  30.1 0.0 copy-start.4
  30.1 0.0 copy-start.12
  30.2 0.0 collective-permute-done.note_ref
  30.2 0.1 combine.1.sent_ref
  30.3 1.3 %collective-permute-start.2 = (bf16[96,256]{1,0:T(8,128)(2,1)S(1)}, bf16[96,256]{1,0:T(8,128)(2,1)S(1)}, u32[]{:S(2)}, u32[]{:S(2)}) collective-permute-start(bf16[96,256]{1,0:T(8,128)(2,1)S(1)} %combine.1.sent_ref), channel_id=1, source_target_pairs={{0,1},{1,0},{2,3},{3,2},{4,5},{5,4},{6,7},{7,6},{8,9},{9,8},{10,11... | collective-permute-start | bytes 147464 | tf_op jit(solution)/shard_map/ppermute | solution.py:255
  31.6 0.4 beside.1.beside_ref
  32.0 1.7 %collective-permute-done.2.got_ref = bf16[96,256]{1,0:T(8,128)(2,1)S(1)} collective-permute-done((bf16[96,256]{1,0:T(8,128)(2,1)S(1)}, bf16[96,256]{1,0:T(8,128)(2,1)S(1)}, u32[]{:S(2)}, u32[]{:S(2)}) %collective-permute-start.2) | collective-permute-done | bytes 49184 | tf_op jit(solution)/shard_map/ppermute | solution.py:255
  33.7 0.2 merge.1.refs_0_
  33.8 4.1 %collective-permute-done.6.refs_6_ = bf16[27,64,256]{2,1,0:T(8,128)(2,1)} collective-permute-done((bf16[27,64,256]{2,1,0:T(8,128)(2,1)}, bf16[27,64,256]{2,1,0:T(8,128)(2,1)}, u32[]{:S(2)}, u32[]{:S(2)}) %collective-permute-start.6) | collective-permute-done | bytes 884768 | tf_op jit(solution)/shard_map/ppermute | solution.py:597
  37.9 0.0 collective-permute-done.7.refs_8_
  37.9 5.5 %collective-permute-start.8 = (bf16[27,64,256]{2,1,0:T(8,128)(2,1)}, bf16[27,64,256]{2,1,0:T(8,128)(2,1)S(1)}, u32[]{:S(2)}, u32[]{:S(2)}) collective-permute-start(bf16[27,64,256]{2,1,0:T(8,128)(2,1)} %collective-permute-done.6.refs_6_), channel_id=1, source_target_pairs={{0,8},{8,0},{16,24},{24,16},{1,9},{9,1},{17,25},{25,17},{2,10},{10... | collective-permute-start | bytes 2654216 | tf_op jit(solution)/shard_map/ppermute | solution.py:606
  43.5 1.3 %collective-permute-start.9 = (bf16[27,64,256]{2,1,0:T(8,128)(2,1)}, bf16[27,64,256]{2,1,0:T(8,128)(2,1)S(1)}, u32[]{:S(2)}, u32[]{:S(2)}) collective-permute-start(bf16[27,64,256]{2,1,0:T(8,128)(2,1)} %collective-permute-done.7.refs_8_), channel_id=1, source_target_pairs={{2,10},{4,12},{8,0},{14,6},{18,26},{20,28},{24,16},{30,22},{3,11},... | collective-permute-start | bytes 2654216 | tf_op jit(solution)/shard_map/ppermute | solution.py:608
  44.8 2.3 %collective-permute-start.3 = (bf16[160,128]{1,0:T(8,128)(2,1)S(1)}, bf16[160,128]{1,0:T(8,128)(2,1)S(1)}, u32[]{:S(2)}, u32[]{:S(2)}) collective-permute-start(bf16[160,128]{1,0:T(8,128)(2,1)S(1)} %merge.1.refs_0_), channel_id=1, source_target_pairs={{0,8},{8,16},{16,24},{24,0},{1,9},{9,17},{17,25},{25,1},{2,10},{10... | collective-permute-start | bytes 122888 | tf_op jit(solution)/shard_map/ppermute | solution.py:657
  47.1 0.3 collective-permute-start.4
  47.3 0.2 collective-permute-start.5
  47.6 0.6 %collective-permute-done.3.refs_1_ = bf16[160,128]{1,0:T(8,128)(2,1)S(1)} collective-permute-done((bf16[160,128]{1,0:T(8,128)(2,1)S(1)}, bf16[160,128]{1,0:T(8,128)(2,1)S(1)}, u32[]{:S(2)}, u32[]{:S(2)}) %collective-permute-start.3) | collective-permute-done | bytes 40992 | tf_op jit(solution)/shard_map/ppermute | solution.py:657
  48.2 1.8 %collective-permute-done.4.refs_2_ = bf16[160,128]{1,0:T(8,128)(2,1)S(1)} collective-permute-done((bf16[160,128]{1,0:T(8,128)(2,1)S(1)}, bf16[160,128]{1,0:T(8,128)(2,1)S(1)}, u32[]{:S(2)}, u32[]{:S(2)}) %collective-permute-start.4) | collective-permute-done | bytes 40992 | tf_op jit(solution)/shard_map/ppermute | solution.py:657
  49.9 0.8 %collective-permute-done.5.refs_3_ = bf16[160,128]{1,0:T(8,128)(2,1)S(1)} collective-permute-done((bf16[160,128]{1,0:T(8,128)(2,1)S(1)}, bf16[160,128]{1,0:T(8,128)(2,1)S(1)}, u32[]{:S(2)}, u32[]{:S(2)}) %collective-permute-start.5) | collective-permute-done | bytes 40992 | tf_op jit(solution)/shard_map/ppermute | solution.py:657
  50.8 0.0 collective-permute-done.8.refs_7_
  50.8 0.0 collective-permute-done.9.refs_9_
  50.8 0.0 copy-done.4
  50.8 0.0 copy-done.12
  50.8 7.5 %decode_block.1 = bf16[4,8,32,256]{3,2,1,0:T(8,128)(2,1)} custom-call(s32[9]{0:T(128)S(1)} %stack.33.place_ref, bf16[160,128]{1,0:T(8,128)(2,1)S(1)} %merge.1.refs_0_, bf16[160,128]{1,0:T(8,128)(2,1)S(1)} %collective-permute-done.3.refs_1_, bf16[160,128]{1,0:T(8,128)(2,1)S(1)} %collective-permute-done.4.refs_2_, ...), custom_call_target="tpu_custom_call" | custom-call | flops 3623878656 | bytes 4063232 | tf_op jit(solution)/shard_map/decode_block/pallas_call | solution.py:579
  (11 shorter events, 0.0 us)
Async XLA Ops:
  0.0 24.3 %collective-permute-start.1 = (bf16[256,2048]{1,0:T(8,128)(2,1)}, bf16[256,2048]{1,0:T(8,128)(2,1)}, u32[]{:S(2)}, u32[]{:S(2)}) collective-permute-start(bf16[256,2048]{1,0:T(8,128)(2,1)} %bitcast.20), channel_id=1, source_target_pairs={{0,1},{1,0},{2,3},{3,2},{4,5},{5,4},{6,7},{7,6},{8,9},{9,8},{10,11... | collective-permute-start | bytes 3145736 | tf_op jit(solution)/shard_map/ppermute | solution.py:184
  1.2 36.7 %collective-permute-start.6 = (bf16[27,64,256]{2,1,0:T(8,128)(2,1)}, bf16[27,64,256]{2,1,0:T(8,128)(2,1)}, u32[]{:S(2)}, u32[]{:S(2)}) collective-permute-start(bf16[27,64,256]{2,1,0:T(8,128)(2,1)} %refs_5_.1), channel_id=1, source_target_pairs={{0,2},{2,0},{4,6},{6,4},{8,12},{10,14},{12,8},{14,10},{16,18},{18,... | collective-permute-start | bytes 2654216 | tf_op jit(solution)/shard_map/ppermute | solution.py:597
  1.3 36.7 %collective-permute-start.7 = (bf16[27,64,256]{2,1,0:T(8,128)(2,1)}, bf16[27,64,256]{2,1,0:T(8,128)(2,1)}, u32[]{:S(2)}, u32[]{:S(2)}) collective-permute-start(bf16[27,64,256]{2,1,0:T(8,128)(2,1)} %refs_5_.1), channel_id=1, source_target_pairs={{2,4},{4,2},{8,14},{14,8},{18,20},{20,18},{24,30},{30,24},{3,5},{5... | collective-permute-start | bytes 2654216 | tf_op jit(solution)/shard_map/ppermute | solution.py:597
  2.9 1.2 %copy-start = (bf16[1,1,4,4,16,2048]{5,4,3,2,1,0:T(8,128)(2,1)S(1)}, bf16[1,1,4,4,16,2048]{5,4,3,2,1,0:T(8,128)(2,1)}, u32[]{:S(2)}) copy-start(bf16[1,1,4,4,16,2048]{5,4,3,2,1,0:T(8,128)(2,1)} %param.10) | copy-start | bytes 3145732
  4.1 1.2 %copy-start.2 = (bf16[1,1,4,4,16,2048]{5,4,3,2,1,0:T(8,128)(2,1)S(1)}, bf16[1,1,4,4,16,2048]{5,4,3,2,1,0:T(8,128)(2,1)}, u32[]{:S(2)}) copy-start(bf16[1,1,4,4,16,2048]{5,4,3,2,1,0:T(8,128)(2,1)} %param.11) | copy-start | bytes 3145732
  5.3 0.9 %copy-start.5 = (bf16[2048,64]{0,1:T(8,128)(2,1)S(1)}, bf16[2048,64]{0,1:T(8,128)(2,1)}, u32[]{:S(2)}) copy-start(bf16[2048,64]{0,1:T(8,128)(2,1)} %param.14) | copy-start | bytes 786436
  6.3 1.2 %copy-start.7 = (bf16[1,1,4,4,16,2048]{5,4,3,2,1,0:T(8,128)(2,1)S(1)}, bf16[1,1,4,4,16,2048]{5,4,3,2,1,0:T(8,128)(2,1)}, u32[]{:S(2)}) copy-start(bf16[1,1,4,4,16,2048]{5,4,3,2,1,0:T(8,128)(2,1)} %param.9) | copy-start | bytes 3145732
  7.5 0.7 %copy-start.8 = (s32[16,2,2]{0,2,1:T(2,128)S(1)}, s32[16,2,2]{0,2,1:T(2,128)}, u32[]{:S(2)}) copy-start(s32[16,2,2]{0,2,1:T(2,128)} %param.12) | copy-start | bytes 772
  8.2 0.7 %copy-start.10 = (s32[16,2]{0,1:T(2,128)S(1)}, s32[16,2]{0,1:T(2,128)}, u32[]{:S(2)}) copy-start(s32[16,2]{0,1:T(2,128)} %param.13) | copy-start | bytes 388
  8.9 8.7 %copy-start.14 = (s32[4]{0:T(128)S(1)}, s32[4]{0:T(128)}, u32[]{:S(2)}) copy-start(s32[4]{0:T(128)} %param.15) | copy-start | bytes 52
  8.9 15.5 %copy-start.3 = (bf16[1,1,4,4,16,2048]{5,4,3,2,1,0:T(8,128)(2,1)S(1)}, bf16[1,1,4,4,16,2048]{5,4,3,2,1,0:T(8,128)(2,1)}, u32[]{:S(2)}) copy-start(bf16[1,1,4,4,16,2048]{5,4,3,2,1,0:T(8,128)(2,1)} %param.11) | copy-start | bytes 3145732
  16.9 0.7 %copy-start.13 = (bf16[608,128]{1,0:T(8,128)(2,1)}, bf16[608,128]{1,0:T(8,128)(2,1)S(1)}, u32[]{:S(2)}) copy-start(bf16[608,128]{1,0:T(8,128)(2,1)S(1)} %get-tuple-element.19) | copy-start | bytes 466948
  17.5 6.8 %copy-start.1 = (bf16[1,1,4,4,16,2048]{5,4,3,2,1,0:T(8,128)(2,1)S(1)}, bf16[1,1,4,4,16,2048]{5,4,3,2,1,0:T(8,128)(2,1)}, u32[]{:S(2)}) copy-start(bf16[1,1,4,4,16,2048]{5,4,3,2,1,0:T(8,128)(2,1)} %param.10) | copy-start | bytes 3145732
  17.5 6.8 %copy-start.6 = (bf16[2048,64]{0,1:T(8,128)(2,1)S(1)}, bf16[2048,64]{0,1:T(8,128)(2,1)}, u32[]{:S(2)}) copy-start(bf16[2048,64]{0,1:T(8,128)(2,1)} %param.14) | copy-start | bytes 786436
  17.5 6.8 %copy-start.9 = (s32[16,2,2]{0,2,1:T(2,128)S(1)}, s32[16,2,2]{0,2,1:T(2,128)}, u32[]{:S(2)}) copy-start(s32[16,2,2]{0,2,1:T(2,128)} %param.12) | copy-start | bytes 772
  17.5 6.8 %copy-start.11 = (s32[16,2]{0,1:T(2,128)S(1)}, s32[16,2]{0,1:T(2,128)}, u32[]{:S(2)}) copy-start(s32[16,2]{0,1:T(2,128)} %param.13) | copy-start | bytes 388
  21.1 9.0 %collective-permute-start = (bf16[608,128]{1,0:T(8,128)(2,1)}, bf16[608,128]{1,0:T(8,128)(2,1)S(1)}, u32[]{:S(2)}, u32[]{:S(2)}) collective-permute-start(bf16[608,128]{1,0:T(8,128)(2,1)} %copy-done.13), channel_id=1, source_target_pairs={{0,1},{1,0},{2,3},{3,2},{4,5},{5,4},{6,7},{7,6},{8,9},{9,8},{10,11... | collective-permute-start | bytes 466952 | tf_op jit(solution)/shard_map/ppermute | solution.py:238
  30.1 20.6 %copy-start.4 = (bf16[2,768,512]{2,1,0:T(8,128)(2,1)S(1)}, bf16[2,768,512]{2,1,0:T(8,128)(2,1)}, u32[]{:S(2)}) copy-start(bf16[2,768,512]{2,1,0:T(8,128)(2,1)} %spread_first_kernel.1.refs_4_) | copy-start | bytes 4718596
  30.1 20.6 %copy-start.12 = (bf16[27,64,256]{2,1,0:T(8,128)(2,1)S(1)}, bf16[27,64,256]{2,1,0:T(8,128)(2,1)}, u32[]{:S(2)}) copy-start(bf16[27,64,256]{2,1,0:T(8,128)(2,1)} %refs_5_.1) | copy-start | bytes 2654212
  30.3 3.4 %collective-permute-start.2 = (bf16[96,256]{1,0:T(8,128)(2,1)S(1)}, bf16[96,256]{1,0:T(8,128)(2,1)S(1)}, u32[]{:S(2)}, u32[]{:S(2)}) collective-permute-start(bf16[96,256]{1,0:T(8,128)(2,1)S(1)} %combine.1.sent_ref), channel_id=1, source_target_pairs={{0,1},{1,0},{2,3},{3,2},{4,5},{5,4},{6,7},{7,6},{8,9},{9,8},{10,11... | collective-permute-start | bytes 147464 | tf_op jit(solution)/shard_map/ppermute | solution.py:255
  37.9 12.8 %collective-permute-start.8 = (bf16[27,64,256]{2,1,0:T(8,128)(2,1)}, bf16[27,64,256]{2,1,0:T(8,128)(2,1)S(1)}, u32[]{:S(2)}, u32[]{:S(2)}) collective-permute-start(bf16[27,64,256]{2,1,0:T(8,128)(2,1)} %collective-permute-done.6.refs_6_), channel_id=1, source_target_pairs={{0,8},{8,0},{16,24},{24,16},{1,9},{9,1},{17,25},{25,17},{2,10},{10... | collective-permute-start | bytes 2654216 | tf_op jit(solution)/shard_map/ppermute | solution.py:606
  43.5 7.3 %collective-permute-start.9 = (bf16[27,64,256]{2,1,0:T(8,128)(2,1)}, bf16[27,64,256]{2,1,0:T(8,128)(2,1)S(1)}, u32[]{:S(2)}, u32[]{:S(2)}) collective-permute-start(bf16[27,64,256]{2,1,0:T(8,128)(2,1)} %collective-permute-done.7.refs_8_), channel_id=1, source_target_pairs={{2,10},{4,12},{8,0},{14,6},{18,26},{20,28},{24,16},{30,22},{3,11},... | collective-permute-start | bytes 2654216 | tf_op jit(solution)/shard_map/ppermute | solution.py:608
  44.8 3.4 %collective-permute-start.3 = (bf16[160,128]{1,0:T(8,128)(2,1)S(1)}, bf16[160,128]{1,0:T(8,128)(2,1)S(1)}, u32[]{:S(2)}, u32[]{:S(2)}) collective-permute-start(bf16[160,128]{1,0:T(8,128)(2,1)S(1)} %merge.1.refs_0_), channel_id=1, source_target_pairs={{0,8},{8,16},{16,24},{24,0},{1,9},{9,17},{17,25},{25,1},{2,10},{10... | collective-permute-start | bytes 122888 | tf_op jit(solution)/shard_map/ppermute | solution.py:657
  47.1 2.9 %collective-permute-start.4 = (bf16[160,128]{1,0:T(8,128)(2,1)S(1)}, bf16[160,128]{1,0:T(8,128)(2,1)S(1)}, u32[]{:S(2)}, u32[]{:S(2)}) collective-permute-start(bf16[160,128]{1,0:T(8,128)(2,1)S(1)} %merge.1.refs_0_), channel_id=1, source_target_pairs={{0,16},{8,24},{16,0},{24,8},{1,17},{9,25},{17,1},{25,9},{2,18},{10... | collective-permute-start | bytes 122888 | tf_op jit(solution)/shard_map/ppermute | solution.py:657
  47.3 3.4 %collective-permute-start.5 = (bf16[160,128]{1,0:T(8,128)(2,1)S(1)}, bf16[160,128]{1,0:T(8,128)(2,1)S(1)}, u32[]{:S(2)}, u32[]{:S(2)}) collective-permute-start(bf16[160,128]{1,0:T(8,128)(2,1)S(1)} %merge.1.refs_0_), channel_id=1, source_target_pairs={{0,24},{8,0},{16,8},{24,16},{1,25},{9,1},{17,9},{25,17},{2,26},{10... | collective-permute-start | bytes 122888 | tf_op jit(solution)/shard_map/ppermute | solution.py:657

commit v7 on v6

--- a/solution.py
+++ b/solution.py
@@ -166,7 +166,7 @@
     out_ref[own:, :] = beside_ref[...]
 
 
-def split_attention(queries, key_states, value_states, kept_tiles, kept_counts, patch_weight, ready):
+def split_attention(queries, key_states, value_states, kept_tiles, kept_counts, patch_weight, ready, forward):
     frames, rows, cols, feature_count = queries.shape[2:]
     tokens = frames * rows * cols
     flat_query = queries.reshape(tokens, feature_count)
@@ -236,6 +236,7 @@
     _, mapped, note = attend(flat_query, 0, "own_queries", with_note=True)
     note, ready = lax.optimization_barrier((note, ready))
     other_note = lax.ppermute(note, "sp", swap)
+    forwarded = forward(ready)
     levels, shares = [], []
     for part, start in zip(other_queries, starts):
         part, _ = lax.optimization_barrier((part, levels[-1] if levels else note))
@@ -271,7 +272,7 @@
         compiler_params=params,
         name="merge",
     )(got, mapped, beside)
-    return message, ready
+    return message, forwarded, ready
 
 
 def to_tiles(grid, tile_size):
@@ -427,17 +428,17 @@
         shard_copies = [pltpu.make_async_copy(shard_refs[0], kernel_ref, sems.at[1])]
     else:
         shard_copies = [
-            pltpu.make_async_copy(ref, kernel_ref.at[place_ref[3 + k]], sems.at[1 + k])
+            pltpu.make_async_copy(ref, kernel_ref.at[place_ref[3 + min(k, 3)]], sems.at[1 + k])
             for k, ref in enumerate(shard_refs)
         ]
-    direct = place_ref[3 + len(shard_refs)]
+    holder = place_ref[7 if len(shard_refs) > 1 else 3]
 
     def each_shard(act):
         for k, copy in enumerate(shard_copies):
-            if len(shard_copies) - k > 2 or len(shard_copies) == 1:
+            if k < 3:
                 act(copy)
             else:
-                pl.when(direct == len(shard_copies) - 1 - k)(functools.partial(act, copy))
+                pl.when(holder == k - 3)(functools.partial(act, copy))
 
     each_shard(lambda copy: copy.start())
 
@@ -593,20 +594,25 @@
 def trade_shards(shard, segment_count):
     segments = range(segment_count)
     near = [(s * 4 + g, s * 4 + (g ^ (1 + s % 2))) for s in segments for g in range(4)]
-    far = [(s * 4 + g, s * 4 + (g ^ 3)) for s in segments for g in ((1, 2), (0, 3))[s % 2]]
-    return [lax.ppermute(shard, ("segment", "grp"), pairs) for pairs in (near, far)]
-
-
-def swap_shards(near, far, ready, segment_count):
-    near, far, _ = lax.optimization_barrier((near, far, ready))
+    inner = [(s * 4 + g, s * 4 + (g ^ 3)) for s in segments[::2] for g in (1, 2)]
+    return [lax.ppermute(shard, ("segment", "grp"), pairs) for pairs in (near, inner)]
+
+
+def forward_shards(near, segment_count, ready):
+    near, _ = lax.optimization_barrier((near, ready))
     segments = range(segment_count)
-    pairs = [(s * 4 + g, (s ^ 1) * 4 + g) for s in segments for g in ((1, 2), (0, 3))[s % 2]]
+    outward = [(s * 4 + a, s * 4 + b) for s in segments[1::2] for a, b in ((1, 0), (2, 3))]
     return (
-        near,
+        lax.ppermute(near, ("segment", "grp"), outward),
         lax.ppermute(near, "segment", [(s, s ^ 1) for s in segments]),
-        far,
-        lax.ppermute(far, ("segment", "grp"), pairs),
-    )
+    )
+
+
+def share_shards(inner, outer, at_inner, segment_count, ready):
+    inner, outer, _ = lax.optimization_barrier((inner, outer, ready))
+    held = jnp.where(at_inner, inner, outer)
+    pairs = [(s * 4 + g, (s ^ 1) * 4 + g) for s in range(segment_count) for g in ((1, 2), (0, 3))[s % 2]]
+    return held, lax.ppermute(held, ("segment", "grp"), pairs)
 
 
 def local(
@@ -636,21 +642,26 @@
     line = group_count == 4 and segment_count % 2 == 0
     places = [sp_rank, jnp.int32(sp_count), step]
     if line:
-        inner = jnp.logical_or(group == 1, group == 2)
-        places += [group, group ^ (1 + core), group ^ (2 - core), group ^ 3, group ^ 3]
-        places.append((inner == (core == 0)).astype(jnp.int32))
-        traded = trade_shards(second_kernel, segment_count)
+        at_inner = jnp.logical_or(group == 1, group == 2)
+        places += [group, group ^ (1 + core), group ^ (2 - core), group ^ 3]
+        places.append(jnp.where(at_inner, core, 1 - core))
+        near, inner = trade_shards(second_kernel, segment_count)
+        forward = functools.partial(forward_shards, near, segment_count)
     else:
         places += [jnp.int32(0)] * 2
+        forward = lambda ready: None
     place = jnp.stack(places).astype(jnp.int32)
 
     arguments = (queries, key_states, value_states, kept_tiles, kept_counts, patch_weight)
     if sp_count == 2 and rows * sp_count == TH and frames == TT:
-        message, (weights, place) = split_attention(*arguments, (weights, place))
+        message, forwarded, (weights, place) = split_attention(*arguments, (weights, place), forward)
     else:
         message = exchanged_attention(*arguments)
+        forwarded = forward(message)
     if line:
-        shards = [second_kernel, *swap_shards(*traded, message, segment_count)]
+        outer, swapped = forwarded
+        last = share_shards(inner, outer, at_inner, segment_count, message)
+        shards = [second_kernel, near, swapped, *last]
     else:
         shards = [lax.all_gather(second_kernel, "grp", axis=0, tiled=False)]
     messages = [message] + [

time: 58.7 us -> 60.3 us (1.027)
  the two profiles are of different devices: /device:TPU:17 before, /device:TPU:19 now
where the time goes in v7:
time: 60.3 us; the launch traced here: 59.9 us
  Pallas kernels  24.2 us (40%)
  starting transfers between devices  14.9 us (25%)
  waiting for transfers between devices  11 us (18%)
  local copies, waits for them, and re-layouts  6.76 us (11%)
  other arithmetic  2.16 us (4%)
  between operations  0.86 us (1%)
    pallas_call x2, Pallas kernels, attend(): pl.pallas_call(functools.partial(attend_kernel, start, grid), grid=(count...  13.7 us
    pallas_call x1, Pallas kernels, decode(): pl.pallas_call(body, grid_spec=grid_spec, out_shape=jax.ShapeDtypeStruct(...  7.53 us
    unnamed x30, local copies, waits for them, and re-layouts  6.68 us
    ppermute x1, starting transfers between devices, forward_shards(): lax.ppermute(near, ('segment', 'grp'), outward)  6.14 us
    ppermute x2, waiting for transfers between devices, trade_shards(): lax.ppermute(shard, ('segment', 'grp'), pairs)  5.17 us
    ppermute x3, waiting for transfers between devices, local(): lax.ppermute(message, 'segment', [(i, (i + step) % segment_count) for i i...  3.42 us
    ppermute x3, starting transfers between devices, local(): lax.ppermute(message, 'segment', [(i, (i + step) % segment_count) for i i...  2.58 us
    ppermute x1, waiting for transfers between devices, split_attention(): got = lax.ppermute(sent, 'sp', swap)  2.41 us
  transfers between devices with their start and end apart: 11, of which 5 were waited for; matrix products, arithmetic and copies ran while one was open for 4% of the time, Pallas kernels for 28%

profile of v7, /device:TPU:19, one launch (start us, length us, event | category | flops | bytes accessed | tf_op | source)
XLA Modules:
  0.0 59.9 jit_solution(13244504090834622290)
XLA Ops:
  0.0 0.1 collective-permute-start.6
  0.1 1.2 %collective-permute-start.1 = (bf16[256,2048]{1,0:T(8,128)(2,1)}, bf16[256,2048]{1,0:T(8,128)(2,1)}, u32[]{:S(2)}, u32[]{:S(2)}) collective-permute-start(bf16[256,2048]{1,0:T(8,128)(2,1)} %bitcast.20), channel_id=1, source_target_pairs={{0,1},{1,0},{2,3},{3,2},{4,5},{5,4},{6,7},{7,6},{8,9},{9,8},{10,11... | collective-permute-start | bytes 3145736 | tf_op jit(solution)/shard_map/ppermute | solution.py:184
  1.3 1.6 %collective-permute-start.8 = (bf16[27,64,256]{2,1,0:T(8,128)(2,1)}, bf16[27,64,256]{2,1,0:T(8,128)(2,1)}, u32[]{:S(2)}, u32[]{:S(2)}) collective-permute-start(bf16[27,64,256]{2,1,0:T(8,128)(2,1)} %refs_5_.1), channel_id=1, source_target_pairs={{2,4},{4,2},{18,20},{20,18},{3,5},{5,3},{19,21},{21,19}} | collective-permute-start | bytes 2654216 | tf_op jit(solution)/shard_map/ppermute | solution.py:598
  2.9 1.2 %copy-done = bf16[1,1,4,4,16,2048]{5,4,3,2,1,0:T(8,128)(2,1)S(1)} copy-done((bf16[1,1,4,4,16,2048]{5,4,3,2,1,0:T(8,128)(2,1)S(1)}, bf16[1,1,4,4,16,2048]{5,4,3,2,1,0:T(8,128)(2,1)}, u32[]{:S(2)}) %copy-start) | copy-done | bytes 1048600
  4.1 1.2 %copy-done.2 = bf16[1,1,4,4,16,2048]{5,4,3,2,1,0:T(8,128)(2,1)S(1)} copy-done((bf16[1,1,4,4,16,2048]{5,4,3,2,1,0:T(8,128)(2,1)S(1)}, bf16[1,1,4,4,16,2048]{5,4,3,2,1,0:T(8,128)(2,1)}, u32[]{:S(2)}) %copy-start.2) | copy-done | bytes 1048600
  5.3 0.9 %copy-done.5 = bf16[2048,64]{0,1:T(8,128)(2,1)S(1)} copy-done((bf16[2048,64]{0,1:T(8,128)(2,1)S(1)}, bf16[2048,64]{0,1:T(8,128)(2,1)}, u32[]{:S(2)}) %copy-start.5) | copy-done | bytes 262168
  6.3 1.2 %copy-done.7 = bf16[1,1,4,4,16,2048]{5,4,3,2,1,0:T(8,128)(2,1)S(1)} copy-done((bf16[1,1,4,4,16,2048]{5,4,3,2,1,0:T(8,128)(2,1)S(1)}, bf16[1,1,4,4,16,2048]{5,4,3,2,1,0:T(8,128)(2,1)}, u32[]{:S(2)}) %copy-start.7) | copy-done | bytes 1048600
  7.5 0.7 %copy-done.8 = s32[16,2,2]{0,2,1:T(2,128)S(1)} copy-done((s32[16,2,2]{0,2,1:T(2,128)S(1)}, s32[16,2,2]{0,2,1:T(2,128)}, u32[]{:S(2)}) %copy-start.8) | copy-done | bytes 280
  8.2 0.7 %copy-done.10 = s32[16,2]{0,1:T(2,128)S(1)} copy-done((s32[16,2]{0,1:T(2,128)S(1)}, s32[16,2]{0,1:T(2,128)}, u32[]{:S(2)}) %copy-start.10) | copy-done | bytes 152
  8.9 8.0 %own_queries.1 = (f32[16,256]{1,0:T(8,128)}, f32[16,64,256]{2,1,0:T(8,128)S(1)}, bf16[608,128]{1,0:T(8,128)(2,1)S(1)}) custom-call(s32[1]{0:T(128)} %bitcast.rank_ref, s32[2,2,16]{2,1,0:T(2,128)S(1)} %bitcast.22, s32[2,16]{1,0:T(2,128)S(1)} %bitcast.24, bf16[256,2048]{1,0:T(8,128)(2,1)S(1)} %bitcast.21, bf16[256,2048]{1,0:T(8,128)(2,1)S(1)} %bitcast.14, ...), custom_call_target="tpu_custom_call" | custom-call | flops 4096 | bytes 4096 | tf_op jit(solution)/shard_map/own_queries/pallas_call | solution.py:206
  16.9 0.7 %copy-done.13 = bf16[608,128]{1,0:T(8,128)(2,1)} copy-done((bf16[608,128]{1,0:T(8,128)(2,1)}, bf16[608,128]{1,0:T(8,128)(2,1)S(1)}, u32[]{:S(2)}) %copy-start.13) | copy-done | bytes 155672
  17.5 0.0 copy-done.14
  17.6 0.7 %fusion = s32[]{:T(128)} fusion(s32[4]{0:T(128)S(1)} %copy-done.14, s32[]{:T(128)S(6)} %axis_index.39), kind=kLoop, calls=%fused_computation.2 | loop fusion | flops 11 | bytes 24 | tf_op jit(solution)/shard_map/reduce_sum | solution.py:637
  19.0 2.2 %spread_first_kernel.1.refs_4_ = bf16[2,768,512]{2,1,0:T(8,128)(2,1)} custom-call(bf16[27,16,256]{2,1,0:T(8,128)(2,1)} %plain_ref.1), custom_call_target="tpu_custom_call" | custom-call | tf_op jit(solution)/shard_map/spread_first_kernel/pallas_call | solution.py:394
  21.2 0.1 stack.28.place_ref
  21.3 5.2 %collective-permute-done.6.refs_6_ = bf16[27,64,256]{2,1,0:T(8,128)(2,1)} collective-permute-done((bf16[27,64,256]{2,1,0:T(8,128)(2,1)}, bf16[27,64,256]{2,1,0:T(8,128)(2,1)}, u32[]{:S(2)}, u32[]{:S(2)}) %collective-permute-start.6) | collective-permute-done | bytes 884768 | tf_op jit(solution)/shard_map/ppermute | solution.py:598
  26.4 6.1 %collective-permute-start.9 = (bf16[27,64,256]{2,1,0:T(8,128)(2,1)}, bf16[27,64,256]{2,1,0:T(8,128)(2,1)S(1)}, u32[]{:S(2)}, u32[]{:S(2)}) collective-permute-start(bf16[27,64,256]{2,1,0:T(8,128)(2,1)} %collective-permute-done.6.refs_6_), channel_id=1, source_target_pairs={{10,8},{12,14},{26,24},{28,30},{11,9},{13,15},{27,25},{29,31}} | collective-permute-start | bytes 2654216 | tf_op jit(solution)/shard_map/ppermute | solution.py:606
  32.6 1.8 %collective-permute-start = (bf16[608,128]{1,0:T(8,128)(2,1)}, bf16[608,128]{1,0:T(8,128)(2,1)S(1)}, u32[]{:S(2)}, u32[]{:S(2)}) collective-permute-start(bf16[608,128]{1,0:T(8,128)(2,1)} %copy-done.13), channel_id=1, source_target_pairs={{0,1},{1,0},{2,3},{3,2},{4,5},{5,4},{6,7},{7,6},{8,9},{9,8},{10,11... | collective-permute-start | bytes 466952 | tf_op jit(solution)/shard_map/ppermute | solution.py:238
  34.4 0.0 collective-permute-done.1.q_ref
  34.4 0.0 copy-done.3
  34.4 0.0 copy-done.1
  34.4 0.0 copy-done.6
  34.4 0.0 copy-done.9
  34.4 0.0 copy-done.11
  34.4 5.8 %other_queries.1 = (f32[16,256]{1,0:T(8,128)S(1)}, f32[16,64,256]{2,1,0:T(8,128)S(1)}) custom-call(s32[1]{0:T(128)} %bitcast.rank_ref, s32[2,2,16]{2,1,0:T(2,128)S(1)} %bitcast.23, s32[2,16]{1,0:T(2,128)S(1)} %bitcast.25, bf16[256,2048]{1,0:T(8,128)(2,1)} %collective-permute-done.1.q_ref, bf16[256,2048]{1,0:T(8,128)(2,1)S(1)} %bitcast.15, ...), custom_call_target="tpu_custom_call" | custom-call | flops 4096 | bytes 4096 | tf_op jit(solution)/shard_map/other_queries/pallas_call | solution.py:206
  40.2 0.0 collective-permute-done.note_ref
  40.2 0.1 combine.1.sent_ref
  40.3 0.1 collective-permute-start.2
  40.4 0.1 collective-permute-start.7
  40.5 0.4 beside.1.beside_ref
  40.9 2.4 %collective-permute-done.2.got_ref = bf16[96,256]{1,0:T(8,128)(2,1)S(1)} collective-permute-done((bf16[96,256]{1,0:T(8,128)(2,1)S(1)}, bf16[96,256]{1,0:T(8,128)(2,1)S(1)}, u32[]{:S(2)}, u32[]{:S(2)}) %collective-permute-start.2) | collective-permute-done | bytes 49184 | tf_op jit(solution)/shard_map/ppermute | solution.py:256
  43.3 0.2 merge.1.refs_0_
  43.5 0.0 copy-start.12
  43.5 0.0 collective-permute-done.8
  43.5 0.0 collective-permute-done.9
  43.5 1.4 %broadcast_select_fusion.refs_8_ = bf16[27,64,256]{2,1,0:T(8,128)(2,1)S(1)} fusion(bf16[27,64,256]{2,1,0:T(8,128)(2,1)} %collective-permute-done.8, bf16[27,64,256]{2,1,0:T(8,128)(2,1)S(1)} %collective-permute-done.9, pred[]{:T(512)S(6)} %or.3), kind=kLoop, calls=%fused_computation | loop fusion | flops 442368 | bytes 2654209 | tf_op jit(solution)/shard_map/jit(_where)/select_n | solution.py:613
  45.0 1.3 %collective-permute-start.10 = (bf16[27,64,256]{2,1,0:T(8,128)(2,1)S(1)}, bf16[27,64,256]{2,1,0:T(8,128)(2,1)S(1)}, u32[]{:S(2)}, u32[]{:S(2)}) collective-permute-start(bf16[27,64,256]{2,1,0:T(8,128)(2,1)S(1)} %broadcast_select_fusion.refs_8_), channel_id=1, source_target_pairs={{2,10},{4,12},{8,0},{14,6},{18,26},{20,28},{24,16},{30,22},{3,11},... | collective-permute-start | bytes 2654216 | tf_op jit(solution)/shard_map/ppermute | solution.py:615
  46.3 1.4 %collective-permute-start.3 = (bf16[160,128]{1,0:T(8,128)(2,1)S(1)}, bf16[160,128]{1,0:T(8,128)(2,1)S(1)}, u32[]{:S(2)}, u32[]{:S(2)}) collective-permute-start(bf16[160,128]{1,0:T(8,128)(2,1)S(1)} %merge.1.refs_0_), channel_id=1, source_target_pairs={{0,8},{8,16},{16,24},{24,0},{1,9},{9,17},{17,25},{25,1},{2,10},{10... | collective-permute-start | bytes 122888 | tf_op jit(solution)/shard_map/ppermute | solution.py:668
  47.7 1.2 %collective-permute-start.4 = (bf16[160,128]{1,0:T(8,128)(2,1)S(1)}, bf16[160,128]{1,0:T(8,128)(2,1)S(1)}, u32[]{:S(2)}, u32[]{:S(2)}) collective-permute-start(bf16[160,128]{1,0:T(8,128)(2,1)S(1)} %merge.1.refs_0_), channel_id=1, source_target_pairs={{0,16},{8,24},{16,0},{24,8},{1,17},{9,25},{17,1},{25,9},{2,18},{10... | collective-permute-start | bytes 122888 | tf_op jit(solution)/shard_map/ppermute | solution.py:668
  48.9 0.0 collective-permute-start.5
  48.9 0.5 collective-permute-done.3.refs_1_
  49.4 1.9 %collective-permute-done.4.refs_2_ = bf16[160,128]{1,0:T(8,128)(2,1)S(1)} collective-permute-done((bf16[160,128]{1,0:T(8,128)(2,1)S(1)}, bf16[160,128]{1,0:T(8,128)(2,1)S(1)}, u32[]{:S(2)}, u32[]{:S(2)}) %collective-permute-start.4) | collective-permute-done | bytes 40992 | tf_op jit(solution)/shard_map/ppermute | solution.py:668
  51.3 1.0 %collective-permute-done.5.refs_3_ = bf16[160,128]{1,0:T(8,128)(2,1)S(1)} collective-permute-done((bf16[160,128]{1,0:T(8,128)(2,1)S(1)}, bf16[160,128]{1,0:T(8,128)(2,1)S(1)}, u32[]{:S(2)}, u32[]{:S(2)}) %collective-permute-start.5) | collective-permute-done | bytes 40992 | tf_op jit(solution)/shard_map/ppermute | solution.py:668
  52.3 0.0 collective-permute-done.7.refs_7_
  52.3 0.0 collective-permute-done.10.refs_9_
  52.3 0.0 copy-done.4
  52.3 0.0 copy-done.12
  52.3 7.5 %decode_block.1 = bf16[4,8,32,256]{3,2,1,0:T(8,128)(2,1)} custom-call(s32[8]{0:T(128)S(1)} %stack.28.place_ref, bf16[160,128]{1,0:T(8,128)(2,1)S(1)} %merge.1.refs_0_, bf16[160,128]{1,0:T(8,128)(2,1)S(1)} %collective-permute-done.3.refs_1_, bf16[160,128]{1,0:T(8,128)(2,1)S(1)} %collective-permute-done.4.refs_2_, ...), custom_call_target="tpu_custom_call" | custom-call | flops 3623878656 | bytes 4063232 | tf_op jit(solution)/shard_map/decode_block/pallas_call | solution.py:580
  (14 shorter events, 0.0 us)
Async XLA Ops:
  0.0 26.4 %collective-permute-start.6 = (bf16[27,64,256]{2,1,0:T(8,128)(2,1)}, bf16[27,64,256]{2,1,0:T(8,128)(2,1)}, u32[]{:S(2)}, u32[]{:S(2)}) collective-permute-start(bf16[27,64,256]{2,1,0:T(8,128)(2,1)} %refs_5_.1), channel_id=1, source_target_pairs={{0,2},{2,0},{4,6},{6,4},{8,12},{10,14},{12,8},{14,10},{16,18},{18,... | collective-permute-start | bytes 2654216 | tf_op jit(solution)/shard_map/ppermute | solution.py:598
  0.1 34.4 %collective-permute-start.1 = (bf16[256,2048]{1,0:T(8,128)(2,1)}, bf16[256,2048]{1,0:T(8,128)(2,1)}, u32[]{:S(2)}, u32[]{:S(2)}) collective-permute-start(bf16[256,2048]{1,0:T(8,128)(2,1)} %bitcast.20), channel_id=1, source_target_pairs={{0,1},{1,0},{2,3},{3,2},{4,5},{5,4},{6,7},{7,6},{8,9},{9,8},{10,11... | collective-permute-start | bytes 3145736 | tf_op jit(solution)/shard_map/ppermute | solution.py:184
  1.3 42.2 %collective-permute-start.8 = (bf16[27,64,256]{2,1,0:T(8,128)(2,1)}, bf16[27,64,256]{2,1,0:T(8,128)(2,1)}, u32[]{:S(2)}, u32[]{:S(2)}) collective-permute-start(bf16[27,64,256]{2,1,0:T(8,128)(2,1)} %refs_5_.1), channel_id=1, source_target_pairs={{2,4},{4,2},{18,20},{20,18},{3,5},{5,3},{19,21},{21,19}} | collective-permute-start | bytes 2654216 | tf_op jit(solution)/shard_map/ppermute | solution.py:598
  2.9 1.2 %copy-start = (bf16[1,1,4,4,16,2048]{5,4,3,2,1,0:T(8,128)(2,1)S(1)}, bf16[1,1,4,4,16,2048]{5,4,3,2,1,0:T(8,128)(2,1)}, u32[]{:S(2)}) copy-start(bf16[1,1,4,4,16,2048]{5,4,3,2,1,0:T(8,128)(2,1)} %param.10) | copy-start | bytes 3145732
  4.1 1.2 %copy-start.2 = (bf16[1,1,4,4,16,2048]{5,4,3,2,1,0:T(8,128)(2,1)S(1)}, bf16[1,1,4,4,16,2048]{5,4,3,2,1,0:T(8,128)(2,1)}, u32[]{:S(2)}) copy-start(bf16[1,1,4,4,16,2048]{5,4,3,2,1,0:T(8,128)(2,1)} %param.11) | copy-start | bytes 3145732
  5.3 0.9 %copy-start.5 = (bf16[2048,64]{0,1:T(8,128)(2,1)S(1)}, bf16[2048,64]{0,1:T(8,128)(2,1)}, u32[]{:S(2)}) copy-start(bf16[2048,64]{0,1:T(8,128)(2,1)} %param.14) | copy-start | bytes 786436
  6.3 1.2 %copy-start.7 = (bf16[1,1,4,4,16,2048]{5,4,3,2,1,0:T(8,128)(2,1)S(1)}, bf16[1,1,4,4,16,2048]{5,4,3,2,1,0:T(8,128)(2,1)}, u32[]{:S(2)}) copy-start(bf16[1,1,4,4,16,2048]{5,4,3,2,1,0:T(8,128)(2,1)} %param.9) | copy-start | bytes 3145732
  7.5 0.7 %copy-start.8 = (s32[16,2,2]{0,2,1:T(2,128)S(1)}, s32[16,2,2]{0,2,1:T(2,128)}, u32[]{:S(2)}) copy-start(s32[16,2,2]{0,2,1:T(2,128)} %param.12) | copy-start | bytes 772
  8.2 0.7 %copy-start.10 = (s32[16,2]{0,1:T(2,128)S(1)}, s32[16,2]{0,1:T(2,128)}, u32[]{:S(2)}) copy-start(s32[16,2]{0,1:T(2,128)} %param.13) | copy-start | bytes 388
  8.9 8.7 %copy-start.14 = (s32[4]{0:T(128)S(1)}, s32[4]{0:T(128)}, u32[]{:S(2)}) copy-start(s32[4]{0:T(128)} %param.15) | copy-start | bytes 52
  8.9 25.5 %copy-start.3 = (bf16[1,1,4,4,16,2048]{5,4,3,2,1,0:T(8,128)(2,1)S(1)}, bf16[1,1,4,4,16,2048]{5,4,3,2,1,0:T(8,128)(2,1)}, u32[]{:S(2)}) copy-start(bf16[1,1,4,4,16,2048]{5,4,3,2,1,0:T(8,128)(2,1)} %param.11) | copy-start | bytes 3145732
  16.9 0.7 %copy-start.13 = (bf16[608,128]{1,0:T(8,128)(2,1)}, bf16[608,128]{1,0:T(8,128)(2,1)S(1)}, u32[]{:S(2)}) copy-start(bf16[608,128]{1,0:T(8,128)(2,1)S(1)} %get-tuple-element.20) | copy-start | bytes 466948
  17.5 16.9 %copy-start.1 = (bf16[1,1,4,4,16,2048]{5,4,3,2,1,0:T(8,128)(2,1)S(1)}, bf16[1,1,4,4,16,2048]{5,4,3,2,1,0:T(8,128)(2,1)}, u32[]{:S(2)}) copy-start(bf16[1,1,4,4,16,2048]{5,4,3,2,1,0:T(8,128)(2,1)} %param.10) | copy-start | bytes 3145732
  17.5 16.9 %copy-start.6 = (bf16[2048,64]{0,1:T(8,128)(2,1)S(1)}, bf16[2048,64]{0,1:T(8,128)(2,1)}, u32[]{:S(2)}) copy-start(bf16[2048,64]{0,1:T(8,128)(2,1)} %param.14) | copy-start | bytes 786436
  17.5 16.9 %copy-start.9 = (s32[16,2,2]{0,2,1:T(2,128)S(1)}, s32[16,2,2]{0,2,1:T(2,128)}, u32[]{:S(2)}) copy-start(s32[16,2,2]{0,2,1:T(2,128)} %param.12) | copy-start | bytes 772
  17.5 16.9 %copy-start.11 = (s32[16,2]{0,1:T(2,128)S(1)}, s32[16,2]{0,1:T(2,128)}, u32[]{:S(2)}) copy-start(s32[16,2]{0,1:T(2,128)} %param.13) | copy-start | bytes 388
  26.4 17.1 %collective-permute-start.9 = (bf16[27,64,256]{2,1,0:T(8,128)(2,1)}, bf16[27,64,256]{2,1,0:T(8,128)(2,1)S(1)}, u32[]{:S(2)}, u32[]{:S(2)}) collective-permute-start(bf16[27,64,256]{2,1,0:T(8,128)(2,1)} %collective-permute-done.6.refs_6_), channel_id=1, source_target_pairs={{10,8},{12,14},{26,24},{28,30},{11,9},{13,15},{27,25},{29,31}} | collective-permute-start | bytes 2654216 | tf_op jit(solution)/shard_map/ppermute | solution.py:606
  32.6 7.6 %collective-permute-start = (bf16[608,128]{1,0:T(8,128)(2,1)}, bf16[608,128]{1,0:T(8,128)(2,1)S(1)}, u32[]{:S(2)}, u32[]{:S(2)}) collective-permute-start(bf16[608,128]{1,0:T(8,128)(2,1)} %copy-done.13), channel_id=1, source_target_pairs={{0,1},{1,0},{2,3},{3,2},{4,5},{5,4},{6,7},{7,6},{8,9},{9,8},{10,11... | collective-permute-start | bytes 466952 | tf_op jit(solution)/shard_map/ppermute | solution.py:238
  40.3 3.0 %collective-permute-start.2 = (bf16[96,256]{1,0:T(8,128)(2,1)S(1)}, bf16[96,256]{1,0:T(8,128)(2,1)S(1)}, u32[]{:S(2)}, u32[]{:S(2)}) collective-permute-start(bf16[96,256]{1,0:T(8,128)(2,1)S(1)} %combine.1.sent_ref), channel_id=1, source_target_pairs={{0,1},{1,0},{2,3},{3,2},{4,5},{5,4},{6,7},{7,6},{8,9},{9,8},{10,11... | collective-permute-start | bytes 147464 | tf_op jit(solution)/shard_map/ppermute | solution.py:256
  40.4 11.9 %collective-permute-start.7 = (bf16[27,64,256]{2,1,0:T(8,128)(2,1)}, bf16[27,64,256]{2,1,0:T(8,128)(2,1)S(1)}, u32[]{:S(2)}, u32[]{:S(2)}) collective-permute-start(bf16[27,64,256]{2,1,0:T(8,128)(2,1)} %collective-permute-done.6.refs_6_), channel_id=1, source_target_pairs={{0,8},{8,0},{16,24},{24,16},{1,9},{9,1},{17,25},{25,17},{2,10},{10... | collective-permute-start | bytes 2654216 | tf_op jit(solution)/shard_map/ppermute | solution.py:607
  43.5 8.8 %copy-start.4 = (bf16[2,768,512]{2,1,0:T(8,128)(2,1)S(1)}, bf16[2,768,512]{2,1,0:T(8,128)(2,1)}, u32[]{:S(2)}) copy-start(bf16[2,768,512]{2,1,0:T(8,128)(2,1)} %spread_first_kernel.1.refs_4_) | copy-start | bytes 4718596
  43.5 8.8 %copy-start.12 = (bf16[27,64,256]{2,1,0:T(8,128)(2,1)S(1)}, bf16[27,64,256]{2,1,0:T(8,128)(2,1)}, u32[]{:S(2)}) copy-start(bf16[27,64,256]{2,1,0:T(8,128)(2,1)} %refs_5_.1) | copy-start | bytes 2654212
  45.0 7.3 %collective-permute-start.10 = (bf16[27,64,256]{2,1,0:T(8,128)(2,1)S(1)}, bf16[27,64,256]{2,1,0:T(8,128)(2,1)S(1)}, u32[]{:S(2)}, u32[]{:S(2)}) collective-permute-start(bf16[27,64,256]{2,1,0:T(8,128)(2,1)S(1)} %broadcast_select_fusion.refs_8_), channel_id=1, source_target_pairs={{2,10},{4,12},{8,0},{14,6},{18,26},{20,28},{24,16},{30,22},{3,11},... | collective-permute-start | bytes 2654216 | tf_op jit(solution)/shard_map/ppermute | solution.py:615
  46.3 3.1 %collective-permute-start.3 = (bf16[160,128]{1,0:T(8,128)(2,1)S(1)}, bf16[160,128]{1,0:T(8,128)(2,1)S(1)}, u32[]{:S(2)}, u32[]{:S(2)}) collective-permute-start(bf16[160,128]{1,0:T(8,128)(2,1)S(1)} %merge.1.refs_0_), channel_id=1, source_target_pairs={{0,8},{8,16},{16,24},{24,0},{1,9},{9,17},{17,25},{25,1},{2,10},{10... | collective-permute-start | bytes 122888 | tf_op jit(solution)/shard_map/ppermute | solution.py:668
  47.7 3.6 %collective-permute-start.4 = (bf16[160,128]{1,0:T(8,128)(2,1)S(1)}, bf16[160,128]{1,0:T(8,128)(2,1)S(1)}, u32[]{:S(2)}, u32[]{:S(2)}) collective-permute-start(bf16[160,128]{1,0:T(8,128)(2,1)S(1)} %merge.1.refs_0_), channel_id=1, source_target_pairs={{0,16},{8,24},{16,0},{24,8},{1,17},{9,25},{17,1},{25,9},{2,18},{10... | collective-permute-start | bytes 122888 | tf_op jit(solution)/shard_map/ppermute | solution.py:668
  48.9 3.4 %collective-permute-start.5 = (bf16[160,128]{1,0:T(8,128)(2,1)S(1)}, bf16[160,128]{1,0:T(8,128)(2,1)S(1)}, u32[]{:S(2)}, u32[]{:S(2)}) collective-permute-start(bf16[160,128]{1,0:T(8,128)(2,1)S(1)} %merge.1.refs_0_), channel_id=1, source_target_pairs={{0,24},{8,0},{16,8},{24,16},{1,25},{9,1},{17,9},{25,17},{2,26},{10... | collective-permute-start | bytes 122888 | tf_op jit(solution)/shard_map/ppermute | solution.py:668

commit v8 on v6

--- a/solution.py
+++ b/solution.py
@@ -406,7 +406,7 @@
     cols,
     place_ref,
     message_refs,
-    weight_hbm,
+    weight_ref,
     shard_refs,
     out_ref,
     token_ref,
@@ -414,20 +414,17 @@
     first_ref,
     act_ref,
     wide_ref,
-    weight_ref,
     kernel_ref,
     sems,
 ):
     at_first = place_ref[0] == 0
     at_last = place_ref[0] == place_ref[1] - 1
     step = place_ref[2]
-    weight_copy = pltpu.make_async_copy(weight_hbm, weight_ref, sems.at[0])
-    weight_copy.start()
     if len(shard_refs) == 1:
-        shard_copies = [pltpu.make_async_copy(shard_refs[0], kernel_ref, sems.at[1])]
+        shard_copies = [pltpu.make_async_copy(shard_refs[0], kernel_ref, sems.at[0])]
     else:
         shard_copies = [
-            pltpu.make_async_copy(ref, kernel_ref.at[place_ref[3 + k]], sems.at[1 + k])
+            pltpu.make_async_copy(ref, kernel_ref.at[place_ref[3 + k]], sems.at[k])
             for k, ref in enumerate(shard_refs)
         ]
     direct = place_ref[3 + len(shard_refs)]
@@ -483,7 +480,6 @@
         pair_ref[side, 0] = pair[0]
         pair_ref[side, 1] = pair[0]
 
-    weight_copy.wait()
     gaps = rows + 1
     for side in range(2):
         columns = jnp.concatenate(
@@ -554,16 +550,17 @@
 
     def body(place_ref, *refs):
         message_refs, refs = refs[:count], refs[count:]
-        weight_hbm, shard_refs = refs[0], refs[1 : 1 + len(shards)]
+        weight_ref, shard_refs = refs[0], refs[1 : 1 + len(shards)]
         decode_kernel(
-            frames, rows, cols, place_ref, message_refs, weight_hbm, shard_refs, *refs[1 + len(shards) :]
+            frames, rows, cols, place_ref, message_refs, weight_ref, shard_refs, *refs[1 + len(shards) :]
         )
 
     grid_spec = pltpu.PrefetchScalarGridSpec(
         num_scalar_prefetch=1,
         grid=(1,),
         in_specs=[whole(part.shape) for part in messages]
-        + [pl.BlockSpec(memory_space=pl.ANY)] * (1 + len(shards)),
+        + [pl.BlockSpec(memory_space=pltpu.VMEM)]
+        + [pl.BlockSpec(memory_space=pl.ANY)] * len(shards),
         out_specs=whole((frames, height, width, CH)),
         scratch_shapes=[
             pltpu.VMEM((frames, rows + 2, cols + 16, 2 * NARROW), jnp.float32),
@@ -571,9 +568,8 @@
             pltpu.VMEM((CH // 128, frames, height + 2, width + 16, 128), jnp.float32),
             pltpu.VMEM((CH // 128, frames, height + 2, width + 16, 128), jnp.float32),
             pltpu.VMEM((frames + 2, height + 2, width, 3 * CH), jnp.bfloat16),
-            pltpu.VMEM(weights.shape, jnp.bfloat16),
             pltpu.VMEM((groups, taps, depth, CH), jnp.bfloat16),
-            pltpu.SemaphoreType.DMA((1 + len(shards),)),
+            pltpu.SemaphoreType.DMA((len(shards),)),
         ],
     )
     return pl.pallas_call(

time: 58.7 us -> 58.6 us (level)
  no operation moved by 1% of the time
where the time goes in v8:
time: 58.6 us; the launch traced here: 58.2 us
  Pallas kernels  24 us (41%)
  starting transfers between devices  14 us (24%)
  waiting for transfers between devices  12 us (20%)
  local copies, waits for them, and re-layouts  6.76 us (12%)
  between operations  0.77 us (1%)
  other arithmetic  0.64 us (1%)
    pallas_call x2, Pallas kernels, attend(): pl.pallas_call(functools.partial(attend_kernel, start, grid), grid=(count...  13.7 us
    pallas_call x1, Pallas kernels, decode(): pl.pallas_call(body, grid_spec=grid_spec, out_shape=jax.ShapeDtypeStruct(...  7.4 us
    unnamed x30, local copies, waits for them, and re-layouts  6.68 us
    ppermute x1, starting transfers between devices, swap_shards(): lax.ppermute(near, 'segment', [(s, s ^ 1) for s in segments])  5.53 us
    ppermute x2, waiting for transfers between devices, trade_shards(): lax.ppermute(shard, ('segment', 'grp'), pairs)  4.1 us
    ppermute x3, waiting for transfers between devices, local(): lax.ppermute(message, 'segment', [(i, (i + step) % segment_count) for i i...  3.21 us
    ppermute x1, waiting for transfers between devices, split_attention(): other_queries = [lax.ppermute(part, 'sp', swap) for part in parts]  3.03 us
    ppermute x3, starting transfers between devices, local(): lax.ppermute(message, 'segment', [(i, (i + step) % segment_count) for i i...  2.8 us
  transfers between devices with their start and end apart: 10, of which 6 were waited for; matrix products, arithmetic and copies ran while one was open for 1% of the time, Pallas kernels for 29%

profile of v8, /device:TPU:17, one launch (start us, length us, event | category | flops | bytes accessed | tf_op | source)
XLA Modules:
  0.0 58.2 jit_solution(18333469147770304592)
XLA Ops:
  0.0 1.2 %collective-permute-start.1 = (bf16[256,2048]{1,0:T(8,128)(2,1)}, bf16[256,2048]{1,0:T(8,128)(2,1)}, u32[]{:S(2)}, u32[]{:S(2)}) collective-permute-start(bf16[256,2048]{1,0:T(8,128)(2,1)} %bitcast.20), channel_id=1, source_target_pairs={{0,1},{1,0},{2,3},{3,2},{4,5},{5,4},{6,7},{7,6},{8,9},{9,8},{10,11... | collective-permute-start | bytes 3145736 | tf_op jit(solution)/shard_map/ppermute | solution.py:184
  1.2 0.1 collective-permute-start.6
  1.3 1.6 %collective-permute-start.7 = (bf16[27,64,256]{2,1,0:T(8,128)(2,1)}, bf16[27,64,256]{2,1,0:T(8,128)(2,1)}, u32[]{:S(2)}, u32[]{:S(2)}) collective-permute-start(bf16[27,64,256]{2,1,0:T(8,128)(2,1)} %refs_5_.1), channel_id=1, source_target_pairs={{2,4},{4,2},{8,14},{14,8},{18,20},{20,18},{24,30},{30,24},{3,5},{5... | collective-permute-start | bytes 2654216 | tf_op jit(solution)/shard_map/ppermute | solution.py:593
  2.9 0.0 copy-start
  2.9 1.2 %copy-done = bf16[1,1,4,4,16,2048]{5,4,3,2,1,0:T(8,128)(2,1)S(1)} copy-done((bf16[1,1,4,4,16,2048]{5,4,3,2,1,0:T(8,128)(2,1)S(1)}, bf16[1,1,4,4,16,2048]{5,4,3,2,1,0:T(8,128)(2,1)}, u32[]{:S(2)}) %copy-start) | copy-done | bytes 1048600
  4.1 0.0 copy-start.2
  4.1 1.2 %copy-done.2 = bf16[1,1,4,4,16,2048]{5,4,3,2,1,0:T(8,128)(2,1)S(1)} copy-done((bf16[1,1,4,4,16,2048]{5,4,3,2,1,0:T(8,128)(2,1)S(1)}, bf16[1,1,4,4,16,2048]{5,4,3,2,1,0:T(8,128)(2,1)}, u32[]{:S(2)}) %copy-start.2) | copy-done | bytes 1048600
  5.3 0.9 %copy-done.5 = bf16[2048,64]{0,1:T(8,128)(2,1)S(1)} copy-done((bf16[2048,64]{0,1:T(8,128)(2,1)S(1)}, bf16[2048,64]{0,1:T(8,128)(2,1)}, u32[]{:S(2)}) %copy-start.5) | copy-done | bytes 262168
  6.3 1.2 %copy-done.7 = bf16[1,1,4,4,16,2048]{5,4,3,2,1,0:T(8,128)(2,1)S(1)} copy-done((bf16[1,1,4,4,16,2048]{5,4,3,2,1,0:T(8,128)(2,1)S(1)}, bf16[1,1,4,4,16,2048]{5,4,3,2,1,0:T(8,128)(2,1)}, u32[]{:S(2)}) %copy-start.7) | copy-done | bytes 1048600
  7.5 0.7 %copy-done.8 = s32[16,2,2]{0,2,1:T(2,128)S(1)} copy-done((s32[16,2,2]{0,2,1:T(2,128)S(1)}, s32[16,2,2]{0,2,1:T(2,128)}, u32[]{:S(2)}) %copy-start.8) | copy-done | bytes 280
  8.2 0.7 %copy-done.10 = s32[16,2]{0,1:T(2,128)S(1)} copy-done((s32[16,2]{0,1:T(2,128)S(1)}, s32[16,2]{0,1:T(2,128)}, u32[]{:S(2)}) %copy-start.10) | copy-done | bytes 152
  8.9 8.0 %own_queries.1 = (f32[16,256]{1,0:T(8,128)}, f32[16,64,256]{2,1,0:T(8,128)S(1)}, bf16[608,128]{1,0:T(8,128)(2,1)S(1)}) custom-call(s32[1]{0:T(128)} %bitcast.rank_ref, s32[2,2,16]{2,1,0:T(2,128)S(1)} %bitcast.22, s32[2,16]{1,0:T(2,128)S(1)} %bitcast.24, bf16[256,2048]{1,0:T(8,128)(2,1)S(1)} %bitcast.21, bf16[256,2048]{1,0:T(8,128)(2,1)S(1)} %bitcast.14, ...), custom_call_target="tpu_custom_call" | custom-call | flops 4096 | bytes 4096 | tf_op jit(solution)/shard_map/own_queries/pallas_call | solution.py:206
  16.9 0.7 %copy-done.13 = bf16[608,128]{1,0:T(8,128)(2,1)} copy-done((bf16[608,128]{1,0:T(8,128)(2,1)}, bf16[608,128]{1,0:T(8,128)(2,1)S(1)}, u32[]{:S(2)}) %copy-start.13) | copy-done | bytes 155672
  17.5 0.0 copy-done.14
  17.6 0.6 %fusion = s32[]{:T(128)} fusion(s32[4]{0:T(128)S(1)} %copy-done.14, s32[]{:T(128)S(6)} %axis_index.39), kind=kLoop, calls=%fused_computation.1 | loop fusion | flops 11 | bytes 24 | tf_op jit(solution)/shard_map/reduce_sum | solution.py:627
  18.8 2.2 %spread_first_kernel.1.refs_4_ = bf16[2,768,512]{2,1,0:T(8,128)(2,1)} custom-call(bf16[27,16,256]{2,1,0:T(8,128)(2,1)} %plain_ref.1), custom_call_target="tpu_custom_call" | custom-call | tf_op jit(solution)/shard_map/spread_first_kernel/pallas_call | solution.py:393
  21.0 0.1 stack.33.place_ref
  21.1 0.2 collective-permute-start
  21.3 3.0 %collective-permute-done.1.q_ref = bf16[256,2048]{1,0:T(8,128)(2,1)} collective-permute-done((bf16[256,2048]{1,0:T(8,128)(2,1)}, bf16[256,2048]{1,0:T(8,128)(2,1)}, u32[]{:S(2)}, u32[]{:S(2)}) %collective-permute-start.1) | collective-permute-done | bytes 1048608 | tf_op jit(solution)/shard_map/ppermute | solution.py:184
  24.3 0.0 copy-done.3
  24.3 0.0 copy-done.1
  24.3 0.0 copy-done.6
  24.4 0.0 copy-done.9
  24.4 0.0 copy-done.11
  24.4 5.8 %other_queries.1 = (f32[16,256]{1,0:T(8,128)S(1)}, f32[16,64,256]{2,1,0:T(8,128)S(1)}) custom-call(s32[1]{0:T(128)} %bitcast.rank_ref, s32[2,2,16]{2,1,0:T(2,128)S(1)} %bitcast.23, s32[2,16]{1,0:T(2,128)S(1)} %bitcast.25, bf16[256,2048]{1,0:T(8,128)(2,1)} %collective-permute-done.1.q_ref, bf16[256,2048]{1,0:T(8,128)(2,1)S(1)} %bitcast.15, ...), custom_call_target="tpu_custom_call" | custom-call | flops 4096 | bytes 4096 | tf_op jit(solution)/shard_map/other_queries/pallas_call | solution.py:206
  30.1 0.0 copy-start.4
  30.1 0.0 copy-start.12
  30.2 0.0 collective-permute-done.note_ref
  30.2 0.1 combine.1.sent_ref
  30.3 1.3 %collective-permute-start.2 = (bf16[96,256]{1,0:T(8,128)(2,1)S(1)}, bf16[96,256]{1,0:T(8,128)(2,1)S(1)}, u32[]{:S(2)}, u32[]{:S(2)}) collective-permute-start(bf16[96,256]{1,0:T(8,128)(2,1)S(1)} %combine.1.sent_ref), channel_id=1, source_target_pairs={{0,1},{1,0},{2,3},{3,2},{4,5},{5,4},{6,7},{7,6},{8,9},{9,8},{10,11... | collective-permute-start | bytes 147464 | tf_op jit(solution)/shard_map/ppermute | solution.py:255
  31.6 0.4 beside.1.beside_ref
  32.0 1.7 %collective-permute-done.2.got_ref = bf16[96,256]{1,0:T(8,128)(2,1)S(1)} collective-permute-done((bf16[96,256]{1,0:T(8,128)(2,1)S(1)}, bf16[96,256]{1,0:T(8,128)(2,1)S(1)}, u32[]{:S(2)}, u32[]{:S(2)}) %collective-permute-start.2) | collective-permute-done | bytes 49184 | tf_op jit(solution)/shard_map/ppermute | solution.py:255
  33.7 0.2 merge.1.refs_0_
  33.8 4.1 %collective-permute-done.6.refs_6_ = bf16[27,64,256]{2,1,0:T(8,128)(2,1)} collective-permute-done((bf16[27,64,256]{2,1,0:T(8,128)(2,1)}, bf16[27,64,256]{2,1,0:T(8,128)(2,1)}, u32[]{:S(2)}, u32[]{:S(2)}) %collective-permute-start.6) | collective-permute-done | bytes 884768 | tf_op jit(solution)/shard_map/ppermute | solution.py:593
  37.9 0.0 collective-permute-done.7.refs_8_
  37.9 5.5 %collective-permute-start.8 = (bf16[27,64,256]{2,1,0:T(8,128)(2,1)}, bf16[27,64,256]{2,1,0:T(8,128)(2,1)S(1)}, u32[]{:S(2)}, u32[]{:S(2)}) collective-permute-start(bf16[27,64,256]{2,1,0:T(8,128)(2,1)} %collective-permute-done.6.refs_6_), channel_id=1, source_target_pairs={{0,8},{8,0},{16,24},{24,16},{1,9},{9,1},{17,25},{25,17},{2,10},{10... | collective-permute-start | bytes 2654216 | tf_op jit(solution)/shard_map/ppermute | solution.py:602
  43.5 1.3 %collective-permute-start.9 = (bf16[27,64,256]{2,1,0:T(8,128)(2,1)}, bf16[27,64,256]{2,1,0:T(8,128)(2,1)S(1)}, u32[]{:S(2)}, u32[]{:S(2)}) collective-permute-start(bf16[27,64,256]{2,1,0:T(8,128)(2,1)} %collective-permute-done.7.refs_8_), channel_id=1, source_target_pairs={{2,10},{4,12},{8,0},{14,6},{18,26},{20,28},{24,16},{30,22},{3,11},... | collective-permute-start | bytes 2654216 | tf_op jit(solution)/shard_map/ppermute | solution.py:604
  44.8 2.3 %collective-permute-start.3 = (bf16[160,128]{1,0:T(8,128)(2,1)S(1)}, bf16[160,128]{1,0:T(8,128)(2,1)S(1)}, u32[]{:S(2)}, u32[]{:S(2)}) collective-permute-start(bf16[160,128]{1,0:T(8,128)(2,1)S(1)} %merge.1.refs_0_), channel_id=1, source_target_pairs={{0,8},{8,16},{16,24},{24,0},{1,9},{9,17},{17,25},{25,1},{2,10},{10... | collective-permute-start | bytes 122888 | tf_op jit(solution)/shard_map/ppermute | solution.py:653
  47.1 0.3 collective-permute-start.4
  47.3 0.2 collective-permute-start.5
  47.6 0.6 %collective-permute-done.3.refs_1_ = bf16[160,128]{1,0:T(8,128)(2,1)S(1)} collective-permute-done((bf16[160,128]{1,0:T(8,128)(2,1)S(1)}, bf16[160,128]{1,0:T(8,128)(2,1)S(1)}, u32[]{:S(2)}, u32[]{:S(2)}) %collective-permute-start.3) | collective-permute-done | bytes 40992 | tf_op jit(solution)/shard_map/ppermute | solution.py:653
  48.2 1.8 %collective-permute-done.4.refs_2_ = bf16[160,128]{1,0:T(8,128)(2,1)S(1)} collective-permute-done((bf16[160,128]{1,0:T(8,128)(2,1)S(1)}, bf16[160,128]{1,0:T(8,128)(2,1)S(1)}, u32[]{:S(2)}, u32[]{:S(2)}) %collective-permute-start.4) | collective-permute-done | bytes 40992 | tf_op jit(solution)/shard_map/ppermute | solution.py:653
  49.9 0.8 %collective-permute-done.5.refs_3_ = bf16[160,128]{1,0:T(8,128)(2,1)S(1)} collective-permute-done((bf16[160,128]{1,0:T(8,128)(2,1)S(1)}, bf16[160,128]{1,0:T(8,128)(2,1)S(1)}, u32[]{:S(2)}, u32[]{:S(2)}) %collective-permute-start.5) | collective-permute-done | bytes 40992 | tf_op jit(solution)/shard_map/ppermute | solution.py:653
  50.8 0.0 collective-permute-done.8.refs_7_
  50.8 0.0 collective-permute-done.9.refs_9_
  50.8 0.0 copy-done.4
  50.8 0.0 copy-done.12
  50.8 7.4 %decode_block.1 = bf16[4,8,32,256]{3,2,1,0:T(8,128)(2,1)} custom-call(s32[9]{0:T(128)S(1)} %stack.33.place_ref, bf16[160,128]{1,0:T(8,128)(2,1)S(1)} %merge.1.refs_0_, bf16[160,128]{1,0:T(8,128)(2,1)S(1)} %collective-permute-done.3.refs_1_, bf16[160,128]{1,0:T(8,128)(2,1)S(1)} %collective-permute-done.4.refs_2_, ...), custom_call_target="tpu_custom_call" | custom-call | flops 3623878656 | bytes 4063232 | tf_op jit(solution)/shard_map/decode_block/pallas_call | solution.py:575
  (11 shorter events, 0.0 us)
Async XLA Ops:
  0.0 24.3 %collective-permute-start.1 = (bf16[256,2048]{1,0:T(8,128)(2,1)}, bf16[256,2048]{1,0:T(8,128)(2,1)}, u32[]{:S(2)}, u32[]{:S(2)}) collective-permute-start(bf16[256,2048]{1,0:T(8,128)(2,1)} %bitcast.20), channel_id=1, source_target_pairs={{0,1},{1,0},{2,3},{3,2},{4,5},{5,4},{6,7},{7,6},{8,9},{9,8},{10,11... | collective-permute-start | bytes 3145736 | tf_op jit(solution)/shard_map/ppermute | solution.py:184
  1.2 36.7 %collective-permute-start.6 = (bf16[27,64,256]{2,1,0:T(8,128)(2,1)}, bf16[27,64,256]{2,1,0:T(8,128)(2,1)}, u32[]{:S(2)}, u32[]{:S(2)}) collective-permute-start(bf16[27,64,256]{2,1,0:T(8,128)(2,1)} %refs_5_.1), channel_id=1, source_target_pairs={{0,2},{2,0},{4,6},{6,4},{8,12},{10,14},{12,8},{14,10},{16,18},{18,... | collective-permute-start | bytes 2654216 | tf_op jit(solution)/shard_map/ppermute | solution.py:593
  1.3 36.7 %collective-permute-start.7 = (bf16[27,64,256]{2,1,0:T(8,128)(2,1)}, bf16[27,64,256]{2,1,0:T(8,128)(2,1)}, u32[]{:S(2)}, u32[]{:S(2)}) collective-permute-start(bf16[27,64,256]{2,1,0:T(8,128)(2,1)} %refs_5_.1), channel_id=1, source_target_pairs={{2,4},{4,2},{8,14},{14,8},{18,20},{20,18},{24,30},{30,24},{3,5},{5... | collective-permute-start | bytes 2654216 | tf_op jit(solution)/shard_map/ppermute | solution.py:593
  2.9 1.2 %copy-start = (bf16[1,1,4,4,16,2048]{5,4,3,2,1,0:T(8,128)(2,1)S(1)}, bf16[1,1,4,4,16,2048]{5,4,3,2,1,0:T(8,128)(2,1)}, u32[]{:S(2)}) copy-start(bf16[1,1,4,4,16,2048]{5,4,3,2,1,0:T(8,128)(2,1)} %param.10) | copy-start | bytes 3145732
  4.1 1.2 %copy-start.2 = (bf16[1,1,4,4,16,2048]{5,4,3,2,1,0:T(8,128)(2,1)S(1)}, bf16[1,1,4,4,16,2048]{5,4,3,2,1,0:T(8,128)(2,1)}, u32[]{:S(2)}) copy-start(bf16[1,1,4,4,16,2048]{5,4,3,2,1,0:T(8,128)(2,1)} %param.11) | copy-start | bytes 3145732
  5.3 0.9 %copy-start.5 = (bf16[2048,64]{0,1:T(8,128)(2,1)S(1)}, bf16[2048,64]{0,1:T(8,128)(2,1)}, u32[]{:S(2)}) copy-start(bf16[2048,64]{0,1:T(8,128)(2,1)} %param.14) | copy-start | bytes 786436
  6.3 1.2 %copy-start.7 = (bf16[1,1,4,4,16,2048]{5,4,3,2,1,0:T(8,128)(2,1)S(1)}, bf16[1,1,4,4,16,2048]{5,4,3,2,1,0:T(8,128)(2,1)}, u32[]{:S(2)}) copy-start(bf16[1,1,4,4,16,2048]{5,4,3,2,1,0:T(8,128)(2,1)} %param.9) | copy-start | bytes 3145732
  7.5 0.7 %copy-start.8 = (s32[16,2,2]{0,2,1:T(2,128)S(1)}, s32[16,2,2]{0,2,1:T(2,128)}, u32[]{:S(2)}) copy-start(s32[16,2,2]{0,2,1:T(2,128)} %param.12) | copy-start | bytes 772
  8.2 0.7 %copy-start.10 = (s32[16,2]{0,1:T(2,128)S(1)}, s32[16,2]{0,1:T(2,128)}, u32[]{:S(2)}) copy-start(s32[16,2]{0,1:T(2,128)} %param.13) | copy-start | bytes 388
  8.9 8.7 %copy-start.14 = (s32[4]{0:T(128)S(1)}, s32[4]{0:T(128)}, u32[]{:S(2)}) copy-start(s32[4]{0:T(128)} %param.15) | copy-start | bytes 52
  8.9 15.5 %copy-start.3 = (bf16[1,1,4,4,16,2048]{5,4,3,2,1,0:T(8,128)(2,1)S(1)}, bf16[1,1,4,4,16,2048]{5,4,3,2,1,0:T(8,128)(2,1)}, u32[]{:S(2)}) copy-start(bf16[1,1,4,4,16,2048]{5,4,3,2,1,0:T(8,128)(2,1)} %param.11) | copy-start | bytes 3145732
  16.9 0.7 %copy-start.13 = (bf16[608,128]{1,0:T(8,128)(2,1)}, bf16[608,128]{1,0:T(8,128)(2,1)S(1)}, u32[]{:S(2)}) copy-start(bf16[608,128]{1,0:T(8,128)(2,1)S(1)} %get-tuple-element.19) | copy-start | bytes 466948
  17.5 6.8 %copy-start.1 = (bf16[1,1,4,4,16,2048]{5,4,3,2,1,0:T(8,128)(2,1)S(1)}, bf16[1,1,4,4,16,2048]{5,4,3,2,1,0:T(8,128)(2,1)}, u32[]{:S(2)}) copy-start(bf16[1,1,4,4,16,2048]{5,4,3,2,1,0:T(8,128)(2,1)} %param.10) | copy-start | bytes 3145732
  17.5 6.8 %copy-start.6 = (bf16[2048,64]{0,1:T(8,128)(2,1)S(1)}, bf16[2048,64]{0,1:T(8,128)(2,1)}, u32[]{:S(2)}) copy-start(bf16[2048,64]{0,1:T(8,128)(2,1)} %param.14) | copy-start | bytes 786436
  17.5 6.8 %copy-start.9 = (s32[16,2,2]{0,2,1:T(2,128)S(1)}, s32[16,2,2]{0,2,1:T(2,128)}, u32[]{:S(2)}) copy-start(s32[16,2,2]{0,2,1:T(2,128)} %param.12) | copy-start | bytes 772
  17.5 6.8 %copy-start.11 = (s32[16,2]{0,1:T(2,128)S(1)}, s32[16,2]{0,1:T(2,128)}, u32[]{:S(2)}) copy-start(s32[16,2]{0,1:T(2,128)} %param.13) | copy-start | bytes 388
  21.1 9.0 %collective-permute-start = (bf16[608,128]{1,0:T(8,128)(2,1)}, bf16[608,128]{1,0:T(8,128)(2,1)S(1)}, u32[]{:S(2)}, u32[]{:S(2)}) collective-permute-start(bf16[608,128]{1,0:T(8,128)(2,1)} %copy-done.13), channel_id=1, source_target_pairs={{0,1},{1,0},{2,3},{3,2},{4,5},{5,4},{6,7},{7,6},{8,9},{9,8},{10,11... | collective-permute-start | bytes 466952 | tf_op jit(solution)/shard_map/ppermute | solution.py:238
  30.1 20.6 %copy-start.4 = (bf16[2,768,512]{2,1,0:T(8,128)(2,1)S(1)}, bf16[2,768,512]{2,1,0:T(8,128)(2,1)}, u32[]{:S(2)}) copy-start(bf16[2,768,512]{2,1,0:T(8,128)(2,1)} %spread_first_kernel.1.refs_4_) | copy-start | bytes 4718596
  30.1 20.6 %copy-start.12 = (bf16[27,64,256]{2,1,0:T(8,128)(2,1)S(1)}, bf16[27,64,256]{2,1,0:T(8,128)(2,1)}, u32[]{:S(2)}) copy-start(bf16[27,64,256]{2,1,0:T(8,128)(2,1)} %refs_5_.1) | copy-start | bytes 2654212
  30.3 3.4 %collective-permute-start.2 = (bf16[96,256]{1,0:T(8,128)(2,1)S(1)}, bf16[96,256]{1,0:T(8,128)(2,1)S(1)}, u32[]{:S(2)}, u32[]{:S(2)}) collective-permute-start(bf16[96,256]{1,0:T(8,128)(2,1)S(1)} %combine.1.sent_ref), channel_id=1, source_target_pairs={{0,1},{1,0},{2,3},{3,2},{4,5},{5,4},{6,7},{7,6},{8,9},{9,8},{10,11... | collective-permute-start | bytes 147464 | tf_op jit(solution)/shard_map/ppermute | solution.py:255
  37.9 12.8 %collective-permute-start.8 = (bf16[27,64,256]{2,1,0:T(8,128)(2,1)}, bf16[27,64,256]{2,1,0:T(8,128)(2,1)S(1)}, u32[]{:S(2)}, u32[]{:S(2)}) collective-permute-start(bf16[27,64,256]{2,1,0:T(8,128)(2,1)} %collective-permute-done.6.refs_6_), channel_id=1, source_target_pairs={{0,8},{8,0},{16,24},{24,16},{1,9},{9,1},{17,25},{25,17},{2,10},{10... | collective-permute-start | bytes 2654216 | tf_op jit(solution)/shard_map/ppermute | solution.py:602
  43.5 7.3 %collective-permute-start.9 = (bf16[27,64,256]{2,1,0:T(8,128)(2,1)}, bf16[27,64,256]{2,1,0:T(8,128)(2,1)S(1)}, u32[]{:S(2)}, u32[]{:S(2)}) collective-permute-start(bf16[27,64,256]{2,1,0:T(8,128)(2,1)} %collective-permute-done.7.refs_8_), channel_id=1, source_target_pairs={{2,10},{4,12},{8,0},{14,6},{18,26},{20,28},{24,16},{30,22},{3,11},... | collective-permute-start | bytes 2654216 | tf_op jit(solution)/shard_map/ppermute | solution.py:604
  44.8 3.4 %collective-permute-start.3 = (bf16[160,128]{1,0:T(8,128)(2,1)S(1)}, bf16[160,128]{1,0:T(8,128)(2,1)S(1)}, u32[]{:S(2)}, u32[]{:S(2)}) collective-permute-start(bf16[160,128]{1,0:T(8,128)(2,1)S(1)} %merge.1.refs_0_), channel_id=1, source_target_pairs={{0,8},{8,16},{16,24},{24,0},{1,9},{9,17},{17,25},{25,1},{2,10},{10... | collective-permute-start | bytes 122888 | tf_op jit(solution)/shard_map/ppermute | solution.py:653
  47.1 2.9 %collective-permute-start.4 = (bf16[160,128]{1,0:T(8,128)(2,1)S(1)}, bf16[160,128]{1,0:T(8,128)(2,1)S(1)}, u32[]{:S(2)}, u32[]{:S(2)}) collective-permute-start(bf16[160,128]{1,0:T(8,128)(2,1)S(1)} %merge.1.refs_0_), channel_id=1, source_target_pairs={{0,16},{8,24},{16,0},{24,8},{1,17},{9,25},{17,1},{25,9},{2,18},{10... | collective-permute-start | bytes 122888 | tf_op jit(solution)/shard_map/ppermute | solution.py:653
  47.3 3.4 %collective-permute-start.5 = (bf16[160,128]{1,0:T(8,128)(2,1)S(1)}, bf16[160,128]{1,0:T(8,128)(2,1)S(1)}, u32[]{:S(2)}, u32[]{:S(2)}) collective-permute-start(bf16[160,128]{1,0:T(8,128)(2,1)S(1)} %merge.1.refs_0_), channel_id=1, source_target_pairs={{0,24},{8,0},{16,8},{24,16},{1,25},{9,1},{17,9},{25,17},{2,26},{10... | collective-permute-start | bytes 122888 | tf_op jit(solution)/shard_map/ppermute | solution.py:653
